TPU v7x, 128 devices: a whole 4x4x4 slice. The times are simulated.
128 devices in a mesh: pipe: 2 (over core), expert: 8 (over y_lo, x), etp: 8 (over y_hi, z).
Axes of the slice: x: 4, y: 4 (y_hi: 2, y_lo: 2; y = y_hi * 2 + y_lo), z: 4, core: 2. Of those that a mesh axis runs over, the one named last changes fastest.
Arguments:
- tokens_in: bfloat16 [2, 1024, 3072], P('pipe', 'expert'), may hold values from -6 to 6
- cotangent_in: bfloat16 [2, 1024, 3072], P('pipe', 'expert'), may hold values from -6 to 6
- expert_ids: int32 [2, 1024, 2], P('pipe'), may hold values from 0 to 7, all different within a row; in each aligned block of 128 rows (0 to 127, 128 to 255, ..., all dimensions but the last counted through in order) at most 64 rows name the same one
- router_weight: bfloat16 [2, 3072, 8], P('pipe'), may hold values from -0.109375 to 0.109375
- gate_weight: bfloat16 [2, 8, 3072, 8192], P('pipe', 'expert', None, 'etp'), may hold values from -0.109375 to 0.109375
- up_weight: bfloat16 [2, 8, 3072, 8192], P('pipe', 'expert', None, 'etp'), may hold values from -0.109375 to 0.109375
- down_weight: bfloat16 [2, 8, 8192, 3072], P('pipe', 'expert', 'etp'), may hold values from -0.0625 to 0.0625
Outputs:
- layer_out: bfloat16 [2, 1024, 3072], P('pipe', ('expert', 'etp'))
- rows_grad: bfloat16 [2, 1024, 3072], P('pipe', ('expert', 'etp'))
Inputs may be any that keep to these rules, and one draw needn't show every extreme that they name: `expert_ids`: the two experts of a token differ. In each aligned block of 128 rows (the tokens of one expert group) no expert is named more than 64 times, a bound that some block reaches.
All inputs are finite; a program needn't handle non-finite values.
Results may differ from a plain program's by a relative error of at most 0.0065.
Values may be sent and summed in bfloat16 or wider, within the bound.
No kernel may reach another device: no remote copies, remote signals or barrier semaphores. Data moves between devices by JAX's collectives and lax.ppermute only.
A program may use at most 192 MiB of HBM per device.

v0:
```python
import jax
import jax.numpy as jnp
from jax import lax
from jax.sharding import PartitionSpec as P


def shifted(x, axis, by):
    count = lax.axis_size(axis)
    return lax.ppermute(x, axis, [(i, (i + by) % count) for i in range(count)])


def route_slots(routes, block_rows, capacity_src, experts):
    count = routes.shape[0]
    flat_ids = routes.reshape(count // block_rows, block_rows * 2)
    onehot = (flat_ids[:, :, None] == jnp.arange(experts, dtype=jnp.int32)[None, None, :]).astype(
        jnp.int32
    )
    before = jnp.cumsum(onehot, axis=1) - onehot
    rank_ids = jnp.sum(before * onehot, axis=2)
    source = jnp.arange(count // block_rows, dtype=jnp.int32)[:, None]
    slot_ids = source * capacity_src + rank_ids
    return (slot_ids.reshape(count, 2), rank_ids.reshape(count, 2))


def pair_weights(scores, routes):
    chosen = jnp.take_along_axis(scores, routes, axis=1)
    score_gap = chosen[:, ::-1] - chosen
    return 1.0 / (1.0 + jnp.exp(score_gap))


def swish_parts(gate_pre):
    sigmoid_part = jax.nn.sigmoid(gate_pre)
    return (gate_pre * sigmoid_part, sigmoid_part * (1.0 + gate_pre * (1.0 - sigmoid_part)))


def expert_pass(expert_rows, scaled_cot, w_gate, w_up, w_down):
    gate_pre = jnp.dot(expert_rows, w_gate, preferred_element_type=jnp.float32)
    up_pre = jnp.dot(expert_rows, w_up, preferred_element_type=jnp.float32)
    swished, swish_slope = swish_parts(gate_pre)
    hidden = (swished * up_pre).astype(jnp.bfloat16)
    expert_out = jnp.dot(hidden, w_down, preferred_element_type=jnp.float32)
    d_hidden = jnp.dot(scaled_cot, w_down.T, preferred_element_type=jnp.float32)
    d_up = (d_hidden * swished).astype(jnp.bfloat16)
    d_gate = (d_hidden * up_pre * swish_slope).astype(jnp.bfloat16)
    d_rows = jnp.dot(d_gate, w_gate.T, preferred_element_type=jnp.float32)
    d_rows = d_rows + jnp.dot(d_up, w_up.T, preferred_element_type=jnp.float32)
    return (expert_out, d_rows)


def score_grad(weights, d_weights, routes, experts):
    d_left = weights[:, 0] * weights[:, 1] * (d_weights[:, 0] - d_weights[:, 1])
    columns = jnp.arange(experts, dtype=jnp.int32)[None, :]
    first = (routes[:, 0:1] == columns).astype(jnp.float32)
    second = (routes[:, 1:2] == columns).astype(jnp.float32)
    return ((first - second) * d_left[:, None]).astype(jnp.bfloat16)


def per_device(
    tokens_in, cotangent_in, expert_ids, router_weight, gate_weight, up_weight, down_weight
):
    arrived = shifted(tokens_in, "pipe", 1)[0]
    upstream = shifted(cotangent_in, "pipe", -1)[0]
    routes = expert_ids[0]
    router = router_weight[0]
    w_gate = gate_weight[0, 0]
    w_up = up_weight[0, 0]
    w_down = down_weight[0, 0]
    experts = router.shape[1]
    width = arrived.shape[1]
    n_expert = lax.axis_size("expert")
    n_etp = lax.axis_size("etp")
    group_count = arrived.shape[0]
    capacity_src = 4 * group_count // n_expert
    capacity = capacity_src * n_expert
    share = group_count // n_etp
    my_group = lax.axis_index("expert")
    my_part = lax.axis_index("etp")
    group_start = my_group * group_count
    part_start = my_part * share
    own_start = group_start + part_start
    own_routes = lax.dynamic_slice_in_dim(routes, own_start, share, 0)
    all_rows, all_cot = (
        lax.all_gather(arrived, "expert", axis=0, tiled=True),
        lax.all_gather(upstream, "expert", axis=0, tiled=True),
    )
    token_count = all_rows.shape[0]
    scores = jnp.dot(all_rows, router, preferred_element_type=jnp.float32)
    weights = pair_weights(scores, routes)
    own_weights = lax.dynamic_slice_in_dim(weights, own_start, share, 0)
    slot_ids, rank_ids = route_slots(routes, group_count, capacity_src, experts)
    slot_index = jnp.where(routes == my_group, slot_ids, capacity)
    token_of = jnp.repeat(jnp.arange(token_count, dtype=jnp.int32), 2)
    choice_of = jnp.tile(jnp.arange(2, dtype=jnp.int32), token_count)
    row_table = (
        jnp.full((capacity,), token_count, jnp.int32)
        .at[slot_index.reshape(-1)]
        .set(token_of, mode="drop")
    )
    pick_table = (
        jnp.zeros((capacity,), jnp.int32).at[slot_index.reshape(-1)].set(choice_of, mode="drop")
    )
    weight_table = (
        jnp.zeros((capacity,), jnp.float32)
        .at[slot_index.reshape(-1)]
        .set(weights.reshape(-1), mode="drop")
    )
    rows_pad = jnp.concatenate([all_rows, jnp.zeros((1, width), jnp.bfloat16)], axis=0)
    cot_pad = jnp.concatenate([all_cot, jnp.zeros((1, width), jnp.bfloat16)], axis=0)
    expert_rows = rows_pad[row_table]
    cot_rows = cot_pad[row_table].astype(jnp.float32)
    scaled_cot = (weight_table[:, None] * cot_rows).astype(jnp.bfloat16)
    expert_out, d_expert = expert_pass(expert_rows, scaled_cot, w_gate, w_up, w_down)
    slot_dot = jnp.sum(cot_rows * expert_out, axis=1)
    term_out = (
        jnp.zeros((token_count, width), jnp.float32)
        .at[row_table]
        .add(weight_table[:, None] * expert_out, mode="drop")
    )
    term_grad = (
        jnp.zeros((token_count, width), jnp.float32).at[row_table].add(d_expert, mode="drop")
    )
    term_weights = (
        jnp.zeros((token_count, 2), jnp.float32)
        .at[row_table, pick_table]
        .add(slot_dot, mode="drop")
    )
    out_sum, grad_sum, d_weights = (
        lax.psum_scatter(term_out, ("expert", "etp"), scatter_dimension=0, tiled=True),
        lax.psum_scatter(term_grad, ("expert", "etp"), scatter_dimension=0, tiled=True),
        lax.psum_scatter(term_weights, ("expert", "etp"), scatter_dimension=0, tiled=True),
    )
    layer_rows = out_sum.astype(jnp.bfloat16)
    d_scores = score_grad(own_weights, d_weights, own_routes, experts)
    grad_rows = grad_sum + jnp.dot(d_scores, router.T, preferred_element_type=jnp.float32)
    return (layer_rows[None], grad_rows.astype(jnp.bfloat16)[None])


def solution(mesh):
    return jax.shard_map(
        per_device,
        mesh=mesh,
        in_specs=(
            P("pipe", "expert", None),
            P("pipe", "expert", None),
            P("pipe", None, None),
            P("pipe", None, None),
            P("pipe", "expert", None, "etp"),
            P("pipe", "expert", None, "etp"),
            P("pipe", "expert", "etp", None),
        ),
        out_specs=(P("pipe", ("expert", "etp"), None), P("pipe", ("expert", "etp"), None)),
        check_vma=False,
    )
```

profile of v0, /device:TPU:0, one launch (start us, length us, event | category | flops | bytes accessed | tf_op | source)
XLA Modules:
  0.0 1365.0 jit_solution(15112108764213976001)
XLA Ops:
  7.2 0.1 collective-permute-start.1
  7.3 2.5 collective-permute-done.1
  9.8 0.9 copy-done.6
  10.7 0.0 all-gather.5.cloned.1.call-start
  10.8 0.2 collective-permute-start
  11.0 2.4 collective-permute-done
  13.3 0.9 copy-done.7
  14.2 0.0 reduce-scatter.10.cloned.1.call-start
  14.3 0.9 copy.29
  15.2 0.3 eq.79
  15.5 0.3 eq.75
  15.8 0.7 broadcast_compare_fusion
  16.5 0.3 copy.28
  16.8 0.4 eq.74
  17.2 0.1 broadcast_bitcast_fusion
  17.2 0.2 add.111
  17.5 0.3 add.112
  17.8 4.5 reduce-window.6
  22.3 0.1 slice.40
  22.4 0.2 copy.31
  22.6 0.1 fusion.40
  22.6 0.1 fusion.30
  22.8 0.3 reshape.144
  23.1 0.7 fusion.37
  23.8 0.2 copy.34
  24.0 0.3 reshape.134
  24.3 0.3 reshape.176
  24.7 8.0 scatter_custom_fusion.4
  32.7 8.2 scatter_custom_fusion
  41.0 0.6 or_select_fusion
  41.6 44.0 %all-gather.7.cloned.1.call-done = bf16[1,1024,3072]{2,1,0:T(8,128)(2,1)} async-done(((bf16[1,128,3072]{2,1,0:T(8,128)(2,1)}), bf16[1,1024,3072]{2,1,0:T(8,128)(2,1)}) %all-gather.7.cloned.1.call-update) | async-done | bytes 6291472 | tf_op jit(solution)/shard_map/all_gather | solution.py:84
  85.5 5.9 concatenate.10
  91.4 66.8 %all-gather.5.cloned.1.call-done = bf16[1,1024,3072]{2,1,0:T(8,128)(2,1)} async-done(((bf16[1,128,3072]{2,1,0:T(8,128)(2,1)}), bf16[1,1024,3072]{2,1,0:T(8,128)(2,1)}) %all-gather.5.cloned.1.call-update) | async-done | bytes 6291472 | tf_op jit(solution)/shard_map/all_gather | solution.py:83
  158.2 5.9 concatenate.9
  164.1 10.6 gather_fusion.1
  174.8 9.9 gather_fusion
  184.7 7.7 fusion.8
  192.4 7.8 fusion.12
  200.2 1.7 fusion.33
  202.0 12.5 gather_fusion.2
  214.5 0.5 reshape.137
  215.0 0.1 and_select_fusion
  215.1 0.7 rev.3
  215.8 11.0 fusion.1
  226.9 24.4 %scatter_fusion = f32[1024,2]{0,1:T(2,128)S(1)} fusion(f32[1024,2]{0,1:T(2,128)S(1)} %broadcast_in_dim.51, s32[512]{0:T(512)S(1)} %bitcast.68, f32[512]{0:T(512)S(1)} %get-tuple-element.6), kind=kCustom, calls=%fused_computation.8 | custom fusion | flops 512 | bytes 10240 | tf_op jit(solution)/shard_map/scatter-add | solution.py:125
  251.3 1.0 copy.37
  252.4 0.0 reduce-scatter.6.cloned.1.call-start
  252.4 0.2 add_divide_fusion.1
  252.6 0.3 reshape.152
  252.9 8.6 scatter_custom_fusion.1
  261.4 16.7 %scatter_custom_fusion.2 = f32[1024,3072]{1,0:T(8,128)} fusion(s32[512]{0:T(512)} %copy-done.8, f32[512,3072]{1,0:T(8,128)} %get-tuple-element.7, f32[]{:T(128)} %constant.16.clone.1, f32[512]{0:T(512)S(1)} %scatter_custom_fusion.1), kind=kCustom, calls=%fused_computation.27 | custom fusion | flops 3145728 | bytes 18876928 | tf_op jit(solution)/shard_map/scatter-add | solution.py:117
  278.2 0.0 reduce-scatter.8.cloned.1.call-start
  278.3 1.8 copy-done.4
  280.1 5.9 fusion.2
  286.0 8.4 fusion.6
  294.5 6.0 fusion.10
  300.4 18.9 %scatter_custom_fusion.3 = f32[1024,3072]{1,0:T(8,128)} fusion(s32[512]{0:T(512)} %copy-done.8, f32[512,3072]{1,0:T(8,128)} %fusion.10, f32[512,3072]{1,0:T(8,128)} %fusion.6, f32[]{:T(128)} %constant.16.clone.1), kind=kCustom, calls=%fused_computation.25 | custom fusion | flops 3145728 | bytes 25166336 | tf_op jit(solution)/shard_map/scatter-add | solution.py:120
  319.3 0.8 dynamic-slice_bitcast_fusion
  320.1 282.2 %reduce-scatter.10.cloned.1.call-done = f32[16,2]{1,0:T(8,128)} async-done(((f32[1024,2]{1,0:T(8,128)}), f32[16,2]{1,0:T(8,128)}) %reduce-scatter.10.cloned.1.call-update) | async-done | bytes 144 | tf_op jit(solution)/shard_map/reduce_scatter | solution.py:130
  602.3 1.0 fusion.39
  603.2 376.0 %reduce-scatter.6.cloned.1.call-done = f32[16,3072]{1,0:T(8,128)} async-done(((f32[1024,3072]{1,0:T(8,128)}), f32[16,3072]{1,0:T(8,128)}) %reduce-scatter.6.cloned.1.call-update) | async-done | bytes 196624 | tf_op jit(solution)/shard_map/reduce_scatter | solution.py:128
  979.2 1.6 convert_bitcast_fusion
  980.8 375.7 %reduce-scatter.8.cloned.1.call-done = f32[16,3072]{1,0:T(8,128)} async-done(((f32[1024,3072]{1,0:T(8,128)}), f32[16,3072]{1,0:T(8,128)}) %reduce-scatter.8.cloned.1.call-update) | async-done | bytes 196624 | tf_op jit(solution)/shard_map/reduce_scatter | solution.py:129
  1356.5 1.8 fusion.21
  (50 shorter events, 0.3 us)
Async XLA Ops:
  7.2 193.0 %copy-start = (bf16[1,3072,8]{1,2,0:T(8,128)(2,1)S(1)}, bf16[1,3072,8]{1,2,0:T(8,128)(2,1)}, u32[]{:S(2)}) copy-start(bf16[1,3072,8]{1,2,0:T(8,128)(2,1)} %param.10) | copy-start | bytes 147460
  7.2 78.4 %all-gather.7.cloned.1.call-start = ((), (), s32[]{:S(2)}) async-start(), calls=%async_computation.6 | async-start | bytes 7077888 | tf_op jit(solution)/shard_map/all_gather | solution.py:84
  7.2 2.6 collective-permute-start.1
  9.8 0.9 copy-start.6
  10.7 147.5 %all-gather.5.cloned.1.call-start = ((), (), s32[]{:S(2)}) async-start(), calls=%async_computation.5 | async-start | bytes 7077888 | tf_op jit(solution)/shard_map/all_gather | solution.py:83
  10.8 2.6 collective-permute-start
  13.3 0.9 copy-start.7
  14.2 588.0 %reduce-scatter.10.cloned.1.call-start = ((), (), s32[]{:S(2)}) async-start(), calls=%async_computation.7 | async-start | bytes 532480 | tf_op jit(solution)/shard_map/reduce_scatter | solution.py:130
  15.2 8.6 copy-start.2
  24.6 66.8 %copy-start.9 = (s32[2048,1]{0,1:T(1,128)}, s32[2048,1]{0,1:T(1,128)S(1)}, u32[]{:S(2)}) copy-start(s32[2048,1]{0,1:T(1,128)S(1)} %compare_select_fusion.1) | copy-start | bytes 24580
  40.9 50.5 %copy-start.8 = (s32[512]{0:T(512)}, s32[512]{0:T(512)S(1)}, u32[]{:S(2)}) copy-start(s32[512]{0:T(512)S(1)} %get-tuple-element.3) | copy-start | bytes 6148
  184.7 15.5 %slice-start = ((s8[6291456]{0:T(1024)(128)(4,1)}), s8[4194304]{0:T(1024)(128)(4,1)S(1)}, s32[]{:S(2)}) async-start(s8[6291456]{0:T(1024)(128)(4,1)} %bitcast.70), calls=%async_computation.8 | async-start | bytes 8388608
  192.4 7.8 slice-start.1
  202.0 13.0 copy-start.3
  215.8 11.1 copy-start.1
  252.4 726.8 %reduce-scatter.6.cloned.1.call-start = ((), (), s32[]{:S(2)}) async-start(), calls=%async_computation.3 | async-start | bytes 12779520 | tf_op jit(solution)/shard_map/reduce_scatter | solution.py:128
  252.6 25.6 %copy-start.5 = (f32[1024,2]{1,0:T(8,128)}, f32[1024,2]{1,0:T(8,128)S(1)}, u32[]{:S(2)}) copy-start(f32[1024,2]{1,0:T(8,128)S(1)} %add_divide_fusion.1) | copy-start | bytes 24580
  278.2 1.9 copy-start.4
  278.2 1078.3 %reduce-scatter.8.cloned.1.call-start = ((), (), s32[]{:S(2)}) async-start(), calls=%async_computation.4 | async-start | bytes 12779520 | tf_op jit(solution)/shard_map/reduce_scatter | solution.py:129
  280.1 5.9 copy-start.11
  280.1 14.4 %slice-start.2 = ((s8[6291456]{0:T(1024)(128)(4,1)}), s8[4194304]{0:T(1024)(128)(4,1)S(1)}, s32[]{:S(2)}) async-start(s8[6291456]{0:T(1024)(128)(4,1)} %bitcast.80), calls=%async_computation.10 | async-start | bytes 8388608
  286.0 8.5 slice-start.3
  286.0 8.5 copy-start.10
Sparse Core Ops, SparseCore 0:
  10.8 74.6 all-gather.6
  87.2 71.0 all-gather.4
  252.5 349.7 reduce-scatter.9
  604.7 374.4 reduce-scatter.5
  981.6 374.8 reduce-scatter.7
where the time goes:
time: 1370 us; the launch traced here: 1360 us
  waiting for transfers between devices  1150 us (84%)
  local copies, waits for them, and re-layouts  80.7 us (6%)
  other arithmetic  69.6 us (5%)
  matrix products  50.3 us (4%)
  between operations  14.3 us (1%)
    reduce_scatter x1, waiting for transfers between devices, per_device(): lax.psum_scatter(term_out, ('expert', 'etp'), scatter_dimension=0, tiled=...  376 us
    reduce_scatter x1, waiting for transfers between devices, per_device(): lax.psum_scatter(term_grad, ('expert', 'etp'), scatter_dimension=0, tiled...  376 us
    reduce_scatter x1, waiting for transfers between devices, per_device(): lax.psum_scatter(term_weights, ('expert', 'etp'), scatter_dimension=0, ti...  282 us
    all_gather x1, waiting for transfers between devices, per_device(): lax.all_gather(arrived, 'expert', axis=0, tiled=True)  66.8 us
    all_gather x1, waiting for transfers between devices, per_device(): lax.all_gather(upstream, 'expert', axis=0, tiled=True)  44 us
  transfers between devices with their start and end apart: 7, of which 7 were waited for; matrix products, arithmetic and copies ran while one was open for 7% of the time, Pallas kernels for 0%

commit v1 on v0

v1 whole, which is shorter than its diff:
```python
import functools

import jax
import jax.numpy as jnp
from jax import lax
from jax.experimental import pallas as pl
from jax.experimental.pallas import tpu as pltpu
from jax.sharding import PartitionSpec as P

F32 = jnp.float32
BF16 = jnp.bfloat16
SIDE = 4
VMEM_LIMIT = 56 * 1024 * 1024


def moved(x, axis, flip, by):
    pairs = [
        (hi * SIDE + lo, (hi ^ flip) * SIDE + (lo + by) % SIDE) for hi in range(2) for lo in range(SIDE)
    ]
    return lax.ppermute(x, axis, pairs)


def column_tile(width):
    return 512 if width % 512 == 0 else width


def slot_targets(pos_ref, row, slots):
    y_lo, x, z = pos_ref[1], pos_ref[2], pos_ref[3]
    quarter = slots // SIDE
    direct = y_lo * (SIDE * slots) + ((x + row // slots) % SIDE) * slots + row % slots
    rest = row - SIDE * slots
    cross = (1 - y_lo) * (SIDE * slots) + ((x + rest // quarter) % SIDE) * slots + z * quarter + rest % quarter
    target = jnp.where(row < SIDE * slots, direct, cross)
    return jnp.where(row < SIDE * slots + slots, target, -1)


def dispatch_kernel(slots, pos_ref, ids_ref, arrived_ref, upstream_ref, router_ref, meta_ref, *outs):
    rows_out, cot_out, cross_out = outs[:SIDE], outs[SIDE : 2 * SIDE], outs[2 * SIDE :]
    count, width = arrived_ref.shape
    experts = router_ref.shape[1]
    quarter = slots // SIDE
    ids = ids_ref[...]
    first, second = ids[:, 0:1], ids[:, 1:2]
    lane = lax.broadcasted_iota(jnp.int32, (count, count), 1)
    row = lax.broadcasted_iota(jnp.int32, (count, count), 0)
    pick0 = (lane == first).astype(F32)
    pick1 = (lane == second).astype(F32)
    below = (row > lane).astype(F32).astype(BF16)
    before = jnp.dot(below, (pick0 + pick1).astype(BF16), preferred_element_type=F32)
    slot0 = first.astype(F32) * slots + jnp.sum(before * pick0, axis=1, keepdims=True)
    slot1 = second.astype(F32) * slots + jnp.sum(before * pick1, axis=1, keepdims=True)
    scores = jnp.dot(arrived_ref[...], router_ref[...], preferred_element_type=F32)
    left = jnp.sum(scores * pick0[:, :experts], axis=1, keepdims=True)
    right = jnp.sum(scores * pick1[:, :experts], axis=1, keepdims=True)
    weight0 = 1.0 / (1.0 + jnp.exp(right - left))
    weight1 = 1.0 / (1.0 + jnp.exp(left - right))
    meta = jnp.where(lane == 0, slot0, 0.0)
    meta = jnp.where(lane == 1, slot1, meta)
    meta = jnp.where(lane == 2, weight0, meta)
    meta = jnp.where(lane == 3, weight1, meta)
    meta_ref[...] = meta
    flat = meta.T
    total = SIDE * slots + slots
    target = slot_targets(pos_ref, lax.broadcasted_iota(jnp.int32, (total, count), 0), slots).astype(F32)
    hit0 = (target == flat[0:1, :]).astype(F32)
    hit1 = (target == flat[1:2, :]).astype(F32)
    scale = jnp.sum(hit0 * flat[2:3, :] + hit1 * flat[3:4, :], axis=1, keepdims=True)
    hits = (hit0 + hit1).astype(BF16)
    tile = column_tile(width)
    for start in range(0, width, tile):
        columns = slice(start, start + tile)
        rows = jnp.dot(hits, arrived_ref[:, columns], preferred_element_type=F32).astype(BF16)
        cot = (scale * jnp.dot(hits, upstream_ref[:, columns], preferred_element_type=F32)).astype(BF16)
        for by in range(SIDE):
            part = slice(by * slots, (by + 1) * slots)
            rows_out[by][:, columns] = rows[part]
            cot_out[by][:, columns] = cot[part]
            part = slice(SIDE * slots + by * quarter, SIDE * slots + (by + 1) * quarter)
            cross_out[by][0:quarter, columns] = rows[part]
            cross_out[by][quarter : 2 * quarter, columns] = cot[part]


def dispatch(position, routes, arrived, upstream, router, slots):
    count, width = arrived.shape
    experts = router.shape[1]
    quarter = slots // SIDE
    whole = lambda *shape: pl.BlockSpec(shape, lambda i, pos: (0,) * len(shape))
    outs = (
        [jax.ShapeDtypeStruct((count, count), F32)]
        + [jax.ShapeDtypeStruct((slots, width), BF16)] * (2 * SIDE)
        + [jax.ShapeDtypeStruct((2 * quarter, width), BF16)] * SIDE
    )
    results = pl.pallas_call(
        functools.partial(dispatch_kernel, slots),
        out_shape=outs,
        grid_spec=pltpu.PrefetchScalarGridSpec(
            num_scalar_prefetch=1,
            grid=(1,),
            in_specs=[
                pl.BlockSpec((count, 2), lambda i, pos: (pos[0], 0)),
                whole(count, width),
                whole(count, width),
                whole(width, experts),
            ],
            out_specs=[whole(*out.shape) for out in outs],
        ),
        compiler_params=pltpu.CompilerParams(vmem_limit_bytes=VMEM_LIMIT),
        cost_estimate=pl.CostEstimate(
            flops=4 * 5 * slots * count * width, bytes_accessed=16 * count * width, transcendentals=0
        ),
        name="dispatch",
    )(position, routes, arrived, upstream, router)
    return results[0], results[1 : 1 + SIDE], results[1 + SIDE : 1 + 2 * SIDE], results[1 + 2 * SIDE :]


def load_chunks(chunks, rows_v, sems):
    size = chunks[0].shape[0]
    copies = [
        pltpu.make_async_copy(chunk, rows_v.at[pl.ds(k * size, size)], sems.at[k])
        for k, chunk in enumerate(chunks)
    ]
    for copy in copies:
        copy.start()
    for copy in copies:
        copy.wait()


def forward_kernel(n_chunks, hidden_steps, *refs):
    chunks, refs = refs[:n_chunks], refs[n_chunks:]
    gate_ref, up_ref, down_ref, refs = refs[0], refs[1], refs[2], refs[3:]
    outs, refs = refs[:n_chunks], refs[n_chunks:]
    swished_ref, slope_ref, rows_v, hidden_v, sems = refs
    step = pl.program_id(0)
    size = outs[0].shape[0]
    tile = gate_ref.shape[1]

    @pl.when(step == 0)
    def _():
        load_chunks(chunks, rows_v, sems)

    @pl.when(step < hidden_steps)
    def _():
        gate_pre = jnp.dot(rows_v[...], gate_ref[...], preferred_element_type=F32)
        up_pre = jnp.dot(rows_v[...], up_ref[...], preferred_element_type=F32)
        sigmoid_part = jax.nn.sigmoid(gate_pre)
        swished = gate_pre * sigmoid_part
        swished_ref[...] = swished
        slope_ref[...] = up_pre * (sigmoid_part * (1.0 + gate_pre * (1.0 - sigmoid_part)))
        hidden_v[:, pl.ds(pl.multiple_of(step * tile, tile), tile)] = (swished * up_pre).astype(BF16)

    @pl.when(step >= hidden_steps)
    def _():
        out = jnp.dot(hidden_v[...], down_ref[...], preferred_element_type=F32).astype(BF16)
        for k, ref in enumerate(outs):
            ref[...] = out[k * size : (k + 1) * size]


def forward(chunks, w_gate, w_up, w_down):
    size, width = chunks[0].shape
    rows = size * len(chunks)
    units = w_gate.shape[1]
    unit_tile = 256 if units % 256 == 0 else units
    tile = column_tile(width)
    hidden_steps, out_steps = units // unit_tile, width // tile
    early = lambda i: (0, jnp.minimum(i, hidden_steps - 1))
    late = lambda i: (0, jnp.maximum(i - hidden_steps, 0))
    results = pl.pallas_call(
        functools.partial(forward_kernel, len(chunks), hidden_steps),
        out_shape=[jax.ShapeDtypeStruct((size, width), BF16)] * len(chunks)
        + [jax.ShapeDtypeStruct((rows, units), F32)] * 2,
        grid=(hidden_steps + out_steps,),
        in_specs=[pl.BlockSpec(memory_space=pl.ANY)] * len(chunks)
        + [
            pl.BlockSpec((width, unit_tile), early),
            pl.BlockSpec((width, unit_tile), early),
            pl.BlockSpec((units, tile), late),
        ],
        out_specs=[pl.BlockSpec((size, tile), late)] * len(chunks)
        + [pl.BlockSpec((rows, unit_tile), early)] * 2,
        scratch_shapes=[
            pltpu.VMEM((rows, width), BF16),
            pltpu.VMEM((rows, units), BF16),
            pltpu.SemaphoreType.DMA((len(chunks),)),
        ],
        compiler_params=pltpu.CompilerParams(vmem_limit_bytes=VMEM_LIMIT),
        cost_estimate=pl.CostEstimate(
            flops=6 * rows * width * units,
            bytes_accessed=6 * width * units + 4 * rows * width + 8 * rows * units,
            transcendentals=rows * units,
        ),
        name="expert_forward",
    )(*chunks, w_gate, w_up, w_down)
    return results[: len(chunks)], results[-2], results[-1]


def transposed_dot(a, b):
    return lax.dot_general(a, b, (((1,), (1,)), ((), ())), preferred_element_type=F32)


def backward_kernel(n_chunks, hidden_steps, *refs):
    chunks, refs = refs[:n_chunks], refs[n_chunks:]
    swished_ref, slope_ref, gate_ref, up_ref, down_ref, refs = *refs[:5], refs[5:]
    outs, refs = refs[:n_chunks], refs[n_chunks:]
    cot_v, d_gate_v, d_up_v, sems = refs
    step = pl.program_id(0)
    size = outs[0].shape[0]
    tile = swished_ref.shape[1]

    @pl.when(step == 0)
    def _():
        load_chunks(chunks, cot_v, sems)

    @pl.when(step < hidden_steps)
    def _():
        d_hidden = transposed_dot(cot_v[...], down_ref[...])
        units = pl.ds(pl.multiple_of(step * tile, tile), tile)
        d_up_v[:, units] = (d_hidden * swished_ref[...]).astype(BF16)
        d_gate_v[:, units] = (d_hidden * slope_ref[...]).astype(BF16)

    @pl.when(step >= hidden_steps)
    def _():
        out = transposed_dot(d_gate_v[...], gate_ref[...]) + transposed_dot(d_up_v[...], up_ref[...])
        out = out.astype(BF16)
        for k, ref in enumerate(outs):
            ref[...] = out[k * size : (k + 1) * size]


def backward(chunks, swished, slope, w_gate, w_up, w_down):
    size, width = chunks[0].shape
    rows = size * len(chunks)
    units = w_gate.shape[1]
    unit_tile = 256 if units % 256 == 0 else units
    tile = column_tile(width)
    hidden_steps, out_steps = units // unit_tile, width // tile
    early = lambda i: jnp.minimum(i, hidden_steps - 1)
    late = lambda i: jnp.maximum(i - hidden_steps, 0)
    return pl.pallas_call(
        functools.partial(backward_kernel, len(chunks), hidden_steps),
        out_shape=[jax.ShapeDtypeStruct((size, width), BF16)] * len(chunks),
        grid=(hidden_steps + out_steps,),
        in_specs=[pl.BlockSpec(memory_space=pl.ANY)] * len(chunks)
        + [
            pl.BlockSpec((rows, unit_tile), lambda i: (0, early(i))),
            pl.BlockSpec((rows, unit_tile), lambda i: (0, early(i))),
            pl.BlockSpec((tile, units), lambda i: (late(i), 0)),
            pl.BlockSpec((tile, units), lambda i: (late(i), 0)),
            pl.BlockSpec((unit_tile, width), lambda i: (early(i), 0)),
        ],
        out_specs=[pl.BlockSpec((size, tile), lambda i: (0, late(i)))] * len(chunks),
        scratch_shapes=[
            pltpu.VMEM((rows, width), BF16),
            pltpu.VMEM((rows, units), BF16),
            pltpu.VMEM((rows, units), BF16),
            pltpu.SemaphoreType.DMA((len(chunks),)),
        ],
        compiler_params=pltpu.CompilerParams(vmem_limit_bytes=VMEM_LIMIT),
        cost_estimate=pl.CostEstimate(
            flops=6 * rows * width * units,
            bytes_accessed=6 * width * units + 4 * rows * width + 8 * rows * units,
            transcendentals=0,
        ),
        name="expert_backward",
    )(*chunks, swished, slope, w_gate, w_up, w_down)


def sum_kernel(*refs):
    parts, outs = refs[:SIDE], refs[SIDE:]
    total = parts[0][...].astype(F32)
    for part in parts[1:]:
        total = total + part[...].astype(F32)
    total = total.astype(BF16)
    size = outs[0].shape[0]
    for k, ref in enumerate(outs):
        ref[...] = total[k * size : (k + 1) * size]


def sum_quarters(parts):
    rows, width = parts[0].shape
    return pl.pallas_call(
        sum_kernel,
        out_shape=[jax.ShapeDtypeStruct((rows // SIDE, width), BF16)] * SIDE,
        compiler_params=pltpu.CompilerParams(vmem_limit_bytes=VMEM_LIMIT),
        cost_estimate=pl.CostEstimate(
            flops=4 * rows * width, bytes_accessed=10 * rows * width, transcendentals=0
        ),
        name="sum_quarters",
    )(*parts)


def combine_kernel(weighted, pos_ref, meta_ref, *refs):
    direct, cross, refs = refs[:SIDE], refs[SIDE : 2 * SIDE], refs[2 * SIDE :]
    slots, width = direct[0].shape
    count = meta_ref.shape[0]
    meta = meta_ref[...]
    padded = 6 * slots
    target = slot_targets(pos_ref, lax.broadcasted_iota(jnp.int32, (count, padded), 1), slots).astype(F32)
    hit0 = (target == meta[:, 0:1]).astype(F32)
    hit1 = (target == meta[:, 1:2]).astype(F32)
    out_ref = refs[-1]
    tile = column_tile(width)
    blank = jnp.zeros((slots, tile), BF16)
    dots0 = dots1 = jnp.zeros((count, 1), F32)
    for start in range(0, width, tile):
        columns = slice(start, start + tile)
        terms = jnp.concatenate([ref[:, columns] for ref in direct + cross] + [blank], axis=0)
        if weighted:
            rows0 = jnp.dot(hit0.astype(BF16), terms, preferred_element_type=F32)
            rows1 = jnp.dot(hit1.astype(BF16), terms, preferred_element_type=F32)
            out_ref[:, columns] = (meta[:, 2:3] * rows0 + meta[:, 3:4] * rows1).astype(BF16)
            upstream = refs[0][:, columns].astype(F32)
            dots0 = dots0 + jnp.sum(upstream * rows0, axis=1, keepdims=True)
            dots1 = dots1 + jnp.sum(upstream * rows1, axis=1, keepdims=True)
        else:
            out_ref[:, columns] = jnp.dot((hit0 + hit1).astype(BF16), terms, preferred_element_type=F32).astype(BF16)
    if weighted:
        lane = lax.broadcasted_iota(jnp.int32, (count, 128), 1)
        high0, high1 = dots0.astype(BF16).astype(F32), dots1.astype(BF16).astype(F32)
        extra = jnp.where(lane == 0, high0, 0.0)
        extra = jnp.where(lane == 1, dots0 - high0, extra)
        extra = jnp.where(lane == 2, high1, extra)
        extra = jnp.where(lane == 3, dots1 - high1, extra)
        out_ref[:, width : width + 128] = extra.astype(BF16)


def combine(position, meta, direct, cross, upstream=None):
    weighted = upstream is not None
    slots, width = direct[0].shape
    count = meta.shape[0]
    vmem = pl.BlockSpec(memory_space=pltpu.VMEM)
    extra = [upstream] if weighted else []
    return pl.pallas_call(
        functools.partial(combine_kernel, weighted),
        out_shape=jax.ShapeDtypeStruct((count, width + (128 if weighted else 0)), BF16),
        in_specs=[pl.BlockSpec(memory_space=pltpu.SMEM)] + [vmem] * (1 + 2 * SIDE + len(extra)),
        out_specs=vmem,
        compiler_params=pltpu.CompilerParams(vmem_limit_bytes=VMEM_LIMIT),
        cost_estimate=pl.CostEstimate(
            flops=4 * count * 6 * slots * width, bytes_accessed=10 * slots * width + 4 * count * width, transcendentals=0
        ),
        name="combine",
    )(position, meta, *direct, *cross, *extra)


def finish_kernel(pos_ref, meta_ref, ids_ref, router_ref, out_ref, grad_ref, layer_ref, rows_ref):
    share = meta_ref.shape[0]
    width = layer_ref.shape[1]
    parts = out_ref.shape[0] // share
    total = out_ref[0:share, :].astype(F32)
    grads = grad_ref[0:share, :].astype(F32)
    for k in range(1, parts):
        total = total + out_ref[k * share : (k + 1) * share, :].astype(F32)
        grads = grads + grad_ref[k * share : (k + 1) * share, :].astype(F32)
    layer_ref[...] = total[:, :width].astype(BF16)
    extra = total[:, width : width + 128]
    d_gap = (extra[:, 0:1] + extra[:, 1:2]) - (extra[:, 2:3] + extra[:, 3:4])
    meta = meta_ref[...]
    d_left = meta[:, 2:3] * meta[:, 3:4] * d_gap
    d_left = d_left.astype(BF16).astype(F32)
    ids = ids_ref[...]
    for e in range(router_ref.shape[0]):
        sign = (ids[:, 0:1] == e).astype(F32) - (ids[:, 1:2] == e).astype(F32)
        grads = grads + (sign * d_left) * router_ref[e : e + 1, :]
    rows_ref[...] = grads.astype(BF16)


def finish(position, meta, routes, router_rows, out_parts, grad_parts, share):
    count, width = grad_parts.shape
    whole = lambda *shape: pl.BlockSpec(shape, lambda i, pos: (0,) * len(shape))
    return pl.pallas_call(
        finish_kernel,
        out_shape=[jax.ShapeDtypeStruct((share, width), BF16)] * 2,
        grid_spec=pltpu.PrefetchScalarGridSpec(
            num_scalar_prefetch=1,
            grid=(1,),
            in_specs=[
                pl.BlockSpec((share, meta.shape[1]), lambda i, pos: (pos[4], 0)),
                pl.BlockSpec((share, 2), lambda i, pos: (pos[5], 0)),
                whole(*router_rows.shape),
                whole(*out_parts.shape),
                whole(*grad_parts.shape),
            ],
            out_specs=[whole(share, width)] * 2,
        ),
        compiler_params=pltpu.CompilerParams(vmem_limit_bytes=VMEM_LIMIT),
        cost_estimate=pl.CostEstimate(flops=30 * count * width, bytes_accessed=4 * count * width, transcendentals=0),
        name="finish",
    )(position, meta, routes, router_rows, out_parts, grad_parts)


def exchange(x, axis):
    parts = lax.axis_size(axis)
    blocks = x.reshape(parts, x.shape[0] // parts, x.shape[1])
    return lax.all_to_all(blocks, axis, 0, 0).reshape(x.shape)


def gather_quarters(block):
    return [block] + [moved(block, "etp", 0, by) for by in range(1, SIDE)]


def send_back(chunks):
    direct, quarters = chunks[:SIDE], chunks[SIDE:]
    direct = [direct[0]] + [moved(direct[by], "expert", 0, -by) for by in range(1, SIDE)]
    quarters = [quarters[0]] + [moved(quarters[by], "etp", 0, -by) for by in range(1, SIDE)]
    cross = sum_quarters(quarters)
    cross = [moved(cross[by], "expert", 1, -by) for by in range(SIDE)]
    return direct, cross


def per_device(
    tokens_in, cotangent_in, expert_ids, router_weight, gate_weight, up_weight, down_weight
):
    swap = [(0, 1), (1, 0)]
    arrived = lax.ppermute(tokens_in[0], "pipe", swap)
    upstream = lax.ppermute(cotangent_in[0], "pipe", swap)
    routes = expert_ids[0]
    router = router_weight[0]
    w_gate = gate_weight[0, 0]
    w_up = up_weight[0, 0]
    w_down = down_weight[0, 0]
    count = arrived.shape[0]
    n_etp = lax.axis_size("etp")
    slots = 4 * count // lax.axis_size("expert")
    quarter = slots // SIDE
    share = count // n_etp
    group = lax.axis_index("expert")
    part = lax.axis_index("etp")
    position = jnp.stack([group, group // SIDE, group % SIDE, part % SIDE, part, group * n_etp + part]).astype(jnp.int32)
    meta, rows, cot, cross = dispatch(position, routes, arrived, upstream, router, slots)
    cross = [moved(cross[by], "expert", 1, by) for by in range(SIDE)]
    rows_direct = [rows[0]] + [moved(rows[by], "expert", 0, by) for by in range(1, SIDE)]
    rows_cross = gather_quarters(jnp.concatenate([c[:quarter] for c in cross], axis=0))
    cot_direct = [cot[0]] + [moved(cot[by], "expert", 0, by) for by in range(1, SIDE)]
    cot_cross = gather_quarters(jnp.concatenate([c[quarter:] for c in cross], axis=0))
    out_chunks, swished, slope = forward(rows_direct + rows_cross, w_gate, w_up, w_down)
    grad_chunks = backward(cot_direct + cot_cross, swished, slope, w_gate, w_up, w_down)
    out_direct, out_cross = send_back(out_chunks)
    out_terms = combine(position, meta, out_direct, out_cross, upstream)
    out_parts = exchange(out_terms, "etp")
    grad_direct, grad_cross = send_back(grad_chunks)
    grad_terms = combine(position, meta, grad_direct, grad_cross)
    grad_parts = exchange(grad_terms, "etp")
    router_rows = router.T.astype(F32)
    layer_rows, grad_rows = finish(position, meta, routes, router_rows, out_parts, grad_parts, share)
    return (layer_rows[None], grad_rows[None])


def solution(mesh):
    return jax.shard_map(
        per_device,
        mesh=mesh,
        in_specs=(
            P("pipe", "expert", None),
            P("pipe", "expert", None),
            P("pipe", None, None),
            P("pipe", None, None),
            P("pipe", "expert", None, "etp"),
            P("pipe", "expert", None, "etp"),
            P("pipe", "expert", "etp", None),
        ),
        out_specs=(P("pipe", ("expert", "etp"), None), P("pipe", ("expert", "etp"), None)),
        check_vma=False,
    )
```

time: 1370 us -> 233 us (0.17)
  waiting for transfers between devices: 1150 us -> 76.7 us
  starting transfers between devices: 0.5 us -> 82.9 us
  local copies, waits for them, and re-layouts: 80.7 us -> 10.4 us
  other arithmetic: 69.6 us -> 0.69 us
  Pallas kernels: 0 us -> 60.3 us
  matrix products: 50.3 us -> 0 us
    reduce_scatter x3 -> x0, waiting for transfers between devices: 1030 us -> none  [the longest x1 376 us: per_device(): lax.psum_scatter(term_out, ('expert', 'etp'), scatter_dimension=0, tiled=...]
    all_gather x2 -> x0, waiting for transfers between devices: 111 us -> none  [the longest x1 66.8 us: per_device(): lax.all_gather(arrived, 'expert', axis=0, tiled=True)]
    ppermute x2 -> x38, starting transfers between devices: 0.3 us -> 73.7 us  [the longest x36 73.1 us: moved(): return lax.ppermute(x, axis, pairs)]
    pallas_call x0 -> x8, Pallas kernels: none -> 60.3 us  [the longest x1 20 us: forward(): pl.pallas_call(functools.partial(forward_kernel, len(chunks), hidden_step...]
    scatter-add x3 -> x0, other arithmetic: 60 us -> none  [the longest x1 24.4 us: per_device(): term_weights = jnp.zeros((token_count, 2), jnp.float32).at[row_table, pic...]
    ppermute x2 -> x38, waiting for transfers between devices: 4.84 us -> 64.4 us  [the longest x36 64.4 us: moved(): return lax.ppermute(x, axis, pairs)]
    dot_general x8 -> x0, matrix products: 50.3 us -> none  [the longest x1 11 us: expert_pass(): expert_out = jnp.dot(hidden, w_down, preferred_element_type=jnp.float32)]
    gather x6 -> x0, local copies, waits for them, and re-layouts: 34.1 us -> none  [the longest x4 13.5 us: pair_weights(): chosen = jnp.take_along_axis(scores, routes, axis=1)]
  transfers between devices with their start and end apart: 7 -> 40, of which waited for: 7 -> 18; matrix products, arithmetic and copies ran while one was open for 7% -> 2% of each run, Pallas kernels for 0% -> 13%
where the time goes in v1:
time: 233 us; the launch traced here: 232 us
  starting transfers between devices  82.9 us (36%)
  waiting for transfers between devices  76.7 us (33%)
  Pallas kernels  60.3 us (26%)
  local copies, waits for them, and re-layouts  10.4 us (4%)
    ppermute x36, starting transfers between devices, moved(): return lax.ppermute(x, axis, pairs)  73.1 us
    ppermute x36, waiting for transfers between devices, moved(): return lax.ppermute(x, axis, pairs)  64.4 us
    pallas_call x1, Pallas kernels, forward(): pl.pallas_call(functools.partial(forward_kernel, len(chunks), hidden_step...  20 us
    pallas_call x1, Pallas kernels, backward(): pl.pallas_call(functools.partial(backward_kernel, len(chunks), hidden_ste...  19.8 us
    all_to_all x2, waiting for transfers between devices, exchange(): return lax.all_to_all(blocks, axis, 0, 0).reshape(x.shape)  12.2 us
    all_to_all x2, starting transfers between devices, exchange(): return lax.all_to_all(blocks, axis, 0, 0).reshape(x.shape)  9.14 us
    unnamed x89, local copies, waits for them, and re-layouts  7.75 us
    pallas_call x2, Pallas kernels, combine(): pl.pallas_call(functools.partial(combine_kernel, weighted), out_shape=jax...  6.91 us
  transfers between devices with their start and end apart: 40, of which 18 were waited for; matrix products, arithmetic and copies ran while one was open for 2% of the time, Pallas kernels for 13%

profile of v1, /device:TPU:0, one launch (start us, length us, event | category | flops | bytes accessed | tf_op | source)
XLA Modules:
  0.0 232.0 jit_solution(16426727519136135541)
XLA Ops:
  1.2 1.7 copy.9
  2.9 2.0 copy.10.router_ref
  4.9 0.7 stack.27.pos_ref
  5.6 0.9 copy-done.3
  6.7 5.9 %dispatch.1 = (f32[128,128]{1,0:T(8,128)}, bf16[64,3072]{1,0:T(8,128)(2,1)}, bf16[64,3072]{1,0:T(8,128)(2,1)}, bf16[64,3072]{1,0:T(8,128)(2,1)}, bf16[64,3072]{1...) custom-call(s32[6]{0:T(128)} %stack.27.pos_ref, ...), custom_call_target="tpu_custom_call" | custom-call | flops 503316480 | bytes 6291456 | tf_op jit(solution)/shard_map/dispatch/pallas_call | solution.py:93
  12.6 3.9 %collective-permute-start.8 = (bf16[32,3072]{1,0:T(8,128)(2,1)}, bf16[32,3072]{1,0:T(8,128)(2,1)S(1)}, u32[]{:S(2)}, u32[]{:S(2)}) collective-permute-start(bf16[32,3072]{1,0:T(8,128)(2,1)} %get-tuple-element.51), channel_id=1, source_target_pairs={{0,56},{8,32},{16,40},{24,48},{32,24},{40,0},{48,8},{56,16},{1,57}... | collective-permute-start | bytes 589832 | tf_op jit(solution)/shard_map/ppermute | solution.py:20
  16.5 2.3 collective-permute-start.3
  18.7 1.1 collective-permute-start.4
  19.9 2.6 %collective-permute-start.7 = (bf16[32,3072]{1,0:T(8,128)(2,1)}, bf16[32,3072]{1,0:T(8,128)(2,1)S(1)}, u32[]{:S(2)}, u32[]{:S(2)}) collective-permute-start(bf16[32,3072]{1,0:T(8,128)(2,1)} %get-tuple-element.50), channel_id=1, source_target_pairs={{0,48},{8,56},{16,32},{24,40},{32,16},{40,24},{48,0},{56,8},{1,49}... | collective-permute-start | bytes 589832 | tf_op jit(solution)/shard_map/ppermute | solution.py:20
  22.5 7.8 %collective-permute-done.8 = bf16[32,3072]{1,0:T(8,128)(2,1)S(1)} collective-permute-done((bf16[32,3072]{1,0:T(8,128)(2,1)}, bf16[32,3072]{1,0:T(8,128)(2,1)S(1)}, u32[]{:S(2)}, u32[]{:S(2)}) %collective-permute-start.8) | collective-permute-done | bytes 196640 | tf_op jit(solution)/shard_map/ppermute | solution.py:20
  30.3 11.2 %collective-permute-done.7 = bf16[32,3072]{1,0:T(8,128)(2,1)S(1)} collective-permute-done((bf16[32,3072]{1,0:T(8,128)(2,1)}, bf16[32,3072]{1,0:T(8,128)(2,1)S(1)}, u32[]{:S(2)}, u32[]{:S(2)}) %collective-permute-start.7) | collective-permute-done | bytes 196640 | tf_op jit(solution)/shard_map/ppermute | solution.py:20
  41.5 1.6 collective-permute-start.5
  43.1 2.4 %collective-permute-done.6 = bf16[32,3072]{1,0:T(8,128)(2,1)S(1)} collective-permute-done((bf16[32,3072]{1,0:T(8,128)(2,1)}, bf16[32,3072]{1,0:T(8,128)(2,1)S(1)}, u32[]{:S(2)}, u32[]{:S(2)}) %collective-permute-start.6) | collective-permute-done | bytes 196640 | tf_op jit(solution)/shard_map/ppermute | solution.py:20
  45.5 3.1 %collective-permute-start.22 = (bf16[64,3072]{1,0:T(8,128)(2,1)}, bf16[64,3072]{1,0:T(8,128)(2,1)S(1)}, u32[]{:S(2)}, u32[]{:S(2)}) collective-permute-start(bf16[64,3072]{1,0:T(8,128)(2,1)} %get-tuple-element.65), channel_id=1, source_target_pairs={{0,8},{8,16},{16,24},{24,0},{32,40},{40,48},{48,56},{56,32},{1,9},... | collective-permute-start | bytes 1179656 | tf_op jit(solution)/shard_map/ppermute | solution.py:20
  48.6 1.0 collective-permute-done.5
  49.7 2.0 collective-permute-start.9
  51.7 3.6 %collective-permute-start.10 = (bf16[64,3072]{1,0:T(8,128)(2,1)S(1)}, bf16[64,3072]{1,0:T(8,128)(2,1)S(1)}, u32[]{:S(2)}, u32[]{:S(2)}) collective-permute-start(bf16[64,3072]{1,0:T(8,128)(2,1)S(1)} %pad_maximum_fusion.refs_4_), channel_id=1, source_target_pairs={{0,2},{1,3},{2,0},{3,1},{4,6},{5,7},{6,4},{7,5},{8,10},{9,11},{10,... | collective-permute-start | bytes 1179656 | tf_op jit(solution)/shard_map/ppermute | solution.py:20
  55.3 1.0 collective-permute-start.11
  56.5 0.7 collective-permute-done.22.refs_1_
  57.2 5.1 %collective-permute-start.24 = (bf16[64,3072]{1,0:T(8,128)(2,1)}, bf16[64,3072]{1,0:T(8,128)(2,1)S(1)}, u32[]{:S(2)}, u32[]{:S(2)}) collective-permute-start(bf16[64,3072]{1,0:T(8,128)(2,1)} %get-tuple-element.67), channel_id=1, source_target_pairs={{0,24},{8,0},{16,8},{24,16},{32,56},{40,32},{48,40},{56,48},{1,25}... | collective-permute-start | bytes 1179656 | tf_op jit(solution)/shard_map/ppermute | solution.py:20
  62.3 0.8 collective-permute-done.9.refs_5_
  63.1 7.0 %collective-permute-start.25 = (bf16[64,3072]{1,0:T(8,128)(2,1)S(1)}, bf16[64,3072]{1,0:T(8,128)(2,1)S(1)}, u32[]{:S(2)}, u32[]{:S(2)}) collective-permute-start(bf16[64,3072]{1,0:T(8,128)(2,1)S(1)} %pad_maximum_fusion.1.refs_4_), channel_id=1, source_target_pairs={{0,1},{1,2},{2,3},{3,0},{4,5},{5,6},{6,7},{7,4},{8,9},{9,10},{10,1... | collective-permute-start | bytes 1179656 | tf_op jit(solution)/shard_map/ppermute | solution.py:20
  70.2 3.5 %collective-permute-done.10.refs_6_ = bf16[64,3072]{1,0:T(8,128)(2,1)S(1)} collective-permute-done((bf16[64,3072]{1,0:T(8,128)(2,1)S(1)}, bf16[64,3072]{1,0:T(8,128)(2,1)S(1)}, u32[]{:S(2)}, u32[]{:S(2)}) %collective-permute-start.10) | collective-permute-done | bytes 393248 | tf_op jit(solution)/shard_map/ppermute | solution.py:20
  73.7 2.1 collective-permute-start.27
  75.9 20.0 %expert_forward.1 = (bf16[64,3072]{1,0:T(8,128)(2,1)}, bf16[64,3072]{1,0:T(8,128)(2,1)}, bf16[64,3072]{1,0:T(8,128)(2,1)}, bf16[64,3072]{1,0:T(8,128)(2,1)}, bf1...) custom-call(bf16[64,3072]{1,0:T(8,128)(2,1)} %get-tuple-element.44.r, ...), custom_call_target="tpu_custom_call" | custom-call | flops 9663676416 | bytes 29360128 | tf_op jit(solution)/shard_map/expert_forward/pallas_call | solution.py:167
  96.0 0.6 copy-done.37
  97.2 19.8 %expert_backward.1 = (bf16[64,3072]{1,0:T(8,128)(2,1)}, bf16[64,3072]{1,0:T(8,128)(2,1)}, bf16[64,3072]{1,0:T(8,128)(2,1)}, bf16[64,3072]{1,0:T(8,128)(2,1)}, bf...) custom-call(bf16[64,3072]{1,0:T(8,128)(2,1)} %get-tuple-element.64.refs_, ...), custom_call_target="tpu_custom_call" | custom-call | flops 9663676416 | bytes 29360128 | tf_op jit(solution)/shard_map/expert_backward/pallas_call | solution.py:237
  117.0 2.2 collective-permute-start.31
  119.4 1.3 collective-permute-start.33
  120.8 2.8 %collective-permute-start.28 = (bf16[64,3072]{1,0:T(8,128)(2,1)}, bf16[64,3072]{1,0:T(8,128)(2,1)S(1)}, u32[]{:S(2)}, u32[]{:S(2)}) collective-permute-start(bf16[64,3072]{1,0:T(8,128)(2,1)} %get-tuple-element.71), channel_id=1, source_target_pairs={{0,24},{8,0},{16,8},{24,16},{32,56},{40,32},{48,40},{56,48},{1,25}... | collective-permute-start | bytes 1179656 | tf_op jit(solution)/shard_map/ppermute | solution.py:20
  123.6 2.5 %collective-permute-start.29 = (bf16[64,3072]{1,0:T(8,128)(2,1)}, bf16[64,3072]{1,0:T(8,128)(2,1)S(1)}, u32[]{:S(2)}, u32[]{:S(2)}) collective-permute-start(bf16[64,3072]{1,0:T(8,128)(2,1)} %get-tuple-element.72), channel_id=1, source_target_pairs={{0,16},{8,24},{16,0},{24,8},{32,48},{40,56},{48,32},{56,40},{1,17}... | collective-permute-start | bytes 1179656 | tf_op jit(solution)/shard_map/ppermute | solution.py:20
  126.1 3.4 %collective-permute-done.31.refs_1_ = bf16[64,3072]{1,0:T(8,128)(2,1)S(1)} collective-permute-done((bf16[64,3072]{1,0:T(8,128)(2,1)}, bf16[64,3072]{1,0:T(8,128)(2,1)S(1)}, u32[]{:S(2)}, u32[]{:S(2)}) %collective-permute-start.31) | collective-permute-done | bytes 393248 | tf_op jit(solution)/shard_map/ppermute | solution.py:20
  129.5 3.2 %collective-permute-start.30 = (bf16[64,3072]{1,0:T(8,128)(2,1)}, bf16[64,3072]{1,0:T(8,128)(2,1)S(1)}, u32[]{:S(2)}, u32[]{:S(2)}) collective-permute-start(bf16[64,3072]{1,0:T(8,128)(2,1)} %get-tuple-element.73), channel_id=1, source_target_pairs={{0,8},{8,16},{16,24},{24,0},{32,40},{40,48},{48,56},{56,32},{1,9},... | collective-permute-start | bytes 1179656 | tf_op jit(solution)/shard_map/ppermute | solution.py:20
  133.0 6.7 %collective-permute-start.15 = (bf16[64,3072]{1,0:T(8,128)(2,1)}, bf16[64,3072]{1,0:T(8,128)(2,1)S(1)}, u32[]{:S(2)}, u32[]{:S(2)}) collective-permute-start(bf16[64,3072]{1,0:T(8,128)(2,1)} %get-tuple-element.57), channel_id=1, source_target_pairs={{0,3},{1,0},{2,1},{3,2},{4,7},{5,4},{6,5},{7,6},{8,11},{9,8},{10,9... | collective-permute-start | bytes 1179656 | tf_op jit(solution)/shard_map/ppermute | solution.py:20
  139.7 0.7 copy-done.12
  140.5 2.2 sum_quarters.3
  142.7 1.5 collective-permute-start.34
  144.2 2.5 %collective-permute-start.35 = (bf16[16,3072]{1,0:T(8,128)(2,1)}, bf16[16,3072]{1,0:T(8,128)(2,1)S(1)}, u32[]{:S(2)}, u32[]{:S(2)}) collective-permute-start(bf16[16,3072]{1,0:T(8,128)(2,1)} %get-tuple-element.79), channel_id=1, source_target_pairs={{0,56},{8,32},{16,40},{24,48},{32,24},{40,0},{48,8},{56,16},{1,57}... | collective-permute-start | bytes 294920 | tf_op jit(solution)/shard_map/ppermute | solution.py:20
  146.7 3.1 %collective-permute-start.36 = (bf16[16,3072]{1,0:T(8,128)(2,1)}, bf16[16,3072]{1,0:T(8,128)(2,1)S(1)}, u32[]{:S(2)}, u32[]{:S(2)}) collective-permute-start(bf16[16,3072]{1,0:T(8,128)(2,1)} %get-tuple-element.80), channel_id=1, source_target_pairs={{0,48},{8,56},{16,32},{24,40},{32,16},{40,24},{48,0},{56,8},{1,49}... | collective-permute-start | bytes 294920 | tf_op jit(solution)/shard_map/ppermute | solution.py:20
  150.3 3.7 %collective-permute-done.36.refs_6_ = bf16[16,3072]{1,0:T(8,128)(2,1)S(1)} collective-permute-done((bf16[16,3072]{1,0:T(8,128)(2,1)}, bf16[16,3072]{1,0:T(8,128)(2,1)S(1)}, u32[]{:S(2)}, u32[]{:S(2)}) %collective-permute-start.36) | collective-permute-done | bytes 98336 | tf_op jit(solution)/shard_map/ppermute | solution.py:20
  154.0 2.7 %collective-permute-done.37.refs_7_ = bf16[16,3072]{1,0:T(8,128)(2,1)S(1)} collective-permute-done((bf16[16,3072]{1,0:T(8,128)(2,1)}, bf16[16,3072]{1,0:T(8,128)(2,1)S(1)}, u32[]{:S(2)}, u32[]{:S(2)}) %collective-permute-start.37) | collective-permute-done | bytes 98336 | tf_op jit(solution)/shard_map/ppermute | solution.py:20
  156.7 0.6 copy-done.22
  157.3 3.0 %combine.3 = bf16[128,3072]{1,0:T(8,128)(2,1)} custom-call(s32[6]{0:T(128)} %stack.27.pos_ref, f32[128,128]{1,0:T(8,128)} %get-tuple-element.43.meta_ref, bf16[64,3072]{1,0:T(8,128)(2,1)} %get-tuple-element.70.refs_0_, bf16[64,3072]{1,0:T(8,128)(2,1)} %copy-done.4, bf16[64,3072]{1,0:T(8,128)(2,1)} %copy-done.5, bf16[64,3072]{1,0:T(8,128)(2,1)} %copy-done.6, ...), custom_call_target="tpu_custom_call" | custom-call | flops 603979776 | bytes 3538944 | tf_op jit(solution)/shard_map/combine/pallas_call | solution.py:331
  160.3 4.1 %all-to-all-start.1 = ((bf16[8,16,3072]{2,1,0:T(8,128)(2,1)}), bf16[8,16,3072]{2,1,0:T(8,128)(2,1)S(1)}, u32[]{:S(2)}, u32[]{:S(2)}) async-start(bf16[8,16,3072]{2,1,0:T(8,128)(2,1)} %bitcast.27), calls=%async_computation.1 | async-start | bytes 1572864 | tf_op jit(solution)/shard_map/all_to_all | solution.py:393
  164.5 3.5 %collective-permute-start.16 = (bf16[64,3072]{1,0:T(8,128)(2,1)S(1)}, bf16[64,3072]{1,0:T(8,128)(2,1)S(1)}, u32[]{:S(2)}, u32[]{:S(2)}) collective-permute-start(bf16[64,3072]{1,0:T(8,128)(2,1)S(1)} %copy-done.31), channel_id=1, source_target_pairs={{0,2},{1,3},{2,0},{3,1},{4,6},{5,7},{6,4},{7,5},{8,10},{9,11},{10,... | collective-permute-start | bytes 1179656 | tf_op jit(solution)/shard_map/ppermute | solution.py:20
  168.7 1.3 collective-permute-start.13
  170.0 0.7 collective-permute-start.14
  170.7 16.0 %collective-permute-done.16.refs_2_ = bf16[64,3072]{1,0:T(8,128)(2,1)S(1)} collective-permute-done((bf16[64,3072]{1,0:T(8,128)(2,1)S(1)}, bf16[64,3072]{1,0:T(8,128)(2,1)S(1)}, u32[]{:S(2)}, u32[]{:S(2)}) %collective-permute-start.16) | collective-permute-done | bytes 393248 | tf_op jit(solution)/shard_map/ppermute | solution.py:20
  186.7 5.1 %collective-permute-done.17.refs_3_ = bf16[64,3072]{1,0:T(8,128)(2,1)S(1)} collective-permute-done((bf16[64,3072]{1,0:T(8,128)(2,1)S(1)}, bf16[64,3072]{1,0:T(8,128)(2,1)S(1)}, u32[]{:S(2)}, u32[]{:S(2)}) %collective-permute-start.17) | collective-permute-done | bytes 393248 | tf_op jit(solution)/shard_map/ppermute | solution.py:20
  191.7 0.7 copy-done.14
  192.5 2.2 sum_quarters.2
  194.7 0.7 collective-permute-start.18
  195.4 0.8 collective-permute-start.19
  196.2 1.8 collective-permute-start.20
  198.0 2.1 collective-permute-start.21
  200.1 3.0 %collective-permute-done.18.refs_4_ = bf16[16,3072]{1,0:T(8,128)(2,1)S(1)} collective-permute-done((bf16[16,3072]{1,0:T(8,128)(2,1)}, bf16[16,3072]{1,0:T(8,128)(2,1)S(1)}, u32[]{:S(2)}, u32[]{:S(2)}) %collective-permute-start.18) | collective-permute-done | bytes 98336 | tf_op jit(solution)/shard_map/ppermute | solution.py:20
  203.1 1.5 collective-permute-done.20.refs_6_
  204.6 0.7 collective-permute-done.21.refs_7_
  205.9 3.9 %combine.2 = bf16[128,3200]{1,0:T(8,128)(2,1)} custom-call(s32[6]{0:T(128)} %stack.27.pos_ref, f32[128,128]{1,0:T(8,128)} %get-tuple-element.43.meta_ref, bf16[64,3072]{1,0:T(8,128)(2,1)} %get-tuple-element.52.refs_0_, bf16[64,3072]{1,0:T(8,128)(2,1)} %copy-done.15, bf16[64,3072]{1,0:T(8,128)(2,1)} %copy-done.16, bf16[64,3072]{1,0:T(8,128)(2,1)} %copy-done.17, ...), custom_call_target="tpu_custom_call" | custom-call | flops 603979776 | bytes 3538944 | tf_op jit(solution)/shard_map/combine/pallas_call | solution.py:331
  209.8 5.0 %all-to-all-start = ((bf16[8,16,3200]{2,1,0:T(8,128)(2,1)}), bf16[8,16,3200]{2,1,0:T(8,128)(2,1)S(1)}, u32[]{:S(2)}, u32[]{:S(2)}) async-start(bf16[8,16,3200]{2,1,0:T(8,128)(2,1)} %bitcast.25), calls=%async_computation | async-start | bytes 1638400 | tf_op jit(solution)/shard_map/all_to_all | solution.py:393
  214.8 0.6 convert_bitcast_fusion.router_ref
  215.5 12.2 %all-to-all-done = bf16[8,16,3200]{2,1,0:T(8,128)(2,1)S(1)} async-done(((bf16[8,16,3200]{2,1,0:T(8,128)(2,1)}), bf16[8,16,3200]{2,1,0:T(8,128)(2,1)S(1)}, u32[]{:S(2)}, u32[]{:S(2)}) %all-to-all-start) | async-done | bytes 819232 | tf_op jit(solution)/shard_map/all_to_all | solution.py:393
  227.7 0.9 copy-done
  228.6 3.4 %finish.1 = (bf16[16,3072]{1,0:T(8,128)(2,1)}, bf16[16,3072]{1,0:T(8,128)(2,1)}) custom-call(s32[6]{0:T(128)} %stack.27.pos_ref, f32[128,128]{1,0:T(8,128)} %get-tuple-element.43.meta_ref, s32[1024,2]{1,0:T(8,128)} %bitcast.23, f32[8,3072]{1,0:T(8,128)} %convert_bitcast_fusion.router_ref, bf16[128,3200]{1,0:T(8,128)(2,1)} %bitcast.24, bf16[128,3072]{1,0:T(8,128)(2,1)} %bitcast.26), custom_call_target="tpu_custom_call" | custom-call | flops 11796480 | bytes 1572864 | tf_op jit(solution)/shard_map/finish/pallas_call | solution.py:369
  (122 shorter events, 4.1 us)
Async XLA Ops:
  0.6 5.0 %collective-permute-start = (bf16[128,3072]{1,0:T(8,128)(2,1)}, bf16[128,3072]{1,0:T(8,128)(2,1)S(1)}, u32[]{:S(2)}, u32[]{:S(2)}) collective-permute-start(bf16[128,3072]{1,0:T(8,128)(2,1)} %bitcast.35), channel_id=1, source_target_pairs={{0,64},{64,0},{1,65},{65,1},{2,66},{66,2},{3,67},{67,3},{4,68},{68... | collective-permute-start | bytes 2359304 | tf_op jit(solution)/shard_map/ppermute | solution.py:413
  0.7 4.9 %collective-permute-start.1 = (bf16[128,3072]{1,0:T(8,128)(2,1)}, bf16[128,3072]{1,0:T(8,128)(2,1)S(1)}, u32[]{:S(2)}, u32[]{:S(2)}) collective-permute-start(bf16[128,3072]{1,0:T(8,128)(2,1)} %bitcast.36), channel_id=1, source_target_pairs={{0,64},{64,0},{1,65},{65,1},{2,66},{66,2},{3,67},{67,3},{4,68},{68... | collective-permute-start | bytes 2359304 | tf_op jit(solution)/shard_map/ppermute | solution.py:414
  12.6 17.7 %collective-permute-start.8 = (bf16[32,3072]{1,0:T(8,128)(2,1)}, bf16[32,3072]{1,0:T(8,128)(2,1)S(1)}, u32[]{:S(2)}, u32[]{:S(2)}) collective-permute-start(bf16[32,3072]{1,0:T(8,128)(2,1)} %get-tuple-element.51), channel_id=1, source_target_pairs={{0,56},{8,32},{16,40},{24,48},{32,24},{40,0},{48,8},{56,16},{1,57}... | collective-permute-start | bytes 589832 | tf_op jit(solution)/shard_map/ppermute | solution.py:20
  16.4 35.3 %collective-permute-start.2 = (bf16[64,3072]{1,0:T(8,128)(2,1)}, bf16[64,3072]{1,0:T(8,128)(2,1)S(1)}, u32[]{:S(2)}, u32[]{:S(2)}) collective-permute-start(bf16[64,3072]{1,0:T(8,128)(2,1)} %get-tuple-element.45), channel_id=1, source_target_pairs={{0,8},{8,16},{16,24},{24,0},{32,40},{40,48},{48,56},{56,32},{1,9},... | collective-permute-start | bytes 1179656 | tf_op jit(solution)/shard_map/ppermute | solution.py:20
  16.5 38.8 %collective-permute-start.3 = (bf16[64,3072]{1,0:T(8,128)(2,1)}, bf16[64,3072]{1,0:T(8,128)(2,1)S(1)}, u32[]{:S(2)}, u32[]{:S(2)}) collective-permute-start(bf16[64,3072]{1,0:T(8,128)(2,1)} %get-tuple-element.46), channel_id=1, source_target_pairs={{0,16},{8,24},{16,0},{24,8},{32,48},{40,56},{48,32},{56,40},{1,17}... | collective-permute-start | bytes 1179656 | tf_op jit(solution)/shard_map/ppermute | solution.py:20
  18.7 37.6 %collective-permute-start.4 = (bf16[64,3072]{1,0:T(8,128)(2,1)}, bf16[64,3072]{1,0:T(8,128)(2,1)S(1)}, u32[]{:S(2)}, u32[]{:S(2)}) collective-permute-start(bf16[64,3072]{1,0:T(8,128)(2,1)} %get-tuple-element.47), channel_id=1, source_target_pairs={{0,24},{8,0},{16,8},{24,16},{32,56},{40,32},{48,40},{56,48},{1,25}... | collective-permute-start | bytes 1179656 | tf_op jit(solution)/shard_map/ppermute | solution.py:20
  19.9 21.6 %collective-permute-start.7 = (bf16[32,3072]{1,0:T(8,128)(2,1)}, bf16[32,3072]{1,0:T(8,128)(2,1)S(1)}, u32[]{:S(2)}, u32[]{:S(2)}) collective-permute-start(bf16[32,3072]{1,0:T(8,128)(2,1)} %get-tuple-element.50), channel_id=1, source_target_pairs={{0,48},{8,56},{16,32},{24,40},{32,16},{40,24},{48,0},{56,8},{1,49}... | collective-permute-start | bytes 589832 | tf_op jit(solution)/shard_map/ppermute | solution.py:20
  30.3 15.2 %collective-permute-start.6 = (bf16[32,3072]{1,0:T(8,128)(2,1)}, bf16[32,3072]{1,0:T(8,128)(2,1)S(1)}, u32[]{:S(2)}, u32[]{:S(2)}) collective-permute-start(bf16[32,3072]{1,0:T(8,128)(2,1)} %get-tuple-element.49), channel_id=1, source_target_pairs={{0,40},{8,48},{16,56},{24,32},{32,8},{40,16},{48,24},{56,0},{1,41}... | collective-permute-start | bytes 589832 | tf_op jit(solution)/shard_map/ppermute | solution.py:20
  41.5 8.1 %collective-permute-start.5 = (bf16[32,3072]{1,0:T(8,128)(2,1)}, bf16[32,3072]{1,0:T(8,128)(2,1)S(1)}, u32[]{:S(2)}, u32[]{:S(2)}) collective-permute-start(bf16[32,3072]{1,0:T(8,128)(2,1)} %get-tuple-element.48), channel_id=1, source_target_pairs={{0,32},{8,40},{16,48},{24,56},{32,0},{40,8},{48,16},{56,24},{1,33}... | collective-permute-start | bytes 589832 | tf_op jit(solution)/shard_map/ppermute | solution.py:20
  45.5 11.7 %collective-permute-start.22 = (bf16[64,3072]{1,0:T(8,128)(2,1)}, bf16[64,3072]{1,0:T(8,128)(2,1)S(1)}, u32[]{:S(2)}, u32[]{:S(2)}) collective-permute-start(bf16[64,3072]{1,0:T(8,128)(2,1)} %get-tuple-element.65), channel_id=1, source_target_pairs={{0,8},{8,16},{16,24},{24,0},{32,40},{40,48},{48,56},{56,32},{1,9},... | collective-permute-start | bytes 1179656 | tf_op jit(solution)/shard_map/ppermute | solution.py:20
  49.7 26.1 %copy-start.8 = (bf16[64,3072]{1,0:T(8,128)(2,1)}, bf16[64,3072]{1,0:T(8,128)(2,1)S(1)}, u32[]{:S(2)}) copy-start(bf16[64,3072]{1,0:T(8,128)(2,1)S(1)} %pad_maximum_fusion.refs_4_) | copy-start | bytes 1179652
  49.7 13.4 %collective-permute-start.9 = (bf16[64,3072]{1,0:T(8,128)(2,1)S(1)}, bf16[64,3072]{1,0:T(8,128)(2,1)S(1)}, u32[]{:S(2)}, u32[]{:S(2)}) collective-permute-start(bf16[64,3072]{1,0:T(8,128)(2,1)S(1)} %pad_maximum_fusion.refs_4_), channel_id=1, source_target_pairs={{0,1},{1,2},{2,3},{3,0},{4,5},{5,6},{6,7},{7,4},{8,9},{9,10},{10,1... | collective-permute-start | bytes 1179656 | tf_op jit(solution)/shard_map/ppermute | solution.py:20
  51.7 24.1 %copy-start.32 = (bf16[64,3072]{1,0:T(8,128)(2,1)}, bf16[64,3072]{1,0:T(8,128)(2,1)S(1)}, u32[]{:S(2)}) copy-start(bf16[64,3072]{1,0:T(8,128)(2,1)S(1)} %collective-permute-done.2.refs_1_) | copy-start | bytes 1179652
  51.7 22.0 %collective-permute-start.10 = (bf16[64,3072]{1,0:T(8,128)(2,1)S(1)}, bf16[64,3072]{1,0:T(8,128)(2,1)S(1)}, u32[]{:S(2)}, u32[]{:S(2)}) collective-permute-start(bf16[64,3072]{1,0:T(8,128)(2,1)S(1)} %pad_maximum_fusion.refs_4_), channel_id=1, source_target_pairs={{0,2},{1,3},{2,0},{3,1},{4,6},{5,7},{6,4},{7,5},{8,10},{9,11},{10,... | collective-permute-start | bytes 1179656 | tf_op jit(solution)/shard_map/ppermute | solution.py:20
  55.3 20.5 %copy-start.33 = (bf16[64,3072]{1,0:T(8,128)(2,1)}, bf16[64,3072]{1,0:T(8,128)(2,1)S(1)}, u32[]{:S(2)}) copy-start(bf16[64,3072]{1,0:T(8,128)(2,1)S(1)} %collective-permute-done.3.refs_2_) | copy-start | bytes 1179652
  55.3 18.4 %collective-permute-start.11 = (bf16[64,3072]{1,0:T(8,128)(2,1)S(1)}, bf16[64,3072]{1,0:T(8,128)(2,1)S(1)}, u32[]{:S(2)}, u32[]{:S(2)}) collective-permute-start(bf16[64,3072]{1,0:T(8,128)(2,1)S(1)} %pad_maximum_fusion.refs_4_), channel_id=1, source_target_pairs={{0,3},{1,0},{2,1},{3,2},{4,7},{5,4},{6,5},{7,6},{8,11},{9,8},{10,9... | collective-permute-start | bytes 1179656 | tf_op jit(solution)/shard_map/ppermute | solution.py:20
  56.3 39.6 %copy-start.7 = (bf16[64,3072]{1,0:T(8,128)(2,1)}, bf16[64,3072]{1,0:T(8,128)(2,1)S(1)}, u32[]{:S(2)}) copy-start(bf16[64,3072]{1,0:T(8,128)(2,1)S(1)} %pad_maximum_fusion.1.refs_4_) | copy-start | bytes 1179652
  56.4 19.5 %copy-start.34 = (bf16[64,3072]{1,0:T(8,128)(2,1)}, bf16[64,3072]{1,0:T(8,128)(2,1)S(1)}, u32[]{:S(2)}) copy-start(bf16[64,3072]{1,0:T(8,128)(2,1)S(1)} %collective-permute-done.4.refs_3_) | copy-start | bytes 1179652
  56.4 39.5 %collective-permute-start.23 = (bf16[64,3072]{1,0:T(8,128)(2,1)}, bf16[64,3072]{1,0:T(8,128)(2,1)S(1)}, u32[]{:S(2)}, u32[]{:S(2)}) collective-permute-start(bf16[64,3072]{1,0:T(8,128)(2,1)} %get-tuple-element.66), channel_id=1, source_target_pairs={{0,16},{8,24},{16,0},{24,8},{32,48},{40,56},{48,32},{56,40},{1,17}... | collective-permute-start | bytes 1179656 | tf_op jit(solution)/shard_map/ppermute | solution.py:20
  57.2 38.7 %copy-start.35 = (bf16[64,3072]{1,0:T(8,128)(2,1)}, bf16[64,3072]{1,0:T(8,128)(2,1)S(1)}, u32[]{:S(2)}) copy-start(bf16[64,3072]{1,0:T(8,128)(2,1)S(1)} %collective-permute-done.22.refs_1_) | copy-start | bytes 1179652
  57.2 38.7 %collective-permute-start.24 = (bf16[64,3072]{1,0:T(8,128)(2,1)}, bf16[64,3072]{1,0:T(8,128)(2,1)S(1)}, u32[]{:S(2)}, u32[]{:S(2)}) collective-permute-start(bf16[64,3072]{1,0:T(8,128)(2,1)} %get-tuple-element.67), channel_id=1, source_target_pairs={{0,24},{8,0},{16,8},{24,16},{32,56},{40,32},{48,40},{56,48},{1,25}... | collective-permute-start | bytes 1179656 | tf_op jit(solution)/shard_map/ppermute | solution.py:20
  63.1 12.7 %copy-start.36 = (bf16[64,3072]{1,0:T(8,128)(2,1)}, bf16[64,3072]{1,0:T(8,128)(2,1)S(1)}, u32[]{:S(2)}) copy-start(bf16[64,3072]{1,0:T(8,128)(2,1)S(1)} %collective-permute-done.9.refs_5_) | copy-start | bytes 1179652
  63.1 32.8 %collective-permute-start.25 = (bf16[64,3072]{1,0:T(8,128)(2,1)S(1)}, bf16[64,3072]{1,0:T(8,128)(2,1)S(1)}, u32[]{:S(2)}, u32[]{:S(2)}) collective-permute-start(bf16[64,3072]{1,0:T(8,128)(2,1)S(1)} %pad_maximum_fusion.1.refs_4_), channel_id=1, source_target_pairs={{0,1},{1,2},{2,3},{3,0},{4,5},{5,6},{6,7},{7,4},{8,9},{9,10},{10,1... | collective-permute-start | bytes 1179656 | tf_op jit(solution)/shard_map/ppermute | solution.py:20
  73.7 22.3 %collective-permute-start.26 = (bf16[64,3072]{1,0:T(8,128)(2,1)S(1)}, bf16[64,3072]{1,0:T(8,128)(2,1)S(1)}, u32[]{:S(2)}, u32[]{:S(2)}) collective-permute-start(bf16[64,3072]{1,0:T(8,128)(2,1)S(1)} %pad_maximum_fusion.1.refs_4_), channel_id=1, source_target_pairs={{0,2},{1,3},{2,0},{3,1},{4,6},{5,7},{6,4},{7,5},{8,10},{9,11},{10,... | collective-permute-start | bytes 1179656 | tf_op jit(solution)/shard_map/ppermute | solution.py:20
  73.7 22.3 %collective-permute-start.27 = (bf16[64,3072]{1,0:T(8,128)(2,1)S(1)}, bf16[64,3072]{1,0:T(8,128)(2,1)S(1)}, u32[]{:S(2)}, u32[]{:S(2)}) collective-permute-start(bf16[64,3072]{1,0:T(8,128)(2,1)S(1)} %pad_maximum_fusion.1.refs_4_), channel_id=1, source_target_pairs={{0,3},{1,0},{2,1},{3,2},{4,7},{5,4},{6,5},{7,6},{8,11},{9,8},{10,9... | collective-permute-start | bytes 1179656 | tf_op jit(solution)/shard_map/ppermute | solution.py:20
  97.2 67.3 %copy-start.31 = (bf16[64,3072]{1,0:T(8,128)(2,1)S(1)}, bf16[64,3072]{1,0:T(8,128)(2,1)}, u32[]{:S(2)}) copy-start(bf16[64,3072]{1,0:T(8,128)(2,1)} %get-tuple-element.58) | copy-start | bytes 1179652
  97.2 70.8 %copy-start.30 = (bf16[64,3072]{1,0:T(8,128)(2,1)S(1)}, bf16[64,3072]{1,0:T(8,128)(2,1)}, u32[]{:S(2)}) copy-start(bf16[64,3072]{1,0:T(8,128)(2,1)} %get-tuple-element.59) | copy-start | bytes 1179652
  97.2 71.4 %copy-start.29 = (bf16[64,3072]{1,0:T(8,128)(2,1)S(1)}, bf16[64,3072]{1,0:T(8,128)(2,1)}, u32[]{:S(2)}) copy-start(bf16[64,3072]{1,0:T(8,128)(2,1)} %get-tuple-element.53) | copy-start | bytes 1179652
  97.2 71.5 %copy-start.28 = (bf16[64,3072]{1,0:T(8,128)(2,1)S(1)}, bf16[64,3072]{1,0:T(8,128)(2,1)}, u32[]{:S(2)}) copy-start(bf16[64,3072]{1,0:T(8,128)(2,1)} %get-tuple-element.54) | copy-start | bytes 1179652
  97.2 72.8 %copy-start.27 = (bf16[64,3072]{1,0:T(8,128)(2,1)S(1)}, bf16[64,3072]{1,0:T(8,128)(2,1)}, u32[]{:S(2)}) copy-start(bf16[64,3072]{1,0:T(8,128)(2,1)} %get-tuple-element.55) | copy-start | bytes 1179652
  117.0 12.5 %collective-permute-start.31 = (bf16[64,3072]{1,0:T(8,128)(2,1)}, bf16[64,3072]{1,0:T(8,128)(2,1)S(1)}, u32[]{:S(2)}, u32[]{:S(2)}) collective-permute-start(bf16[64,3072]{1,0:T(8,128)(2,1)} %get-tuple-element.75), channel_id=1, source_target_pairs={{0,3},{1,0},{2,1},{3,2},{4,7},{5,4},{6,5},{7,6},{8,11},{9,8},{10,9... | collective-permute-start | bytes 1179656 | tf_op jit(solution)/shard_map/ppermute | solution.py:20
  119.2 13.8 %collective-permute-start.32 = (bf16[64,3072]{1,0:T(8,128)(2,1)}, bf16[64,3072]{1,0:T(8,128)(2,1)S(1)}, u32[]{:S(2)}, u32[]{:S(2)}) collective-permute-start(bf16[64,3072]{1,0:T(8,128)(2,1)} %get-tuple-element.76), channel_id=1, source_target_pairs={{0,2},{1,3},{2,0},{3,1},{4,6},{5,7},{6,4},{7,5},{8,10},{9,11},{10,... | collective-permute-start | bytes 1179656 | tf_op jit(solution)/shard_map/ppermute | solution.py:20
  119.4 20.3 %collective-permute-start.33 = (bf16[64,3072]{1,0:T(8,128)(2,1)}, bf16[64,3072]{1,0:T(8,128)(2,1)S(1)}, u32[]{:S(2)}, u32[]{:S(2)}) collective-permute-start(bf16[64,3072]{1,0:T(8,128)(2,1)} %get-tuple-element.77), channel_id=1, source_target_pairs={{0,1},{1,2},{2,3},{3,0},{4,5},{5,6},{6,7},{7,4},{8,9},{9,10},{10,1... | collective-permute-start | bytes 1179656 | tf_op jit(solution)/shard_map/ppermute | solution.py:20
  120.8 23.4 %collective-permute-start.28 = (bf16[64,3072]{1,0:T(8,128)(2,1)}, bf16[64,3072]{1,0:T(8,128)(2,1)S(1)}, u32[]{:S(2)}, u32[]{:S(2)}) collective-permute-start(bf16[64,3072]{1,0:T(8,128)(2,1)} %get-tuple-element.71), channel_id=1, source_target_pairs={{0,24},{8,0},{16,8},{24,16},{32,56},{40,32},{48,40},{56,48},{1,25}... | collective-permute-start | bytes 1179656 | tf_op jit(solution)/shard_map/ppermute | solution.py:20
  123.6 23.1 %collective-permute-start.29 = (bf16[64,3072]{1,0:T(8,128)(2,1)}, bf16[64,3072]{1,0:T(8,128)(2,1)S(1)}, u32[]{:S(2)}, u32[]{:S(2)}) collective-permute-start(bf16[64,3072]{1,0:T(8,128)(2,1)} %get-tuple-element.72), channel_id=1, source_target_pairs={{0,16},{8,24},{16,0},{24,8},{32,48},{40,56},{48,32},{56,40},{1,17}... | collective-permute-start | bytes 1179656 | tf_op jit(solution)/shard_map/ppermute | solution.py:20
  129.5 10.2 %copy-start.10 = (bf16[64,3072]{1,0:T(8,128)(2,1)}, bf16[64,3072]{1,0:T(8,128)(2,1)S(1)}, u32[]{:S(2)}) copy-start(bf16[64,3072]{1,0:T(8,128)(2,1)S(1)} %collective-permute-done.31.refs_1_) | copy-start | bytes 1179652
  129.5 20.2 %collective-permute-start.30 = (bf16[64,3072]{1,0:T(8,128)(2,1)}, bf16[64,3072]{1,0:T(8,128)(2,1)S(1)}, u32[]{:S(2)}, u32[]{:S(2)}) collective-permute-start(bf16[64,3072]{1,0:T(8,128)(2,1)} %get-tuple-element.73), channel_id=1, source_target_pairs={{0,8},{8,16},{16,24},{24,0},{32,40},{40,48},{48,56},{56,32},{1,9},... | collective-permute-start | bytes 1179656 | tf_op jit(solution)/shard_map/ppermute | solution.py:20
  133.0 6.7 %copy-start.11 = (bf16[64,3072]{1,0:T(8,128)(2,1)}, bf16[64,3072]{1,0:T(8,128)(2,1)S(1)}, u32[]{:S(2)}) copy-start(bf16[64,3072]{1,0:T(8,128)(2,1)S(1)} %collective-permute-done.32.refs_2_) | copy-start | bytes 1179652
  133.0 37.0 %collective-permute-start.15 = (bf16[64,3072]{1,0:T(8,128)(2,1)}, bf16[64,3072]{1,0:T(8,128)(2,1)S(1)}, u32[]{:S(2)}, u32[]{:S(2)}) collective-permute-start(bf16[64,3072]{1,0:T(8,128)(2,1)} %get-tuple-element.57), channel_id=1, source_target_pairs={{0,3},{1,0},{2,1},{3,2},{4,7},{5,4},{6,5},{7,6},{8,11},{9,8},{10,9... | collective-permute-start | bytes 1179656 | tf_op jit(solution)/shard_map/ppermute | solution.py:20
  140.5 74.4 %copy-start.18 = (bf16[1,3072,8]{1,2,0:T(8,128)(2,1)S(1)}, bf16[1,3072,8]{1,2,0:T(8,128)(2,1)}, u32[]{:S(2)}) copy-start(bf16[1,3072,8]{1,2,0:T(8,128)(2,1)} %param.10) | copy-start | bytes 147460
  142.7 7.1 %collective-permute-start.34 = (bf16[16,3072]{1,0:T(8,128)(2,1)}, bf16[16,3072]{1,0:T(8,128)(2,1)S(1)}, u32[]{:S(2)}, u32[]{:S(2)}) collective-permute-start(bf16[16,3072]{1,0:T(8,128)(2,1)} %get-tuple-element.78), channel_id=1, source_target_pairs={{0,32},{8,40},{16,48},{24,56},{32,0},{40,8},{48,16},{56,24},{1,33}... | collective-permute-start | bytes 294920 | tf_op jit(solution)/shard_map/ppermute | solution.py:20
  144.2 12.5 %copy-start.4 = (bf16[64,3072]{1,0:T(8,128)(2,1)}, bf16[64,3072]{1,0:T(8,128)(2,1)S(1)}, u32[]{:S(2)}) copy-start(bf16[64,3072]{1,0:T(8,128)(2,1)S(1)} %collective-permute-done.28.refs_1_) | copy-start | bytes 1179652
  144.2 6.1 %collective-permute-start.35 = (bf16[16,3072]{1,0:T(8,128)(2,1)}, bf16[16,3072]{1,0:T(8,128)(2,1)S(1)}, u32[]{:S(2)}, u32[]{:S(2)}) collective-permute-start(bf16[16,3072]{1,0:T(8,128)(2,1)} %get-tuple-element.79), channel_id=1, source_target_pairs={{0,56},{8,32},{16,40},{24,48},{32,24},{40,0},{48,8},{56,16},{1,57}... | collective-permute-start | bytes 294920 | tf_op jit(solution)/shard_map/ppermute | solution.py:20
  146.7 10.0 %copy-start.5 = (bf16[64,3072]{1,0:T(8,128)(2,1)}, bf16[64,3072]{1,0:T(8,128)(2,1)S(1)}, u32[]{:S(2)}) copy-start(bf16[64,3072]{1,0:T(8,128)(2,1)S(1)} %collective-permute-done.29.refs_2_) | copy-start | bytes 1179652
  146.7 7.3 %collective-permute-start.36 = (bf16[16,3072]{1,0:T(8,128)(2,1)}, bf16[16,3072]{1,0:T(8,128)(2,1)S(1)}, u32[]{:S(2)}, u32[]{:S(2)}) collective-permute-start(bf16[16,3072]{1,0:T(8,128)(2,1)} %get-tuple-element.80), channel_id=1, source_target_pairs={{0,48},{8,56},{16,32},{24,40},{32,16},{40,24},{48,0},{56,8},{1,49}... | collective-permute-start | bytes 294920 | tf_op jit(solution)/shard_map/ppermute | solution.py:20
  149.8 6.9 %copy-start.6 = (bf16[64,3072]{1,0:T(8,128)(2,1)}, bf16[64,3072]{1,0:T(8,128)(2,1)S(1)}, u32[]{:S(2)}) copy-start(bf16[64,3072]{1,0:T(8,128)(2,1)S(1)} %collective-permute-done.30.refs_3_) | copy-start | bytes 1179652
  149.8 6.9 %collective-permute-start.37 = (bf16[16,3072]{1,0:T(8,128)(2,1)}, bf16[16,3072]{1,0:T(8,128)(2,1)S(1)}, u32[]{:S(2)}, u32[]{:S(2)}) collective-permute-start(bf16[16,3072]{1,0:T(8,128)(2,1)} %get-tuple-element.81), channel_id=1, source_target_pairs={{0,40},{8,48},{16,56},{24,32},{32,8},{40,16},{48,24},{56,0},{1,41}... | collective-permute-start | bytes 294920 | tf_op jit(solution)/shard_map/ppermute | solution.py:20
  149.8 6.9 %copy-start.19 = (bf16[16,3072]{1,0:T(8,128)(2,1)}, bf16[16,3072]{1,0:T(8,128)(2,1)S(1)}, u32[]{:S(2)}) copy-start(bf16[16,3072]{1,0:T(8,128)(2,1)S(1)} %collective-permute-done.34.refs_4_) | copy-start | bytes 294916
  150.3 6.4 %copy-start.20 = (bf16[16,3072]{1,0:T(8,128)(2,1)}, bf16[16,3072]{1,0:T(8,128)(2,1)S(1)}, u32[]{:S(2)}) copy-start(bf16[16,3072]{1,0:T(8,128)(2,1)S(1)} %collective-permute-done.35.refs_5_) | copy-start | bytes 294916
  160.3 49.5 %all-to-all-start.1 = ((bf16[8,16,3072]{2,1,0:T(8,128)(2,1)}), bf16[8,16,3072]{2,1,0:T(8,128)(2,1)S(1)}, u32[]{:S(2)}, u32[]{:S(2)}) async-start(bf16[8,16,3072]{2,1,0:T(8,128)(2,1)} %bitcast.27), calls=%async_computation.1 | async-start | bytes 1572864 | tf_op jit(solution)/shard_map/all_to_all | solution.py:393
  164.5 22.2 %collective-permute-start.16 = (bf16[64,3072]{1,0:T(8,128)(2,1)S(1)}, bf16[64,3072]{1,0:T(8,128)(2,1)S(1)}, u32[]{:S(2)}, u32[]{:S(2)}) collective-permute-start(bf16[64,3072]{1,0:T(8,128)(2,1)S(1)} %copy-done.31), channel_id=1, source_target_pairs={{0,2},{1,3},{2,0},{3,1},{4,6},{5,7},{6,4},{7,5},{8,10},{9,11},{10,... | collective-permute-start | bytes 1179656 | tf_op jit(solution)/shard_map/ppermute | solution.py:20
  168.0 23.7 %collective-permute-start.17 = (bf16[64,3072]{1,0:T(8,128)(2,1)S(1)}, bf16[64,3072]{1,0:T(8,128)(2,1)S(1)}, u32[]{:S(2)}, u32[]{:S(2)}) collective-permute-start(bf16[64,3072]{1,0:T(8,128)(2,1)S(1)} %copy-done.30), channel_id=1, source_target_pairs={{0,1},{1,2},{2,3},{3,0},{4,5},{5,6},{6,7},{7,4},{8,9},{9,10},{10,1... | collective-permute-start | bytes 1179656 | tf_op jit(solution)/shard_map/ppermute | solution.py:20
  168.6 27.7 %collective-permute-start.12 = (bf16[64,3072]{1,0:T(8,128)(2,1)S(1)}, bf16[64,3072]{1,0:T(8,128)(2,1)S(1)}, u32[]{:S(2)}, u32[]{:S(2)}) collective-permute-start(bf16[64,3072]{1,0:T(8,128)(2,1)S(1)} %copy-done.29), channel_id=1, source_target_pairs={{0,24},{8,0},{16,8},{24,16},{32,56},{40,32},{48,40},{56,48},{1,25}... | collective-permute-start | bytes 1179656 | tf_op jit(solution)/shard_map/ppermute | solution.py:20
  168.7 29.3 %collective-permute-start.13 = (bf16[64,3072]{1,0:T(8,128)(2,1)S(1)}, bf16[64,3072]{1,0:T(8,128)(2,1)S(1)}, u32[]{:S(2)}, u32[]{:S(2)}) collective-permute-start(bf16[64,3072]{1,0:T(8,128)(2,1)S(1)} %copy-done.28), channel_id=1, source_target_pairs={{0,16},{8,24},{16,0},{24,8},{32,48},{40,56},{48,32},{56,40},{1,17}... | collective-permute-start | bytes 1179656 | tf_op jit(solution)/shard_map/ppermute | solution.py:20
  170.0 21.7 %copy-start.9 = (bf16[64,3072]{1,0:T(8,128)(2,1)}, bf16[64,3072]{1,0:T(8,128)(2,1)S(1)}, u32[]{:S(2)}) copy-start(bf16[64,3072]{1,0:T(8,128)(2,1)S(1)} %collective-permute-done.15.refs_1_) | copy-start | bytes 1179652
  170.0 30.1 %collective-permute-start.14 = (bf16[64,3072]{1,0:T(8,128)(2,1)S(1)}, bf16[64,3072]{1,0:T(8,128)(2,1)S(1)}, u32[]{:S(2)}, u32[]{:S(2)}) collective-permute-start(bf16[64,3072]{1,0:T(8,128)(2,1)S(1)} %copy-done.27), channel_id=1, source_target_pairs={{0,8},{8,16},{16,24},{24,0},{32,40},{40,48},{48,56},{56,32},{1,9},... | collective-permute-start | bytes 1179656 | tf_op jit(solution)/shard_map/ppermute | solution.py:20
  194.7 8.4 %collective-permute-start.18 = (bf16[16,3072]{1,0:T(8,128)(2,1)}, bf16[16,3072]{1,0:T(8,128)(2,1)S(1)}, u32[]{:S(2)}, u32[]{:S(2)}) collective-permute-start(bf16[16,3072]{1,0:T(8,128)(2,1)} %get-tuple-element.60), channel_id=1, source_target_pairs={{0,32},{8,40},{16,48},{24,56},{32,0},{40,8},{48,16},{56,24},{1,33}... | collective-permute-start | bytes 294920 | tf_op jit(solution)/shard_map/ppermute | solution.py:20
  195.4 7.7 %collective-permute-start.19 = (bf16[16,3072]{1,0:T(8,128)(2,1)}, bf16[16,3072]{1,0:T(8,128)(2,1)S(1)}, u32[]{:S(2)}, u32[]{:S(2)}) collective-permute-start(bf16[16,3072]{1,0:T(8,128)(2,1)} %get-tuple-element.61), channel_id=1, source_target_pairs={{0,56},{8,32},{16,40},{24,48},{32,24},{40,0},{48,8},{56,16},{1,57}... | collective-permute-start | bytes 294920 | tf_op jit(solution)/shard_map/ppermute | solution.py:20
  196.2 9.0 %copy-start.15 = (bf16[64,3072]{1,0:T(8,128)(2,1)}, bf16[64,3072]{1,0:T(8,128)(2,1)S(1)}, u32[]{:S(2)}) copy-start(bf16[64,3072]{1,0:T(8,128)(2,1)S(1)} %collective-permute-done.12.refs_1_) | copy-start | bytes 1179652
  196.2 8.3 %collective-permute-start.20 = (bf16[16,3072]{1,0:T(8,128)(2,1)}, bf16[16,3072]{1,0:T(8,128)(2,1)S(1)}, u32[]{:S(2)}, u32[]{:S(2)}) collective-permute-start(bf16[16,3072]{1,0:T(8,128)(2,1)} %get-tuple-element.62), channel_id=1, source_target_pairs={{0,48},{8,56},{16,32},{24,40},{32,16},{40,24},{48,0},{56,8},{1,49}... | collective-permute-start | bytes 294920 | tf_op jit(solution)/shard_map/ppermute | solution.py:20
  198.0 7.3 %copy-start.16 = (bf16[64,3072]{1,0:T(8,128)(2,1)}, bf16[64,3072]{1,0:T(8,128)(2,1)S(1)}, u32[]{:S(2)}) copy-start(bf16[64,3072]{1,0:T(8,128)(2,1)S(1)} %collective-permute-done.13.refs_2_) | copy-start | bytes 1179652
  198.0 7.2 %collective-permute-start.21 = (bf16[16,3072]{1,0:T(8,128)(2,1)}, bf16[16,3072]{1,0:T(8,128)(2,1)S(1)}, u32[]{:S(2)}, u32[]{:S(2)}) collective-permute-start(bf16[16,3072]{1,0:T(8,128)(2,1)} %get-tuple-element.63), channel_id=1, source_target_pairs={{0,40},{8,48},{16,56},{24,32},{32,8},{40,16},{48,24},{56,0},{1,41}... | collective-permute-start | bytes 294920 | tf_op jit(solution)/shard_map/ppermute | solution.py:20
  209.8 17.9 %copy-start.1 = (bf16[8,16,3072]{2,1,0:T(8,128)(2,1)}, bf16[8,16,3072]{2,1,0:T(8,128)(2,1)S(1)}, u32[]{:S(2)}) copy-start(bf16[8,16,3072]{2,1,0:T(8,128)(2,1)S(1)} %all-to-all-done.1) | copy-start | bytes 2359300
  209.8 17.9 %all-to-all-start = ((bf16[8,16,3200]{2,1,0:T(8,128)(2,1)}), bf16[8,16,3200]{2,1,0:T(8,128)(2,1)S(1)}, u32[]{:S(2)}, u32[]{:S(2)}) async-start(bf16[8,16,3200]{2,1,0:T(8,128)(2,1)} %bitcast.25), calls=%async_computation | async-start | bytes 1638400 | tf_op jit(solution)/shard_map/all_to_all | solution.py:393
  (20 other events, 32.9 us)

commit v2 on v1

v2 whole, which is shorter than its diff:
```python
import functools

import jax
import jax.numpy as jnp
from jax import lax
from jax.experimental import pallas as pl
from jax.experimental.pallas import tpu as pltpu
from jax.sharding import PartitionSpec as P

F32 = jnp.float32
BF16 = jnp.bfloat16
SIDE = 4
STEPS = (0, 1, SIDE - 1, 2)
FORWARD_TILES = (256, 1024)
BACKWARD_TILES = (512, 512)
AHEAD = 2
VMEM_LIMIT = 56 * 1024 * 1024


def moved(x, axis, by):
    pairs = [(hi * SIDE + lo, hi * SIDE + (lo + by) % SIDE) for hi in range(2) for lo in range(SIDE)]
    return lax.ppermute(x, axis, pairs)


def exchange(x, axis, low=False):
    size = lax.axis_size(axis)
    groups = [list(range(start, start + SIDE)) for start in range(0, size, SIDE)] if low else None
    parts = SIDE if low else size
    blocks = x.reshape(parts, x.shape[0] // parts, x.shape[1])
    return lax.all_to_all(blocks, axis, 0, 0, axis_index_groups=groups).reshape(x.shape)


def column_tile(width):
    return 512 if width % 512 == 0 else width


def slot_targets(pos_ref, row, slots):
    y_lo, x, z = pos_ref[1], pos_ref[2], pos_ref[3]
    quarter = slots // SIDE
    head = 2 * SIDE * quarter
    expert = row // quarter
    first = expert * slots + jnp.where(expert // SIDE == y_lo, 0, z * quarter) + row % quarter
    rest = row - head
    more = slots - quarter
    second = (y_lo * SIDE + (x + rest // more) % SIDE) * slots + quarter + rest % more
    target = jnp.where(row < head, first, second)
    return jnp.where(row < head + SIDE * more, target, -1)


def route_kernel(slots, pos_ref, ids_ref, arrived_ref, router_ref, meta_ref, *refs):
    count, width = arrived_ref.shape
    experts = router_ref.shape[0]
    ids = jnp.concatenate([ids_ref[...].astype(F32), jnp.zeros((count - 2, count), F32)], axis=0).T.astype(jnp.int32)
    first, second = ids[:, 0:1], ids[:, 1:2]
    lane = lax.broadcasted_iota(jnp.int32, (count, count), 1)
    row = lax.broadcasted_iota(jnp.int32, (count, count), 0)
    pick0 = (lane == first).astype(F32)
    pick1 = (lane == second).astype(F32)
    below = (row > lane).astype(F32).astype(BF16)
    before = jnp.dot(below, (pick0 + pick1).astype(BF16), preferred_element_type=F32)
    slot0 = first.astype(F32) * slots + jnp.sum(before * pick0, axis=1, keepdims=True)
    slot1 = second.astype(F32) * slots + jnp.sum(before * pick1, axis=1, keepdims=True)
    scores = transposed_dot(arrived_ref[...], router_ref[...])
    left = jnp.sum(scores * pick0[:, :experts], axis=1, keepdims=True)
    right = jnp.sum(scores * pick1[:, :experts], axis=1, keepdims=True)
    weight0 = 1.0 / (1.0 + jnp.exp(right - left))
    weight1 = 1.0 / (1.0 + jnp.exp(left - right))
    meta = jnp.where(lane == 0, slot0, 0.0)
    meta = jnp.where(lane == 1, slot1, meta)
    meta = jnp.where(lane == 2, weight0, meta)
    meta = jnp.where(lane == 3, weight1, meta)
    meta_ref[...] = meta
    hits, _ = dispatch_hits(slots, pos_ref, meta)
    write_rows(hits, None, arrived_ref, refs)


def dispatch_hits(slots, pos_ref, meta):
    count = meta.shape[0]
    total = 2 * slots + SIDE * (slots - slots // SIDE)
    flat = meta.T
    target = slot_targets(pos_ref, lax.broadcasted_iota(jnp.int32, (total, count), 0), slots).astype(F32)
    hit0 = (target == flat[0:1, :]).astype(F32)
    hit1 = (target == flat[1:2, :]).astype(F32)
    scale = jnp.sum(hit0 * flat[2:3, :] + hit1 * flat[3:4, :], axis=1, keepdims=True)
    return (hit0 + hit1).astype(BF16), scale


def write_rows(hits, scale, source_ref, refs):
    width = source_ref.shape[1]
    tile = column_tile(width)
    for start in range(0, width, tile):
        columns = slice(start, start + tile)
        rows = jnp.dot(hits, source_ref[:, columns], preferred_element_type=F32)
        if scale is not None:
            rows = scale * rows
        write_chunks(rows.astype(BF16), [ref.at[:, columns] for ref in refs])


def cot_kernel(slots, pos_ref, meta_ref, upstream_ref, *refs):
    hits, scale = dispatch_hits(slots, pos_ref, meta_ref[...])
    write_rows(hits, scale, upstream_ref, refs)


def dispatch_shapes(slots, width):
    return [jax.ShapeDtypeStruct((2 * slots, width), BF16)] + [
        jax.ShapeDtypeStruct((slots - slots // SIDE, width), BF16)
    ] * SIDE


def dispatch_rows(position, routes, arrived, router, slots):
    count, width = arrived.shape
    whole = lambda *shape: pl.BlockSpec(shape, lambda i, pos: (0,) * len(shape))
    outs = [jax.ShapeDtypeStruct((count, count), F32)] + dispatch_shapes(slots, width)
    return pl.pallas_call(
        functools.partial(route_kernel, slots),
        out_shape=outs,
        grid_spec=pltpu.PrefetchScalarGridSpec(
            num_scalar_prefetch=1,
            grid=(1,),
            in_specs=[
                pl.BlockSpec((2, count), lambda i, pos: (0, pos[0])),
                whole(count, width),
                whole(*router.shape),
            ],
            out_specs=[whole(*out.shape) for out in outs],
        ),
        compiler_params=pltpu.CompilerParams(vmem_limit_bytes=VMEM_LIMIT),
        cost_estimate=pl.CostEstimate(
            flops=2 * 5 * slots * count * width, bytes_accessed=8 * count * width, transcendentals=0
        ),
        name="dispatch_rows",
    )(position, routes, arrived, router)


def dispatch_cot(position, meta, upstream, slots):
    count, width = upstream.shape
    whole = lambda *shape: pl.BlockSpec(shape, lambda i, pos: (0,) * len(shape))
    outs = dispatch_shapes(slots, width)
    return pl.pallas_call(
        functools.partial(cot_kernel, slots),
        out_shape=outs,
        grid_spec=pltpu.PrefetchScalarGridSpec(
            num_scalar_prefetch=1,
            grid=(1,),
            in_specs=[whole(*meta.shape), whole(count, width)],
            out_specs=[whole(*out.shape) for out in outs],
        ),
        compiler_params=pltpu.CompilerParams(vmem_limit_bytes=VMEM_LIMIT),
        cost_estimate=pl.CostEstimate(
            flops=2 * 5 * slots * count * width, bytes_accessed=8 * count * width, transcendentals=0
        ),
        name="dispatch_cot",
    )(position, meta, upstream)


def chunk_places(pos_ref, slots, apart):
    more = slots - slots // SIDE
    places = [(k * more, more) for k in range(SIDE)] + [(SIDE * more, slots)]
    base = SIDE * more + slots
    if not apart:
        return places + [(base, SIDE * slots)]
    z = pos_ref[3]
    return places + [(pl.multiple_of(base + lax.rem(z + SIDE - by, SIDE) * slots, slots), slots) for by in STEPS]


def chunk_shapes(slots, width, apart):
    sizes = [slots - slots // SIDE] * SIDE + [slots] + ([slots] * SIDE if apart else [SIDE * slots])
    return [jax.ShapeDtypeStruct((size, width), BF16) for size in sizes]


def row_copies(places, refs, rows_v, sems):
    return [
        pltpu.make_async_copy(ref, rows_v.at[pl.ds(start, size)], sems.at[k])
        for k, ((start, size), ref) in enumerate(zip(places, refs))
    ]


def result_copies(places, rows_v, columns, refs, sems):
    return [
        pltpu.make_async_copy(rows_v.at[pl.ds(start, size), columns], ref.at[:, columns], sems.at[k])
        for k, ((start, size), ref) in enumerate(zip(places, refs))
    ]


def tiles(extent, size):
    size = size if extent % size == 0 else extent
    return [pl.ds(start, size) for start in range(0, extent, size)]


def begin(copies):
    for copy in copies:
        copy.start()


def finish_copies(copies):
    for copy in copies:
        copy.wait()


def write_chunks(out, refs):
    start = 0
    for ref in refs:
        size = ref.shape[0]
        ref[...] = out[start : start + size]
        start += size


def forward_kernel(slots, pos_ref, *refs):
    places_in, places_out = chunk_places(pos_ref, slots, True), chunk_places(pos_ref, slots, False)
    chunks, refs = refs[: len(places_in)], refs[len(places_in) :]
    (gate, up, down), refs = refs[:3], refs[3:]
    outs, refs = refs[: len(places_out)], refs[len(places_out) :]
    (swished, slope), refs = refs[:2], refs[2:]
    rows_v, gate_v, up_v, down_v, gate_pre, up_pre, swished_v, slope_v, hidden_v, out_v, *sems = refs
    row_sem, gate_sem, up_sem, down_sem, swished_sem, slope_sem, out_sem = sems
    units, width = down.shape
    unit_tiles, column_tiles = tiles(units, FORWARD_TILES[0]), tiles(width, FORWARD_TILES[1])
    loads = []
    for k, part in enumerate(unit_tiles):
        loads.append(
            [
                pltpu.make_async_copy(gate.at[:, part], gate_v.at[:, part], gate_sem.at[k]),
                pltpu.make_async_copy(up.at[:, part], up_v.at[:, part], up_sem.at[k]),
            ]
        )
    for k, part in enumerate(column_tiles):
        loads.append([pltpu.make_async_copy(down.at[:, part], down_v.at[:, part], down_sem.at[k])])
    saves = []

    def activate(k):
        part = unit_tiles[k]
        gates, ups = gate_pre[k % 2], up_pre[k % 2]
        sigmoid_part = jax.nn.sigmoid(gates)
        swish = gates * sigmoid_part
        swished_v[:, part] = swish
        slope_v[:, part] = ups * (sigmoid_part * (1.0 + gates * (1.0 - sigmoid_part)))
        hidden_v[:, part] = (swish * ups).astype(BF16)

    def save(k):
        part = unit_tiles[k]
        copies = [
            pltpu.make_async_copy(swished_v.at[:, part], swished.at[:, part], swished_sem.at[k]),
            pltpu.make_async_copy(slope_v.at[:, part], slope.at[:, part], slope_sem.at[k]),
        ]
        begin(copies)
        saves.extend(copies)

    rows = row_copies(places_in, chunks, rows_v, row_sem)
    begin(rows)
    for k in range(AHEAD):
        begin(loads[k])
    finish_copies(rows)
    for k, part in enumerate(unit_tiles):
        finish_copies(loads[k])
        if k + AHEAD < len(loads):
            begin(loads[k + AHEAD])
        gate_pre[k % 2] = jnp.dot(rows_v[...], gate_v[:, part], preferred_element_type=F32)
        up_pre[k % 2] = jnp.dot(rows_v[...], up_v[:, part], preferred_element_type=F32)
        if k > 0:
            activate(k - 1)
            save(k - 1)
    activate(len(unit_tiles) - 1)
    save(len(unit_tiles) - 1)
    for k, part in enumerate(column_tiles):
        at = len(unit_tiles) + k
        finish_copies(loads[at])
        if at + AHEAD < len(loads):
            begin(loads[at + AHEAD])
        out_v[:, part] = jnp.dot(hidden_v[...], down_v[:, part], preferred_element_type=F32).astype(BF16)
        copies = result_copies(places_out, out_v, part, outs, out_sem.at[k])
        begin(copies)
        saves.extend(copies)
    finish_copies(saves)


def forward(position, chunks, w_gate, w_up, w_down, slots):
    width, units = w_gate.shape
    outs = chunk_shapes(slots, width, False)
    rows = sum(out.shape[0] for out in outs)
    unit_tiles, column_tiles = tiles(units, FORWARD_TILES[0]), tiles(width, FORWARD_TILES[1])
    unit_tile = unit_tiles[0].size
    anywhere = pl.BlockSpec(memory_space=pl.ANY)
    dma = pltpu.SemaphoreType.DMA
    results = pl.pallas_call(
        functools.partial(forward_kernel, slots),
        out_shape=outs + [jax.ShapeDtypeStruct((rows, units), F32)] * 2,
        in_specs=[pl.BlockSpec(memory_space=pltpu.SMEM)] + [anywhere] * (len(chunks) + 3),
        out_specs=[anywhere] * (len(outs) + 2),
        scratch_shapes=[
            pltpu.VMEM((rows, width), BF16),
            pltpu.VMEM((width, units), BF16),
            pltpu.VMEM((width, units), BF16),
            pltpu.VMEM((units, width), BF16),
            pltpu.VMEM((2, rows, unit_tile), F32),
            pltpu.VMEM((2, rows, unit_tile), F32),
            pltpu.VMEM((rows, units), F32),
            pltpu.VMEM((rows, units), F32),
            pltpu.VMEM((rows, units), BF16),
            pltpu.VMEM((rows, width), BF16),
            dma((len(chunks),)),
            dma((len(unit_tiles),)),
            dma((len(unit_tiles),)),
            dma((len(column_tiles),)),
            dma((len(unit_tiles),)),
            dma((len(unit_tiles),)),
            dma((len(column_tiles), len(outs))),
        ],
        compiler_params=pltpu.CompilerParams(vmem_limit_bytes=VMEM_LIMIT),
        cost_estimate=pl.CostEstimate(
            flops=6 * rows * width * units,
            bytes_accessed=6 * width * units + 4 * rows * width + 8 * rows * units,
            transcendentals=rows * units,
        ),
        name="expert_forward",
    )(position, *chunks, w_gate, w_up, w_down)
    return results


def transposed_dot(a, b):
    return lax.dot_general(a, b, (((1,), (1,)), ((), ())), preferred_element_type=F32)


def backward_kernel(slots, pos_ref, *refs):
    places_in, places_out = chunk_places(pos_ref, slots, False), chunk_places(pos_ref, slots, True)
    chunks, refs = refs[: len(places_in)], refs[len(places_in) :]
    (swished, slope, gate, up, down), refs = refs[:5], refs[5:]
    outs, refs = refs[: len(places_out)], refs[len(places_out) :]
    cot_v, gate_v, up_v, down_v, swished_v, slope_v, d_hidden, d_gate, d_up, out_v, *sems = refs
    row_sem, gate_sem, up_sem, down_sem, swished_sem, slope_sem, out_sem = sems
    units, width = down.shape
    unit_tiles, column_tiles = tiles(units, BACKWARD_TILES[0]), tiles(width, BACKWARD_TILES[1])
    loads = []
    for k, part in enumerate(unit_tiles):
        loads.append(
            [
                pltpu.make_async_copy(down.at[part], down_v.at[part], down_sem.at[k]),
                pltpu.make_async_copy(swished.at[:, part], swished_v.at[:, part], swished_sem.at[k]),
                pltpu.make_async_copy(slope.at[:, part], slope_v.at[:, part], slope_sem.at[k]),
            ]
        )
    for k, part in enumerate(column_tiles):
        loads.append(
            [
                pltpu.make_async_copy(gate.at[part], gate_v.at[part], gate_sem.at[k]),
                pltpu.make_async_copy(up.at[part], up_v.at[part], up_sem.at[k]),
            ]
        )
    saves = []

    def activate(k):
        part = unit_tiles[k]
        d_up[:, part] = (d_hidden[k % 2] * swished_v[:, part]).astype(BF16)
        d_gate[:, part] = (d_hidden[k % 2] * slope_v[:, part]).astype(BF16)

    rows = row_copies(places_in, chunks, cot_v, row_sem)
    begin(rows)
    for k in range(AHEAD):
        begin(loads[k])
    finish_copies(rows)
    for k, part in enumerate(unit_tiles):
        finish_copies(loads[k])
        if k + AHEAD < len(loads):
            begin(loads[k + AHEAD])
        d_hidden[k % 2] = transposed_dot(cot_v[...], down_v[part, :])
        if k > 0:
            activate(k - 1)
    activate(len(unit_tiles) - 1)
    for k, part in enumerate(column_tiles):
        at = len(unit_tiles) + k
        finish_copies(loads[at])
        if at + AHEAD < len(loads):
            begin(loads[at + AHEAD])
        out = transposed_dot(d_gate[...], gate_v[part, :]) + transposed_dot(d_up[...], up_v[part, :])
        out_v[:, part] = out.astype(BF16)
        copies = result_copies(places_out, out_v, part, outs, out_sem.at[k])
        begin(copies)
        saves.extend(copies)
    finish_copies(saves)


def backward(position, chunks, swished, slope, w_gate, w_up, w_down, slots):
    width, units = w_gate.shape
    outs = chunk_shapes(slots, width, True)
    rows = sum(out.shape[0] for out in outs)
    unit_tiles, column_tiles = tiles(units, BACKWARD_TILES[0]), tiles(width, BACKWARD_TILES[1])
    anywhere = pl.BlockSpec(memory_space=pl.ANY)
    dma = pltpu.SemaphoreType.DMA
    return pl.pallas_call(
        functools.partial(backward_kernel, slots),
        out_shape=outs,
        in_specs=[pl.BlockSpec(memory_space=pltpu.SMEM)] + [anywhere] * (len(chunks) + 5),
        out_specs=[anywhere] * len(outs),
        scratch_shapes=[
            pltpu.VMEM((rows, width), BF16),
            pltpu.VMEM((width, units), BF16),
            pltpu.VMEM((width, units), BF16),
            pltpu.VMEM((units, width), BF16),
            pltpu.VMEM((rows, units), F32),
            pltpu.VMEM((rows, units), F32),
            pltpu.VMEM((2, rows, unit_tiles[0].size), F32),
            pltpu.VMEM((rows, units), BF16),
            pltpu.VMEM((rows, units), BF16),
            pltpu.VMEM((rows, width), BF16),
            dma((len(chunks),)),
            dma((len(column_tiles),)),
            dma((len(column_tiles),)),
            dma((len(unit_tiles),)),
            dma((len(unit_tiles),)),
            dma((len(unit_tiles),)),
            dma((len(column_tiles), len(outs))),
        ],
        compiler_params=pltpu.CompilerParams(vmem_limit_bytes=VMEM_LIMIT),
        cost_estimate=pl.CostEstimate(
            flops=6 * rows * width * units,
            bytes_accessed=6 * width * units + 4 * rows * width + 8 * rows * units,
            transcendentals=0,
        ),
        name="expert_backward",
    )(position, *chunks, swished, slope, w_gate, w_up, w_down)


def sum_kernel(pos_ref, own_ref, *refs):
    parts, out_ref = refs[:-1], refs[-1]
    size = own_ref.shape[0]
    total = jnp.zeros(own_ref.shape, F32)
    for part in parts:
        for start in range(0, part.shape[0], size):
            total = total + part[start : start + size, :].astype(F32)
    y_lo = pos_ref[1]
    out_ref[pl.ds(pl.multiple_of(y_lo * size, size), size), :] = own_ref[...]
    out_ref[pl.ds(pl.multiple_of((1 - y_lo) * size, size), size), :] = total.astype(BF16)


def sum_quarters(position, parts, own):
    rows, width = own.shape
    vmem = pl.BlockSpec(memory_space=pltpu.VMEM)
    return pl.pallas_call(
        sum_kernel,
        out_shape=jax.ShapeDtypeStruct((2 * rows, width), BF16),
        in_specs=[pl.BlockSpec(memory_space=pltpu.SMEM)] + [vmem] * (1 + len(parts)),
        out_specs=vmem,
        compiler_params=pltpu.CompilerParams(vmem_limit_bytes=VMEM_LIMIT),
        cost_estimate=pl.CostEstimate(
            flops=4 * rows * width, bytes_accessed=14 * rows * width, transcendentals=0
        ),
        name="sum_quarters",
    )(position, own, *parts)


def combine_kernel(slots, pos_ref, meta_ref, upstream_ref, *refs):
    outputs, grads, out_ref = refs[: 1 + SIDE], refs[1 + SIDE : 2 + 2 * SIDE], refs[-1]
    count, width = upstream_ref.shape
    meta = meta_ref[...]
    padded = 6 * slots
    target = slot_targets(pos_ref, lax.broadcasted_iota(jnp.int32, (count, padded), 1), slots).astype(F32)
    hit0 = (target == meta[:, 0:1]).astype(F32)
    hit1 = (target == meta[:, 1:2]).astype(F32)
    both = (hit0 + hit1).astype(BF16)
    hit0, hit1 = hit0.astype(BF16), hit1.astype(BF16)
    tile = column_tile(width)
    blank = jnp.zeros((slots, tile), BF16)
    dots0 = dots1 = jnp.zeros((count, 1), F32)

    def terms(parts, columns):
        return jnp.concatenate([ref[:, columns] for ref in parts] + [blank], axis=0)

    for start in range(0, width, tile):
        columns = slice(start, start + tile)
        out_terms = terms(outputs, columns)
        rows0 = jnp.dot(hit0, out_terms, preferred_element_type=F32)
        rows1 = jnp.dot(hit1, out_terms, preferred_element_type=F32)
        out_ref[:, columns] = (meta[:, 2:3] * rows0 + meta[:, 3:4] * rows1).astype(BF16)
        upstream = upstream_ref[:, columns].astype(F32)
        dots0 = dots0 + jnp.sum(upstream * rows0, axis=1, keepdims=True)
        dots1 = dots1 + jnp.sum(upstream * rows1, axis=1, keepdims=True)
        summed = jnp.dot(both, terms(grads, columns), preferred_element_type=F32)
        out_ref[:, width + start : width + start + tile] = summed.astype(BF16)
    lane = lax.broadcasted_iota(jnp.int32, (count, 128), 1)
    high0, high1 = dots0.astype(BF16).astype(F32), dots1.astype(BF16).astype(F32)
    extra = jnp.where(lane == 0, high0, 0.0)
    extra = jnp.where(lane == 1, dots0 - high0, extra)
    extra = jnp.where(lane == 2, high1, extra)
    extra = jnp.where(lane == 3, dots1 - high1, extra)
    out_ref[:, 2 * width :] = extra.astype(BF16)


def combine(position, meta, upstream, outputs, grads, slots):
    count, width = upstream.shape
    vmem = pl.BlockSpec(memory_space=pltpu.VMEM)
    return pl.pallas_call(
        functools.partial(combine_kernel, slots),
        out_shape=jax.ShapeDtypeStruct((count, 2 * width + 128), BF16),
        in_specs=[pl.BlockSpec(memory_space=pltpu.SMEM)] + [vmem] * (4 + 2 * SIDE),
        out_specs=vmem,
        compiler_params=pltpu.CompilerParams(vmem_limit_bytes=VMEM_LIMIT),
        cost_estimate=pl.CostEstimate(
            flops=6 * count * 6 * slots * width, bytes_accessed=20 * slots * width + 6 * count * width, transcendentals=0
        ),
        name="combine",
    )(position, meta, upstream, *outputs, *grads)


def finish_kernel(slots, pos_ref, meta_ref, router_ref, parts_ref, layer_ref, rows_ref):
    share = meta_ref.shape[0]
    width = layer_ref.shape[1]
    total = parts_ref[0:share, :].astype(F32)
    for k in range(1, parts_ref.shape[0] // share):
        total = total + parts_ref[k * share : (k + 1) * share, :].astype(F32)
    layer_ref[...] = total[:, :width].astype(BF16)
    grads = total[:, width : 2 * width]
    extra = total[:, 2 * width :]
    d_gap = (extra[:, 0:1] + extra[:, 1:2]) - (extra[:, 2:3] + extra[:, 3:4])
    meta = meta_ref[...]
    d_left = meta[:, 2:3] * meta[:, 3:4] * d_gap
    d_left = d_left.astype(BF16).astype(F32)
    chosen = meta.astype(jnp.int32) // slots
    router = router_ref[...].astype(F32)
    for e in range(router.shape[0]):
        sign = (chosen[:, 0:1] == e).astype(F32) - (chosen[:, 1:2] == e).astype(F32)
        grads = grads + (sign * d_left) * router[e : e + 1, :]
    rows_ref[...] = grads.astype(BF16)


def finish(position, meta, router, parts, share, slots):
    count, width = parts.shape[0], router.shape[1]
    whole = lambda *shape: pl.BlockSpec(shape, lambda i, pos: (0,) * len(shape))
    return pl.pallas_call(
        functools.partial(finish_kernel, slots),
        out_shape=[jax.ShapeDtypeStruct((share, width), BF16)] * 2,
        grid_spec=pltpu.PrefetchScalarGridSpec(
            num_scalar_prefetch=1,
            grid=(1,),
            in_specs=[
                pl.BlockSpec((share, meta.shape[1]), lambda i, pos: (pos[4], 0)),
                whole(*router.shape),
                whole(*parts.shape),
            ],
            out_specs=[whole(share, width)] * 2,
        ),
        compiler_params=pltpu.CompilerParams(vmem_limit_bytes=VMEM_LIMIT),
        cost_estimate=pl.CostEstimate(flops=30 * count * width, bytes_accessed=5 * count * width, transcendentals=0),
        name="finish",
    )(position, meta, router, parts)


def along(axis, sign, chunks):
    return [chunk if by == 0 else moved(chunk, axis, sign * by) for chunk, by in zip(chunks, STEPS)]


def halves(position, head, slots):
    y_lo = position[1]
    return [lax.dynamic_slice_in_dim(head, half * slots, slots, 0) for half in (y_lo, 1 - y_lo)]


def per_device(
    tokens_in, cotangent_in, expert_ids, router_weight, gate_weight, up_weight, down_weight
):
    swap = [(0, 1), (1, 0)]
    arrived = lax.ppermute(tokens_in[0], "pipe", swap)
    upstream = lax.ppermute(cotangent_in[0], "pipe", swap)
    routes = expert_ids[0].T
    router = router_weight[0].T
    w_gate = gate_weight[0, 0]
    w_up = up_weight[0, 0]
    w_down = down_weight[0, 0]
    count = arrived.shape[0]
    n_etp = lax.axis_size("etp")
    slots = 4 * count // lax.axis_size("expert")
    share = count // n_etp
    group = lax.axis_index("expert")
    part = lax.axis_index("etp")
    position = jnp.stack([group, group // SIDE, group % SIDE, part % SIDE, part]).astype(jnp.int32)
    meta, rows_head, *rows = dispatch_rows(position, routes, arrived, router, slots)
    rows_head = exchange(rows_head, "expert")
    *rows, rows_far = [rows[by] for by in STEPS]
    rows = along("expert", 1, rows)
    cot_head, *cot = dispatch_cot(position, meta, upstream, slots)
    rows_head, rows, cot_head = lax.optimization_barrier((rows_head, rows, cot_head))
    own, quarter = halves(position, rows_head, slots)
    quarters = along("etp", 1, [quarter] * SIDE)
    rows_far = moved(rows_far, "expert", STEPS[-1])
    cot_head = exchange(cot_head, "expert")
    rows_far, quarters, cot_head, cot = lax.optimization_barrier((rows_far, quarters, cot_head, cot))
    chunks = (*rows, rows_far, own, *quarters)
    own, quarter = halves(position, cot_head, slots)
    quarters = exchange(jnp.broadcast_to(quarter[None], (SIDE, *quarter.shape)).reshape(SIDE * slots, -1), "etp", low=True)
    cot = along("expert", 1, [cot[by] for by in STEPS])
    *out, own_out, out_quarters, swished, slope = forward(position, chunks, w_gate, w_up, w_down, slots)
    out_quarters = exchange(out_quarters, "etp", low=True)
    out = along("expert", -1, out)
    grad = backward(position, (*cot, own, quarters), swished, slope, w_gate, w_up, w_down, slots)
    out_quarters, out, grad = lax.optimization_barrier((out_quarters, out, grad))
    grad, own_grad, grad_quarters = grad[:SIDE], grad[SIDE], grad[1 + SIDE :]
    grad_quarters = along("etp", -1, grad_quarters)
    *grad, grad_far = grad
    grad = along("expert", -1, grad)
    out_head = exchange(sum_quarters(position, [out_quarters], own_out), "expert")
    grad_quarters, grad, out_head, grad_far = lax.optimization_barrier((grad_quarters, grad, out_head, grad_far))
    grad_head = exchange(sum_quarters(position, grad_quarters, own_grad), "expert")
    grad = [*grad, moved(grad_far, "expert", -STEPS[-1])]
    in_order = lambda head, chunks: [head] + [chunks[STEPS.index(by)] for by in range(SIDE)]
    parts = exchange(combine(position, meta, upstream, in_order(out_head, out), in_order(grad_head, grad), slots), "etp")
    layer_rows, grad_rows = finish(position, meta, router, parts, share, slots)
    return (layer_rows[None], grad_rows[None])


def solution(mesh):
    return jax.shard_map(
        per_device,
        mesh=mesh,
        in_specs=(
            P("pipe", "expert", None),
            P("pipe", "expert", None),
            P("pipe", None, None),
            P("pipe", None, None),
            P("pipe", "expert", None, "etp"),
            P("pipe", "expert", None, "etp"),
            P("pipe", "expert", "etp", None),
        ),
        out_specs=(P("pipe", ("expert", "etp"), None), P("pipe", ("expert", "etp"), None)),
        check_vma=False,
    )
```

time: 233 us -> 199 us (0.85)
  waiting for transfers between devices: 76.7 us -> 45.8 us
  blocking collectives: 0 us -> 23.2 us
  starting transfers between devices: 82.9 us -> 61.7 us
  Pallas kernels: 60.3 us -> 56.8 us
    ppermute x36 -> x18, starting transfers between devices: 73.1 us -> 33.8 us  [moved(): return lax.ppermute(x, axis, pairs)]
    all_to_all x0 -> x1, blocking collectives: none -> 23.2 us  [exchange(): lax.all_to_all(blocks, axis, 0, 0, axis_index_groups=groups)]
    ppermute x36 -> x18, waiting for transfers between devices: 64.4 us -> 44.4 us  [moved(): return lax.ppermute(x, axis, pairs)]
    all_to_all x2 -> x6, starting transfers between devices: 9.14 us -> 27.3 us  [exchange(): lax.all_to_all(blocks, axis, 0, 0, axis_index_groups=groups)]
    all_to_all x2 -> x6, waiting for transfers between devices: 12.2 us -> 0.02 us  [exchange(): lax.all_to_all(blocks, axis, 0, 0, axis_index_groups=groups)]
    pallas_call x8, Pallas kernels: 60.3 us -> 56.8 us  [the longest x1 17.3 us: backward(): pl.pallas_call(functools.partial(backward_kernel, slots), out_shape=outs,...]
    unnamed x89 -> x48, local copies, waits for them, and re-layouts: 7.75 us -> 5.8 us
  transfers between devices with their start and end apart: 40 -> 26, of which waited for: 18 -> 9; matrix products, arithmetic and copies ran while one was open for 2% -> 1% of each run, Pallas kernels for 13% -> 22%
where the time goes in v2:
time: 199 us; the launch traced here: 198 us
  starting transfers between devices  61.7 us (31%)
  Pallas kernels  56.8 us (29%)
  waiting for transfers between devices  45.8 us (23%)
  blocking collectives  23.2 us (12%)
  local copies, waits for them, and re-layouts  9.47 us (5%)
    ppermute x18, waiting for transfers between devices, moved(): return lax.ppermute(x, axis, pairs)  44.4 us
    ppermute x18, starting transfers between devices, moved(): return lax.ppermute(x, axis, pairs)  33.8 us
    all_to_all x6, starting transfers between devices, exchange(): lax.all_to_all(blocks, axis, 0, 0, axis_index_groups=groups)  27.3 us
    all_to_all x1, blocking collectives, exchange(): lax.all_to_all(blocks, axis, 0, 0, axis_index_groups=groups)  23.2 us
    pallas_call x1, Pallas kernels, backward(): pl.pallas_call(functools.partial(backward_kernel, slots), out_shape=outs,...  17.3 us
    pallas_call x1, Pallas kernels, forward(): pl.pallas_call(functools.partial(forward_kernel, slots), out_shape=outs +...  17.1 us
    unnamed x48, local copies, waits for them, and re-layouts  5.8 us
    pallas_call x2, Pallas kernels, sum_quarters(): pl.pallas_call(sum_kernel, out_shape=jax.ShapeDtypeStruct((2 * rows, widt...  5.36 us
  transfers between devices with their start and end apart: 26, of which 9 were waited for; matrix products, arithmetic and copies ran while one was open for 1% of the time, Pallas kernels for 22%

profile of v2, /device:TPU:0, one launch (start us, length us, event | category | flops | bytes accessed | tf_op | source)
XLA Modules:
  0.0 197.8 jit_solution(17857145299386202752)
XLA Ops:
  0.6 0.1 collective-permute-start
  0.7 0.5 collective-permute-start.1
  1.2 0.6 stack.23.pos_ref
  1.9 1.4 collective-permute-done.arrived_ref
  3.2 0.9 copy-done.14
  4.1 4.6 %dispatch_rows.1 = (f32[128,128]{1,0:T(8,128)}, bf16[128,3072]{1,0:T(8,128)(2,1)}, bf16[48,3072]{1,0:T(8,128)(2,1)}, bf16[48,3072]{1,0:T(8,128)(2,1)}, bf16[48,3...) custom-call(s32[5]{0:T(128)} %stack.23.pos_ref, s32[2,1024]{1,0:T(2,128)} %bitcast.56, bf16[128,3072]{1,0:T(8,128)(2,1)} %copy-done.14, ...), custom_call_target="tpu_custom_call" | custom-call | flops 251658240 | bytes 3145728 | tf_op jit(solution)/shard_map/dispatch_rows/pallas_call | solution.py:114
  8.7 5.4 %all-to-all-start = ((bf16[8,16,3072]{2,1,0:T(8,128)(2,1)}), bf16[8,16,3072]{2,1,0:T(8,128)(2,1)S(1)}, u32[]{:S(2)}, u32[]{:S(2)}) async-start(bf16[8,16,3072]{2,1,0:T(8,128)(2,1)} %bitcast.43), calls=%async_computation | async-start | bytes 1572864 | tf_op jit(solution)/shard_map/all_to_all | solution.py:30
  14.1 2.0 %collective-permute-start.2 = (bf16[48,3072]{1,0:T(8,128)(2,1)}, bf16[48,3072]{1,0:T(8,128)(2,1)S(1)}, u32[]{:S(2)}, u32[]{:S(2)}) collective-permute-start(bf16[48,3072]{1,0:T(8,128)(2,1)} %get-tuple-element.73), channel_id=1, source_target_pairs={{0,8},{8,16},{16,24},{24,0},{32,40},{40,48},{48,56},{56,32},{1,9},... | collective-permute-start | bytes 884744 | tf_op jit(solution)/shard_map/ppermute | solution.py:22
  16.1 1.2 collective-permute-start.3
  17.3 0.0 collective-permute-done.1.upstream_ref
  17.4 0.9 copy-done.4
  18.3 3.9 %dispatch_cot.1 = (bf16[128,3072]{1,0:T(8,128)(2,1)}, bf16[48,3072]{1,0:T(8,128)(2,1)}, bf16[48,3072]{1,0:T(8,128)(2,1)}, bf16[48,3072]{1,0:T(8,128)(2,1)}, bf16[48,3072]{1,0:T(8,128)(2,1)}) custom-call(s32[5]{0:T(128)} %stack.23.pos_ref, f32[128,128]{1,0:T(8,128)} %get-tuple-element.70.meta_ref, bf16[128,3072]{1,0:T(8,128)(2,1)} %copy-done.4), custom_call_target="tpu_custom_call" | custom-call | flops 251658240 | bytes 3145728 | tf_op jit(solution)/shard_map/dispatch_cot/pallas_call | solution.py:139
  22.2 10.5 %collective-permute-done.2.refs_1_ = bf16[48,3072]{1,0:T(8,128)(2,1)S(1)} collective-permute-done((bf16[48,3072]{1,0:T(8,128)(2,1)}, bf16[48,3072]{1,0:T(8,128)(2,1)S(1)}, u32[]{:S(2)}, u32[]{:S(2)}) %collective-permute-start.2) | collective-permute-done | bytes 294944 | tf_op jit(solution)/shard_map/ppermute | solution.py:22
  32.7 3.7 %all-to-all-start.1 = ((bf16[8,16,3072]{2,1,0:T(8,128)(2,1)}), bf16[8,16,3072]{2,1,0:T(8,128)(2,1)S(1)}, u32[]{:S(2)}, u32[]{:S(2)}) async-start(bf16[8,16,3072]{2,1,0:T(8,128)(2,1)} %bitcast.42), calls=%async_computation.1 | async-start | bytes 1572864 | tf_op jit(solution)/shard_map/all_to_all | solution.py:30
  36.4 0.8 constant_dynamic-slice_fusion.2
  37.2 3.9 %collective-permute-start.7 = (bf16[64,3072]{1,0:T(8,128)(2,1)S(1)}, bf16[64,3072]{1,0:T(8,128)(2,1)S(1)}, u32[]{:S(2)}, u32[]{:S(2)}) collective-permute-start(bf16[64,3072]{1,0:T(8,128)(2,1)S(1)} %get-tuple-element.87.refs_5_), channel_id=1, source_target_pairs={{0,2},{1,3},{2,0},{3,1},{4,6},{5,7},{6,4},{7,5},{8,10},{9,11},{10,... | collective-permute-start | bytes 1179656 | tf_op jit(solution)/shard_map/ppermute | solution.py:22
  41.1 0.7 collective-permute-start.6
  41.8 1.3 collective-permute-start.5
  43.1 3.5 %collective-permute-start.4 = (bf16[48,3072]{1,0:T(8,128)(2,1)S(1)}, bf16[48,3072]{1,0:T(8,128)(2,1)S(1)}, u32[]{:S(2)}, u32[]{:S(2)}) collective-permute-start(bf16[48,3072]{1,0:T(8,128)(2,1)S(1)} %copy-done.22), channel_id=1, source_target_pairs={{0,16},{8,24},{16,0},{24,8},{32,48},{40,56},{48,32},{56,40},{1,17}... | collective-permute-start | bytes 884744 | tf_op jit(solution)/shard_map/ppermute | solution.py:22
  46.6 8.3 %collective-permute-done.4.refs_3_ = bf16[48,3072]{1,0:T(8,128)(2,1)S(1)} collective-permute-done((bf16[48,3072]{1,0:T(8,128)(2,1)S(1)}, bf16[48,3072]{1,0:T(8,128)(2,1)S(1)}, u32[]{:S(2)}, u32[]{:S(2)}) %collective-permute-start.4) | collective-permute-done | bytes 294944 | tf_op jit(solution)/shard_map/ppermute | solution.py:22
  55.0 4.2 %collective-permute-done.6.refs_7_ = bf16[64,3072]{1,0:T(8,128)(2,1)S(1)} collective-permute-done((bf16[64,3072]{1,0:T(8,128)(2,1)S(1)}, bf16[64,3072]{1,0:T(8,128)(2,1)S(1)}, u32[]{:S(2)}, u32[]{:S(2)}) %collective-permute-start.6) | collective-permute-done | bytes 393248 | tf_op jit(solution)/shard_map/ppermute | solution.py:22
  59.2 0.9 constant_dynamic-slice_fusion
  60.1 1.3 broadcast_in_dim.12
  61.4 3.9 %all-to-all-start.3 = ((bf16[4,64,3072]{2,1,0:T(8,128)(2,1)}), bf16[4,64,3072]{2,1,0:T(8,128)(2,1)S(1)}, u32[]{:S(2)}, u32[]{:S(2)}) async-start(bf16[4,64,3072]{2,1,0:T(8,128)(2,1)} %broadcast_in_dim.12), calls=%async_computation.3 | async-start | bytes 3145728 | tf_op jit(solution)/shard_map/all_to_all | solution.py:30
  65.3 1.6 collective-permute-start.11
  67.0 1.6 collective-permute-start.12
  68.6 1.9 collective-permute-start.13
  70.5 17.1 %expert_forward.1 = (bf16[48,3072]{1,0:T(8,128)(2,1)}, bf16[48,3072]{1,0:T(8,128)(2,1)}, bf16[48,3072]{1,0:T(8,128)(2,1)}, bf16[48,3072]{1,0:T(8,128)(2,1)}, bf1...) custom-call(s32[5]{0:T(128)} %stack.23.pos_ref, ...), custom_call_target="tpu_custom_call" | custom-call | flops 9663676416 | bytes 29360128 | tf_op jit(solution)/shard_map/expert_forward/pallas_call | solution.py:284
  87.6 0.0 all-to-all-done.3
  87.6 4.8 %all-to-all-start.2 = ((bf16[4,64,3072]{2,1,0:T(8,128)(2,1)}), bf16[4,64,3072]{2,1,0:T(8,128)(2,1)S(1)}, u32[]{:S(2)}, u32[]{:S(2)}) async-start(bf16[4,64,3072]{2,1,0:T(8,128)(2,1)} %bitcast.41), calls=%async_computation.2 | async-start | bytes 3145728 | tf_op jit(solution)/shard_map/all_to_all | solution.py:30
  92.4 1.2 collective-permute-start.8
  93.6 0.9 collective-permute-start.9
  94.5 1.6 collective-permute-start.10
  96.1 0.0 collective-permute-done.12.refs_2_
  96.1 0.0 collective-permute-done.13.refs_3_
  96.1 17.3 %expert_backward.1 = (bf16[48,3072]{1,0:T(8,128)(2,1)}, bf16[48,3072]{1,0:T(8,128)(2,1)}, bf16[48,3072]{1,0:T(8,128)(2,1)}, bf16[48,3072]{1,0:T(8,128)(2,1)}, bf...) custom-call(s32[5]{0:T(128)} %stack.23.pos_ref, ...), custom_call_target="tpu_custom_call" | custom-call | flops 9663676416 | bytes 29360128 | tf_op jit(solution)/shard_map/expert_backward/pallas_call | solution.py:388
  113.4 0.7 copy-done.10
  114.2 0.0 collective-permute-done.10.refs_3_
  114.2 0.0 all-to-all-done.2
  114.2 1.2 copy-done
  115.4 2.7 %sum_quarters.2 = bf16[128,3072]{1,0:T(8,128)(2,1)} custom-call(s32[5]{0:T(128)} %stack.23.pos_ref, bf16[64,3072]{1,0:T(8,128)(2,1)} %get-tuple-element.119.own_ref, bf16[256,3072]{1,0:T(8,128)(2,1)} %bitcast.33), custom_call_target="tpu_custom_call" | custom-call | flops 786432 | bytes 2752512 | tf_op jit(solution)/shard_map/sum_quarters/pallas_call | solution.py:437
  118.1 4.1 %all-to-all-start.4 = ((bf16[8,16,3072]{2,1,0:T(8,128)(2,1)}), bf16[8,16,3072]{2,1,0:T(8,128)(2,1)S(1)}, u32[]{:S(2)}, u32[]{:S(2)}) async-start(bf16[8,16,3072]{2,1,0:T(8,128)(2,1)} %bitcast.38), calls=%async_computation.4 | async-start | bytes 1572864 | tf_op jit(solution)/shard_map/all_to_all | solution.py:30
  122.2 3.2 %collective-permute-start.14 = (bf16[64,3072]{1,0:T(8,128)(2,1)}, bf16[64,3072]{1,0:T(8,128)(2,1)S(1)}, u32[]{:S(2)}, u32[]{:S(2)}) collective-permute-start(bf16[64,3072]{1,0:T(8,128)(2,1)} %get-tuple-element.113), channel_id=1, source_target_pairs={{0,3},{1,0},{2,1},{3,2},{4,7},{5,4},{6,5},{7,6},{8,11},{9,8},{10,9... | collective-permute-start | bytes 1179656 | tf_op jit(solution)/shard_map/ppermute | solution.py:22
  125.4 0.0 collective-permute-start.15
  125.4 2.3 %collective-permute-start.16 = (bf16[64,3072]{1,0:T(8,128)(2,1)S(1)}, bf16[64,3072]{1,0:T(8,128)(2,1)S(1)}, u32[]{:S(2)}, u32[]{:S(2)}) collective-permute-start(bf16[64,3072]{1,0:T(8,128)(2,1)S(1)} %copy-done.15), channel_id=1, source_target_pairs={{0,2},{1,3},{2,0},{3,1},{4,6},{5,7},{6,4},{7,5},{8,10},{9,11},{10,... | collective-permute-start | bytes 1179656 | tf_op jit(solution)/shard_map/ppermute | solution.py:22
  127.8 3.2 %collective-permute-start.17 = (bf16[48,3072]{1,0:T(8,128)(2,1)}, bf16[48,3072]{1,0:T(8,128)(2,1)S(1)}, u32[]{:S(2)}, u32[]{:S(2)}) collective-permute-start(bf16[48,3072]{1,0:T(8,128)(2,1)} %get-tuple-element.117), channel_id=1, source_target_pairs={{0,24},{8,0},{16,8},{24,16},{32,56},{40,32},{48,40},{56,48},{1,25}... | collective-permute-start | bytes 884744 | tf_op jit(solution)/shard_map/ppermute | solution.py:22
  131.0 0.0 collective-permute-start.18
  131.0 6.0 %collective-permute-done.17.refs_7_ = bf16[48,3072]{1,0:T(8,128)(2,1)S(1)} collective-permute-done((bf16[48,3072]{1,0:T(8,128)(2,1)}, bf16[48,3072]{1,0:T(8,128)(2,1)S(1)}, u32[]{:S(2)}, u32[]{:S(2)}) %collective-permute-start.17) | collective-permute-done | bytes 294944 | tf_op jit(solution)/shard_map/ppermute | solution.py:22
  137.0 2.2 %collective-permute-done.18.refs_9_ = bf16[48,3072]{1,0:T(8,128)(2,1)S(1)} collective-permute-done((bf16[48,3072]{1,0:T(8,128)(2,1)}, bf16[48,3072]{1,0:T(8,128)(2,1)S(1)}, u32[]{:S(2)}, u32[]{:S(2)}) %collective-permute-start.18) | collective-permute-done | bytes 294944 | tf_op jit(solution)/shard_map/ppermute | solution.py:22
  139.1 0.5 collective-permute-done.14.refs_1_
  139.6 3.3 %collective-permute-done.15.refs_2_ = bf16[64,3072]{1,0:T(8,128)(2,1)S(1)} collective-permute-done((bf16[64,3072]{1,0:T(8,128)(2,1)}, bf16[64,3072]{1,0:T(8,128)(2,1)S(1)}, u32[]{:S(2)}, u32[]{:S(2)}) %collective-permute-start.15) | collective-permute-done | bytes 393248 | tf_op jit(solution)/shard_map/ppermute | solution.py:22
  143.0 0.0 collective-permute-done.16.refs_3_
  143.0 0.0 all-to-all-done.4
  143.0 0.7 copy-done.7
  143.7 0.2 copy-done.8
  143.9 2.7 %sum_quarters.3 = bf16[128,3072]{1,0:T(8,128)(2,1)} custom-call(s32[5]{0:T(128)} %stack.23.pos_ref, bf16[64,3072]{1,0:T(8,128)(2,1)} %get-tuple-element.127.own_ref, bf16[64,3072]{1,0:T(8,128)(2,1)} %get-tuple-element.128.refs_0_, bf16[64,3072]{1,0:T(8,128)(2,1)} %copy-done.6, bf16[64,3072]{1,0:T(8,128)(2,1)} %copy-done.7, bf16[64,3072]{1,0:T(8,128)(2,1)} %copy-done.8), custom_call_target="tpu_custom_call" | custom-call | flops 786432 | bytes 2752512 | tf_op jit(solution)/shard_map/sum_quarters/pallas_call | solution.py:437
  146.6 5.4 %all-to-all-start.5 = ((bf16[8,16,3072]{2,1,0:T(8,128)(2,1)}), bf16[8,16,3072]{2,1,0:T(8,128)(2,1)S(1)}, u32[]{:S(2)}, u32[]{:S(2)}) async-start(bf16[8,16,3072]{2,1,0:T(8,128)(2,1)} %bitcast.39), calls=%async_computation.5 | async-start | bytes 1572864 | tf_op jit(solution)/shard_map/all_to_all | solution.py:30
  152.0 3.5 %collective-permute-start.19 = (bf16[48,3072]{1,0:T(8,128)(2,1)S(1)}, bf16[48,3072]{1,0:T(8,128)(2,1)S(1)}, u32[]{:S(2)}, u32[]{:S(2)}) collective-permute-start(bf16[48,3072]{1,0:T(8,128)(2,1)S(1)} %copy-done.21), channel_id=1, source_target_pairs={{0,16},{8,24},{16,0},{24,8},{32,48},{40,56},{48,32},{56,40},{1,17}... | collective-permute-start | bytes 884744 | tf_op jit(solution)/shard_map/ppermute | solution.py:22
  155.5 9.4 %collective-permute-done.19.refs_8_ = bf16[48,3072]{1,0:T(8,128)(2,1)S(1)} collective-permute-done((bf16[48,3072]{1,0:T(8,128)(2,1)S(1)}, bf16[48,3072]{1,0:T(8,128)(2,1)S(1)}, u32[]{:S(2)}, u32[]{:S(2)}) %collective-permute-start.19) | collective-permute-done | bytes 294944 | tf_op jit(solution)/shard_map/ppermute | solution.py:22
  165.0 0.7 copy-done.13
  165.7 0.3 copy-done.2
  166.0 5.2 %combine.1 = bf16[128,6272]{1,0:T(8,128)(2,1)} custom-call(s32[5]{0:T(128)} %stack.23.pos_ref, f32[128,128]{1,0:T(8,128)} %get-tuple-element.70.meta_ref, bf16[128,3072]{1,0:T(8,128)(2,1)} %copy-done.4, bf16[128,3072]{1,0:T(8,128)(2,1)} %bitcast.34, bf16[48,3072]{1,0:T(8,128)(2,1)} %get-tuple-element.123.refs_1_, bf16[48,3072]{1,0:T(8,128)(2,1)} %copy-done.9, ...), custom_call_target="tpu_custom_call" | custom-call | flops 905969664 | bytes 6291456 | tf_op jit(solution)/shard_map/combine/pallas_call | solution.py:490
  171.2 23.2 %all_to_all.35 = bf16[8,16,6272]{2,1,0:T(8,128)(2,1)} all-to-all(bf16[8,16,6272]{2,1,0:T(8,128)(2,1)} %bitcast.31), channel_id=1, replica_groups=mesh['pipe'=2,'expert'=8,'etp'=8] {'etp'}, dimensions={0} | all-to-all | bytes 3211264 | tf_op jit(solution)/shard_map/all_to_all | solution.py:30
  194.4 3.4 %finish.1 = (bf16[16,3072]{1,0:T(8,128)(2,1)}, bf16[16,3072]{1,0:T(8,128)(2,1)}) custom-call(s32[5]{0:T(128)} %stack.23.pos_ref, f32[128,128]{1,0:T(8,128)} %get-tuple-element.70.meta_ref, bf16[8,3072]{1,0:T(8,128)(2,1)} %bitcast.45, bf16[128,6272]{1,0:T(8,128)(2,1)} %bitcast.32), custom_call_target="tpu_custom_call" | custom-call | flops 11796480 | bytes 1966080 | tf_op jit(solution)/shard_map/finish/pallas_call | solution.py:527
  (49 shorter events, 0.1 us)
Async XLA Ops:
  0.6 2.6 %collective-permute-start = (bf16[128,3072]{1,0:T(8,128)(2,1)}, bf16[128,3072]{1,0:T(8,128)(2,1)S(1)}, u32[]{:S(2)}, u32[]{:S(2)}) collective-permute-start(bf16[128,3072]{1,0:T(8,128)(2,1)} %bitcast.52), channel_id=1, source_target_pairs={{0,64},{64,0},{1,65},{65,1},{2,66},{66,2},{3,67},{67,3},{4,68},{68... | collective-permute-start | bytes 2359304 | tf_op jit(solution)/shard_map/ppermute | solution.py:559
  0.7 16.6 %collective-permute-start.1 = (bf16[128,3072]{1,0:T(8,128)(2,1)}, bf16[128,3072]{1,0:T(8,128)(2,1)S(1)}, u32[]{:S(2)}, u32[]{:S(2)}) collective-permute-start(bf16[128,3072]{1,0:T(8,128)(2,1)} %bitcast.53), channel_id=1, source_target_pairs={{0,64},{64,0},{1,65},{65,1},{2,66},{66,2},{3,67},{67,3},{4,68},{68... | collective-permute-start | bytes 2359304 | tf_op jit(solution)/shard_map/ppermute | solution.py:560
  3.2 0.9 copy-start.14
  8.7 24.0 %all-to-all-start = ((bf16[8,16,3072]{2,1,0:T(8,128)(2,1)}), bf16[8,16,3072]{2,1,0:T(8,128)(2,1)S(1)}, u32[]{:S(2)}, u32[]{:S(2)}) async-start(bf16[8,16,3072]{2,1,0:T(8,128)(2,1)} %bitcast.43), calls=%async_computation | async-start | bytes 1572864 | tf_op jit(solution)/shard_map/all_to_all | solution.py:30
  14.1 18.6 %collective-permute-start.2 = (bf16[48,3072]{1,0:T(8,128)(2,1)}, bf16[48,3072]{1,0:T(8,128)(2,1)S(1)}, u32[]{:S(2)}, u32[]{:S(2)}) collective-permute-start(bf16[48,3072]{1,0:T(8,128)(2,1)} %get-tuple-element.73), channel_id=1, source_target_pairs={{0,8},{8,16},{16,24},{24,0},{32,40},{40,48},{48,56},{56,32},{1,9},... | collective-permute-start | bytes 884744 | tf_op jit(solution)/shard_map/ppermute | solution.py:22
  16.1 16.6 %collective-permute-start.3 = (bf16[48,3072]{1,0:T(8,128)(2,1)}, bf16[48,3072]{1,0:T(8,128)(2,1)S(1)}, u32[]{:S(2)}, u32[]{:S(2)}) collective-permute-start(bf16[48,3072]{1,0:T(8,128)(2,1)} %get-tuple-element.74), channel_id=1, source_target_pairs={{0,24},{8,0},{16,8},{24,16},{32,56},{40,32},{48,40},{56,48},{1,25}... | collective-permute-start | bytes 884744 | tf_op jit(solution)/shard_map/ppermute | solution.py:22
  17.4 0.9 copy-start.4
  22.2 20.9 %copy-start.22 = (bf16[48,3072]{1,0:T(8,128)(2,1)S(1)}, bf16[48,3072]{1,0:T(8,128)(2,1)}, u32[]{:S(2)}) copy-start(bf16[48,3072]{1,0:T(8,128)(2,1)} %get-tuple-element.79) | copy-start | bytes 884740
  32.7 8.4 %copy-start.19 = (bf16[48,3072]{1,0:T(8,128)(2,1)}, bf16[48,3072]{1,0:T(8,128)(2,1)S(1)}, u32[]{:S(2)}) copy-start(bf16[48,3072]{1,0:T(8,128)(2,1)S(1)} %collective-permute-done.2.refs_1_) | copy-start | bytes 884740
  32.7 8.4 %copy-start.20 = (bf16[48,3072]{1,0:T(8,128)(2,1)}, bf16[48,3072]{1,0:T(8,128)(2,1)S(1)}, u32[]{:S(2)}) copy-start(bf16[48,3072]{1,0:T(8,128)(2,1)S(1)} %collective-permute-done.3.refs_2_) | copy-start | bytes 884740
  32.7 26.5 %all-to-all-start.1 = ((bf16[8,16,3072]{2,1,0:T(8,128)(2,1)}), bf16[8,16,3072]{2,1,0:T(8,128)(2,1)S(1)}, u32[]{:S(2)}, u32[]{:S(2)}) async-start(bf16[8,16,3072]{2,1,0:T(8,128)(2,1)} %bitcast.42), calls=%async_computation.1 | async-start | bytes 1572864 | tf_op jit(solution)/shard_map/all_to_all | solution.py:30
  37.2 24.2 %copy-start.5 = (bf16[64,3072]{1,0:T(8,128)(2,1)}, bf16[64,3072]{1,0:T(8,128)(2,1)S(1)}, u32[]{:S(2)}) copy-start(bf16[64,3072]{1,0:T(8,128)(2,1)S(1)} %get-tuple-element.87.refs_5_) | copy-start | bytes 1179652
  37.2 17.8 %collective-permute-start.7 = (bf16[64,3072]{1,0:T(8,128)(2,1)S(1)}, bf16[64,3072]{1,0:T(8,128)(2,1)S(1)}, u32[]{:S(2)}, u32[]{:S(2)}) collective-permute-start(bf16[64,3072]{1,0:T(8,128)(2,1)S(1)} %get-tuple-element.87.refs_5_), channel_id=1, source_target_pairs={{0,2},{1,3},{2,0},{3,1},{4,6},{5,7},{6,4},{7,5},{8,10},{9,11},{10,... | collective-permute-start | bytes 1179656 | tf_op jit(solution)/shard_map/ppermute | solution.py:22
  41.1 18.1 %collective-permute-start.6 = (bf16[64,3072]{1,0:T(8,128)(2,1)S(1)}, bf16[64,3072]{1,0:T(8,128)(2,1)S(1)}, u32[]{:S(2)}, u32[]{:S(2)}) collective-permute-start(bf16[64,3072]{1,0:T(8,128)(2,1)S(1)} %get-tuple-element.87.refs_5_), channel_id=1, source_target_pairs={{0,3},{1,0},{2,1},{3,2},{4,7},{5,4},{6,5},{7,6},{8,11},{9,8},{10,9... | collective-permute-start | bytes 1179656 | tf_op jit(solution)/shard_map/ppermute | solution.py:22
  41.8 17.4 %collective-permute-start.5 = (bf16[64,3072]{1,0:T(8,128)(2,1)S(1)}, bf16[64,3072]{1,0:T(8,128)(2,1)S(1)}, u32[]{:S(2)}, u32[]{:S(2)}) collective-permute-start(bf16[64,3072]{1,0:T(8,128)(2,1)S(1)} %get-tuple-element.87.refs_5_), channel_id=1, source_target_pairs={{0,1},{1,2},{2,3},{3,0},{4,5},{5,6},{6,7},{7,4},{8,9},{9,10},{10,1... | collective-permute-start | bytes 1179656 | tf_op jit(solution)/shard_map/ppermute | solution.py:22
  43.1 11.9 %collective-permute-start.4 = (bf16[48,3072]{1,0:T(8,128)(2,1)S(1)}, bf16[48,3072]{1,0:T(8,128)(2,1)S(1)}, u32[]{:S(2)}, u32[]{:S(2)}) collective-permute-start(bf16[48,3072]{1,0:T(8,128)(2,1)S(1)} %copy-done.22), channel_id=1, source_target_pairs={{0,16},{8,24},{16,0},{24,8},{32,48},{40,56},{48,32},{56,40},{1,17}... | collective-permute-start | bytes 884744 | tf_op jit(solution)/shard_map/ppermute | solution.py:22
  55.0 6.4 %copy-start.23 = (bf16[48,3072]{1,0:T(8,128)(2,1)}, bf16[48,3072]{1,0:T(8,128)(2,1)S(1)}, u32[]{:S(2)}) copy-start(bf16[48,3072]{1,0:T(8,128)(2,1)S(1)} %collective-permute-done.4.refs_3_) | copy-start | bytes 884740
  55.0 6.4 %copy-start.16 = (bf16[64,3072]{1,0:T(8,128)(2,1)}, bf16[64,3072]{1,0:T(8,128)(2,1)S(1)}, u32[]{:S(2)}) copy-start(bf16[64,3072]{1,0:T(8,128)(2,1)S(1)} %collective-permute-done.7.refs_8_) | copy-start | bytes 1179652
  59.2 2.2 %copy-start.17 = (bf16[64,3072]{1,0:T(8,128)(2,1)}, bf16[64,3072]{1,0:T(8,128)(2,1)S(1)}, u32[]{:S(2)}) copy-start(bf16[64,3072]{1,0:T(8,128)(2,1)S(1)} %collective-permute-done.6.refs_7_) | copy-start | bytes 1179652
  59.2 2.2 %copy-start.18 = (bf16[64,3072]{1,0:T(8,128)(2,1)}, bf16[64,3072]{1,0:T(8,128)(2,1)S(1)}, u32[]{:S(2)}) copy-start(bf16[64,3072]{1,0:T(8,128)(2,1)S(1)} %collective-permute-done.5.refs_6_) | copy-start | bytes 1179652
  61.4 26.2 %all-to-all-start.3 = ((bf16[4,64,3072]{2,1,0:T(8,128)(2,1)}), bf16[4,64,3072]{2,1,0:T(8,128)(2,1)S(1)}, u32[]{:S(2)}, u32[]{:S(2)}) async-start(bf16[4,64,3072]{2,1,0:T(8,128)(2,1)} %broadcast_in_dim.12), calls=%async_computation.3 | async-start | bytes 3145728 | tf_op jit(solution)/shard_map/all_to_all | solution.py:30
  65.3 29.1 %collective-permute-start.11 = (bf16[48,3072]{1,0:T(8,128)(2,1)}, bf16[48,3072]{1,0:T(8,128)(2,1)}, u32[]{:S(2)}, u32[]{:S(2)}) collective-permute-start(bf16[48,3072]{1,0:T(8,128)(2,1)} %get-tuple-element.97), channel_id=1, source_target_pairs={{0,8},{8,16},{16,24},{24,0},{32,40},{40,48},{48,56},{56,32},{1,9},... | collective-permute-start | bytes 884744 | tf_op jit(solution)/shard_map/ppermute | solution.py:22
  67.0 29.1 %collective-permute-start.12 = (bf16[48,3072]{1,0:T(8,128)(2,1)}, bf16[48,3072]{1,0:T(8,128)(2,1)}, u32[]{:S(2)}, u32[]{:S(2)}) collective-permute-start(bf16[48,3072]{1,0:T(8,128)(2,1)} %get-tuple-element.98), channel_id=1, source_target_pairs={{0,24},{8,0},{16,8},{24,16},{32,56},{40,32},{48,40},{56,48},{1,25}... | collective-permute-start | bytes 884744 | tf_op jit(solution)/shard_map/ppermute | solution.py:22
  68.6 27.5 %collective-permute-start.13 = (bf16[48,3072]{1,0:T(8,128)(2,1)}, bf16[48,3072]{1,0:T(8,128)(2,1)}, u32[]{:S(2)}, u32[]{:S(2)}) collective-permute-start(bf16[48,3072]{1,0:T(8,128)(2,1)} %get-tuple-element.99), channel_id=1, source_target_pairs={{0,16},{8,24},{16,0},{24,8},{32,48},{40,56},{48,32},{56,40},{1,17}... | collective-permute-start | bytes 884744 | tf_op jit(solution)/shard_map/ppermute | solution.py:22
  87.6 8.5 %copy-start.3 = (bf16[4,64,3072]{2,1,0:T(8,128)(2,1)}, bf16[4,64,3072]{2,1,0:T(8,128)(2,1)S(1)}, u32[]{:S(2)}) copy-start(bf16[4,64,3072]{2,1,0:T(8,128)(2,1)S(1)} %all-to-all-done.3) | copy-start | bytes 4718596
  87.6 26.6 %all-to-all-start.2 = ((bf16[4,64,3072]{2,1,0:T(8,128)(2,1)}), bf16[4,64,3072]{2,1,0:T(8,128)(2,1)S(1)}, u32[]{:S(2)}, u32[]{:S(2)}) async-start(bf16[4,64,3072]{2,1,0:T(8,128)(2,1)} %bitcast.41), calls=%async_computation.2 | async-start | bytes 3145728 | tf_op jit(solution)/shard_map/all_to_all | solution.py:30
  92.4 21.0 %collective-permute-start.8 = (bf16[48,3072]{1,0:T(8,128)(2,1)}, bf16[48,3072]{1,0:T(8,128)(2,1)S(1)}, u32[]{:S(2)}, u32[]{:S(2)}) collective-permute-start(bf16[48,3072]{1,0:T(8,128)(2,1)} %get-tuple-element.93), channel_id=1, source_target_pairs={{0,24},{8,0},{16,8},{24,16},{32,56},{40,32},{48,40},{56,48},{1,25}... | collective-permute-start | bytes 884744 | tf_op jit(solution)/shard_map/ppermute | solution.py:22
  93.6 19.8 %collective-permute-start.9 = (bf16[48,3072]{1,0:T(8,128)(2,1)}, bf16[48,3072]{1,0:T(8,128)(2,1)S(1)}, u32[]{:S(2)}, u32[]{:S(2)}) collective-permute-start(bf16[48,3072]{1,0:T(8,128)(2,1)} %get-tuple-element.94), channel_id=1, source_target_pairs={{0,8},{8,16},{16,24},{24,0},{32,40},{40,48},{48,56},{56,32},{1,9},... | collective-permute-start | bytes 884744 | tf_op jit(solution)/shard_map/ppermute | solution.py:22
  94.5 19.7 %collective-permute-start.10 = (bf16[48,3072]{1,0:T(8,128)(2,1)}, bf16[48,3072]{1,0:T(8,128)(2,1)}, u32[]{:S(2)}, u32[]{:S(2)}) collective-permute-start(bf16[48,3072]{1,0:T(8,128)(2,1)} %get-tuple-element.95), channel_id=1, source_target_pairs={{0,16},{8,24},{16,0},{24,8},{32,48},{40,56},{48,32},{56,40},{1,17}... | collective-permute-start | bytes 884744 | tf_op jit(solution)/shard_map/ppermute | solution.py:22
  113.4 51.5 %copy-start.9 = (bf16[48,3072]{1,0:T(8,128)(2,1)}, bf16[48,3072]{1,0:T(8,128)(2,1)S(1)}, u32[]{:S(2)}) copy-start(bf16[48,3072]{1,0:T(8,128)(2,1)S(1)} %collective-permute-done.8.refs_2_) | copy-start | bytes 884740
  113.4 0.8 copy-start.10
  114.2 1.2 copy-start
  115.4 10.1 %copy-start.15 = (bf16[64,3072]{1,0:T(8,128)(2,1)S(1)}, bf16[64,3072]{1,0:T(8,128)(2,1)}, u32[]{:S(2)}) copy-start(bf16[64,3072]{1,0:T(8,128)(2,1)} %get-tuple-element.115) | copy-start | bytes 1179652
  118.1 24.9 %all-to-all-start.4 = ((bf16[8,16,3072]{2,1,0:T(8,128)(2,1)}), bf16[8,16,3072]{2,1,0:T(8,128)(2,1)S(1)}, u32[]{:S(2)}, u32[]{:S(2)}) async-start(bf16[8,16,3072]{2,1,0:T(8,128)(2,1)} %bitcast.38), calls=%async_computation.4 | async-start | bytes 1572864 | tf_op jit(solution)/shard_map/all_to_all | solution.py:30
  122.2 17.4 %collective-permute-start.14 = (bf16[64,3072]{1,0:T(8,128)(2,1)}, bf16[64,3072]{1,0:T(8,128)(2,1)S(1)}, u32[]{:S(2)}, u32[]{:S(2)}) collective-permute-start(bf16[64,3072]{1,0:T(8,128)(2,1)} %get-tuple-element.113), channel_id=1, source_target_pairs={{0,3},{1,0},{2,1},{3,2},{4,7},{5,4},{6,5},{7,6},{8,11},{9,8},{10,9... | collective-permute-start | bytes 1179656 | tf_op jit(solution)/shard_map/ppermute | solution.py:22
  125.4 17.5 %collective-permute-start.15 = (bf16[64,3072]{1,0:T(8,128)(2,1)}, bf16[64,3072]{1,0:T(8,128)(2,1)S(1)}, u32[]{:S(2)}, u32[]{:S(2)}) collective-permute-start(bf16[64,3072]{1,0:T(8,128)(2,1)} %get-tuple-element.114), channel_id=1, source_target_pairs={{0,1},{1,2},{2,3},{3,0},{4,5},{5,6},{6,7},{7,4},{8,9},{9,10},{10,1... | collective-permute-start | bytes 1179656 | tf_op jit(solution)/shard_map/ppermute | solution.py:22
  125.4 17.5 %collective-permute-start.16 = (bf16[64,3072]{1,0:T(8,128)(2,1)S(1)}, bf16[64,3072]{1,0:T(8,128)(2,1)S(1)}, u32[]{:S(2)}, u32[]{:S(2)}) collective-permute-start(bf16[64,3072]{1,0:T(8,128)(2,1)S(1)} %copy-done.15), channel_id=1, source_target_pairs={{0,2},{1,3},{2,0},{3,1},{4,6},{5,7},{6,4},{7,5},{8,10},{9,11},{10,... | collective-permute-start | bytes 1179656 | tf_op jit(solution)/shard_map/ppermute | solution.py:22
  127.8 9.2 %collective-permute-start.17 = (bf16[48,3072]{1,0:T(8,128)(2,1)}, bf16[48,3072]{1,0:T(8,128)(2,1)S(1)}, u32[]{:S(2)}, u32[]{:S(2)}) collective-permute-start(bf16[48,3072]{1,0:T(8,128)(2,1)} %get-tuple-element.117), channel_id=1, source_target_pairs={{0,24},{8,0},{16,8},{24,16},{32,56},{40,32},{48,40},{56,48},{1,25}... | collective-permute-start | bytes 884744 | tf_op jit(solution)/shard_map/ppermute | solution.py:22
  131.0 8.1 %collective-permute-start.18 = (bf16[48,3072]{1,0:T(8,128)(2,1)}, bf16[48,3072]{1,0:T(8,128)(2,1)S(1)}, u32[]{:S(2)}, u32[]{:S(2)}) collective-permute-start(bf16[48,3072]{1,0:T(8,128)(2,1)} %get-tuple-element.118), channel_id=1, source_target_pairs={{0,8},{8,16},{16,24},{24,0},{32,40},{40,48},{48,56},{56,32},{1,9},... | collective-permute-start | bytes 884744 | tf_op jit(solution)/shard_map/ppermute | solution.py:22
  137.0 28.0 %copy-start.11 = (bf16[48,3072]{1,0:T(8,128)(2,1)}, bf16[48,3072]{1,0:T(8,128)(2,1)S(1)}, u32[]{:S(2)}) copy-start(bf16[48,3072]{1,0:T(8,128)(2,1)S(1)} %collective-permute-done.17.refs_7_) | copy-start | bytes 884740
  139.1 25.8 %copy-start.12 = (bf16[48,3072]{1,0:T(8,128)(2,1)}, bf16[48,3072]{1,0:T(8,128)(2,1)S(1)}, u32[]{:S(2)}) copy-start(bf16[48,3072]{1,0:T(8,128)(2,1)S(1)} %collective-permute-done.18.refs_9_) | copy-start | bytes 884740
  139.6 3.3 %copy-start.6 = (bf16[64,3072]{1,0:T(8,128)(2,1)}, bf16[64,3072]{1,0:T(8,128)(2,1)S(1)}, u32[]{:S(2)}) copy-start(bf16[64,3072]{1,0:T(8,128)(2,1)S(1)} %collective-permute-done.14.refs_1_) | copy-start | bytes 1179652
  143.0 0.8 copy-start.7
  143.0 0.9 copy-start.8
  143.0 3.6 %copy-start.1 = (bf16[8,16,3072]{2,1,0:T(8,128)(2,1)}, bf16[8,16,3072]{2,1,0:T(8,128)(2,1)S(1)}, u32[]{:S(2)}) copy-start(bf16[8,16,3072]{2,1,0:T(8,128)(2,1)S(1)} %all-to-all-done.4) | copy-start | bytes 2359300
  143.9 8.1 %copy-start.21 = (bf16[48,3072]{1,0:T(8,128)(2,1)S(1)}, bf16[48,3072]{1,0:T(8,128)(2,1)}, u32[]{:S(2)}) copy-start(bf16[48,3072]{1,0:T(8,128)(2,1)} %get-tuple-element.134) | copy-start | bytes 884740
  146.6 18.4 %all-to-all-start.5 = ((bf16[8,16,3072]{2,1,0:T(8,128)(2,1)}), bf16[8,16,3072]{2,1,0:T(8,128)(2,1)S(1)}, u32[]{:S(2)}, u32[]{:S(2)}) async-start(bf16[8,16,3072]{2,1,0:T(8,128)(2,1)} %bitcast.39), calls=%async_computation.5 | async-start | bytes 1572864 | tf_op jit(solution)/shard_map/all_to_all | solution.py:30
  152.0 12.9 %collective-permute-start.19 = (bf16[48,3072]{1,0:T(8,128)(2,1)S(1)}, bf16[48,3072]{1,0:T(8,128)(2,1)S(1)}, u32[]{:S(2)}, u32[]{:S(2)}) collective-permute-start(bf16[48,3072]{1,0:T(8,128)(2,1)S(1)} %copy-done.21), channel_id=1, source_target_pairs={{0,16},{8,24},{16,0},{24,8},{32,48},{40,56},{48,32},{56,40},{1,17}... | collective-permute-start | bytes 884744 | tf_op jit(solution)/shard_map/ppermute | solution.py:22
  164.9 0.7 copy-start.13
  164.9 1.1 copy-start.2

commit v3 on v2

--- a/solution.py
+++ b/solution.py
@@ -47,10 +47,18 @@
     return jnp.where(row < head + SIDE * more, target, -1)
 
 
-def route_kernel(slots, pos_ref, ids_ref, arrived_ref, router_ref, meta_ref, *refs):
-    count, width = arrived_ref.shape
-    experts = router_ref.shape[0]
-    ids = jnp.concatenate([ids_ref[...].astype(F32), jnp.zeros((count - 2, count), F32)], axis=0).T.astype(jnp.int32)
+def slot_hits(slots, pos_ref, plan):
+    count = plan.shape[0]
+    total = 2 * slots + SIDE * (slots - slots // SIDE)
+    flat = plan.T
+    target = slot_targets(pos_ref, lax.broadcasted_iota(jnp.int32, (total, count), 0), slots).astype(F32)
+    return (target == flat[0:1, :]).astype(F32), (target == flat[1:2, :]).astype(F32)
+
+
+def plan_kernel(slots, pos_ref, ids_ref, plan_ref, hits_ref):
+    count = plan_ref.shape[0]
+    ids = ids_ref[:, pl.ds(pl.multiple_of(pos_ref[0] * count, count), count)].astype(F32)
+    ids = jnp.concatenate([ids, jnp.zeros((count - 2, count), F32)], axis=0).T.astype(jnp.int32)
     first, second = ids[:, 0:1], ids[:, 1:2]
     lane = lax.broadcasted_iota(jnp.int32, (count, count), 1)
     row = lax.broadcasted_iota(jnp.int32, (count, count), 0)
@@ -60,29 +68,24 @@
     before = jnp.dot(below, (pick0 + pick1).astype(BF16), preferred_element_type=F32)
     slot0 = first.astype(F32) * slots + jnp.sum(before * pick0, axis=1, keepdims=True)
     slot1 = second.astype(F32) * slots + jnp.sum(before * pick1, axis=1, keepdims=True)
-    scores = transposed_dot(arrived_ref[...], router_ref[...])
-    left = jnp.sum(scores * pick0[:, :experts], axis=1, keepdims=True)
-    right = jnp.sum(scores * pick1[:, :experts], axis=1, keepdims=True)
-    weight0 = 1.0 / (1.0 + jnp.exp(right - left))
-    weight1 = 1.0 / (1.0 + jnp.exp(left - right))
-    meta = jnp.where(lane == 0, slot0, 0.0)
-    meta = jnp.where(lane == 1, slot1, meta)
-    meta = jnp.where(lane == 2, weight0, meta)
-    meta = jnp.where(lane == 3, weight1, meta)
-    meta_ref[...] = meta
-    hits, _ = dispatch_hits(slots, pos_ref, meta)
-    write_rows(hits, None, arrived_ref, refs)
-
-
-def dispatch_hits(slots, pos_ref, meta):
-    count = meta.shape[0]
+    plan = jnp.where(lane == 0, slot0, jnp.where(lane == 1, slot1, 0.0))
+    plan_ref[...] = plan
+    hit0, hit1 = slot_hits(slots, pos_ref, plan)
+    hits_ref[...] = (hit0 + hit1).astype(BF16)
+
+
+def plan_slots(position, routes, count, slots):
+    vmem = pl.BlockSpec(memory_space=pltpu.VMEM)
     total = 2 * slots + SIDE * (slots - slots // SIDE)
-    flat = meta.T
-    target = slot_targets(pos_ref, lax.broadcasted_iota(jnp.int32, (total, count), 0), slots).astype(F32)
-    hit0 = (target == flat[0:1, :]).astype(F32)
-    hit1 = (target == flat[1:2, :]).astype(F32)
-    scale = jnp.sum(hit0 * flat[2:3, :] + hit1 * flat[3:4, :], axis=1, keepdims=True)
-    return (hit0 + hit1).astype(BF16), scale
+    return pl.pallas_call(
+        functools.partial(plan_kernel, slots),
+        out_shape=[jax.ShapeDtypeStruct((count, count), F32), jax.ShapeDtypeStruct((total, count), BF16)],
+        in_specs=[pl.BlockSpec(memory_space=pltpu.SMEM), vmem],
+        out_specs=[vmem] * 2,
+        compiler_params=pltpu.CompilerParams(vmem_limit_bytes=VMEM_LIMIT),
+        cost_estimate=pl.CostEstimate(flops=2 * count**3, bytes_accessed=8 * total * count, transcendentals=0),
+        name="plan_slots",
+    )(position, routes)
 
 
 def write_rows(hits, scale, source_ref, refs):
@@ -96,9 +99,26 @@
         write_chunks(rows.astype(BF16), [ref.at[:, columns] for ref in refs])
 
 
-def cot_kernel(slots, pos_ref, meta_ref, upstream_ref, *refs):
-    hits, scale = dispatch_hits(slots, pos_ref, meta_ref[...])
-    write_rows(hits, scale, upstream_ref, refs)
+def rows_kernel(hits_ref, arrived_ref, *refs):
+    write_rows(hits_ref[...], None, arrived_ref, refs)
+
+
+def cot_kernel(slots, pos_ref, plan_ref, arrived_ref, upstream_ref, router_ref, meta_ref, *refs):
+    plan = plan_ref[...]
+    scores = transposed_dot(arrived_ref[...], router_ref[...])
+    expert = lax.broadcasted_iota(jnp.int32, scores.shape, 1)
+    chosen = plan.astype(jnp.int32) // slots
+    left = jnp.sum(jnp.where(expert == chosen[:, 0:1], scores, 0.0), axis=1, keepdims=True)
+    right = jnp.sum(jnp.where(expert == chosen[:, 1:2], scores, 0.0), axis=1, keepdims=True)
+    weight0 = 1.0 / (1.0 + jnp.exp(right - left))
+    weight1 = 1.0 / (1.0 + jnp.exp(left - right))
+    lane = lax.broadcasted_iota(jnp.int32, plan.shape, 1)
+    meta = jnp.where(lane == 2, weight0, jnp.where(lane == 3, weight1, plan))
+    meta_ref[...] = meta
+    hit0, hit1 = slot_hits(slots, pos_ref, plan)
+    flat = meta.T
+    scale = jnp.sum(hit0 * flat[2:3, :] + hit1 * flat[3:4, :], axis=1, keepdims=True)
+    write_rows((hit0 + hit1).astype(BF16), scale, upstream_ref, refs)
 
 
 def dispatch_shapes(slots, width):
@@ -107,50 +127,38 @@
     ] * SIDE
 
 
-def dispatch_rows(position, routes, arrived, router, slots):
+def dispatch_rows(hits, arrived, slots):
     count, width = arrived.shape
-    whole = lambda *shape: pl.BlockSpec(shape, lambda i, pos: (0,) * len(shape))
-    outs = [jax.ShapeDtypeStruct((count, count), F32)] + dispatch_shapes(slots, width)
-    return pl.pallas_call(
-        functools.partial(route_kernel, slots),
+    vmem = pl.BlockSpec(memory_space=pltpu.VMEM)
+    outs = dispatch_shapes(slots, width)
+    return pl.pallas_call(
+        rows_kernel,
         out_shape=outs,
-        grid_spec=pltpu.PrefetchScalarGridSpec(
-            num_scalar_prefetch=1,
-            grid=(1,),
-            in_specs=[
-                pl.BlockSpec((2, count), lambda i, pos: (0, pos[0])),
-                whole(count, width),
-                whole(*router.shape),
-            ],
-            out_specs=[whole(*out.shape) for out in outs],
-        ),
+        in_specs=[vmem] * 2,
+        out_specs=[vmem] * len(outs),
         compiler_params=pltpu.CompilerParams(vmem_limit_bytes=VMEM_LIMIT),
         cost_estimate=pl.CostEstimate(
             flops=2 * 5 * slots * count * width, bytes_accessed=8 * count * width, transcendentals=0
         ),
         name="dispatch_rows",
-    )(position, routes, arrived, router)
-
-
-def dispatch_cot(position, meta, upstream, slots):
+    )(hits, arrived)
+
+
+def dispatch_cot(position, plan, arrived, upstream, router, slots):
     count, width = upstream.shape
-    whole = lambda *shape: pl.BlockSpec(shape, lambda i, pos: (0,) * len(shape))
-    outs = dispatch_shapes(slots, width)
+    vmem = pl.BlockSpec(memory_space=pltpu.VMEM)
+    outs = [jax.ShapeDtypeStruct(plan.shape, F32)] + dispatch_shapes(slots, width)
     return pl.pallas_call(
         functools.partial(cot_kernel, slots),
         out_shape=outs,
-        grid_spec=pltpu.PrefetchScalarGridSpec(
-            num_scalar_prefetch=1,
-            grid=(1,),
-            in_specs=[whole(*meta.shape), whole(count, width)],
-            out_specs=[whole(*out.shape) for out in outs],
-        ),
-        compiler_params=pltpu.CompilerParams(vmem_limit_bytes=VMEM_LIMIT),
-        cost_estimate=pl.CostEstimate(
-            flops=2 * 5 * slots * count * width, bytes_accessed=8 * count * width, transcendentals=0
+        in_specs=[pl.BlockSpec(memory_space=pltpu.SMEM)] + [vmem] * 4,
+        out_specs=[vmem] * len(outs),
+        compiler_params=pltpu.CompilerParams(vmem_limit_bytes=VMEM_LIMIT),
+        cost_estimate=pl.CostEstimate(
+            flops=2 * 5 * slots * count * width, bytes_accessed=10 * count * width, transcendentals=0
         ),
         name="dispatch_cot",
-    )(position, meta, upstream)
+    )(position, plan, arrived, upstream, router)
 
 
 def chunk_places(pos_ref, slots, apart):
@@ -447,70 +455,97 @@
     )(position, own, *parts)
 
 
-def combine_kernel(slots, pos_ref, meta_ref, upstream_ref, *refs):
-    outputs, grads, out_ref = refs[: 1 + SIDE], refs[1 + SIDE : 2 + 2 * SIDE], refs[-1]
+def combine_hits(slots, pos_ref, meta):
+    count = meta.shape[0]
+    target = slot_targets(pos_ref, lax.broadcasted_iota(jnp.int32, (count, 6 * slots), 1), slots).astype(F32)
+    return (target == meta[:, 0:1]).astype(F32), (target == meta[:, 1:2]).astype(F32)
+
+
+def returned_rows(refs, columns, blank):
+    return jnp.concatenate([ref[:, columns] for ref in refs] + [jnp.zeros(blank, BF16)], axis=0)
+
+
+def combine_out_kernel(slots, pos_ref, meta_ref, upstream_ref, *refs):
+    returned, (out_ref, dots_ref) = refs[:-2], refs[-2:]
     count, width = upstream_ref.shape
     meta = meta_ref[...]
-    padded = 6 * slots
-    target = slot_targets(pos_ref, lax.broadcasted_iota(jnp.int32, (count, padded), 1), slots).astype(F32)
-    hit0 = (target == meta[:, 0:1]).astype(F32)
-    hit1 = (target == meta[:, 1:2]).astype(F32)
-    both = (hit0 + hit1).astype(BF16)
-    hit0, hit1 = hit0.astype(BF16), hit1.astype(BF16)
+    hit0, hit1 = [hit.astype(BF16) for hit in combine_hits(slots, pos_ref, meta)]
     tile = column_tile(width)
-    blank = jnp.zeros((slots, tile), BF16)
     dots0 = dots1 = jnp.zeros((count, 1), F32)
-
-    def terms(parts, columns):
-        return jnp.concatenate([ref[:, columns] for ref in parts] + [blank], axis=0)
-
     for start in range(0, width, tile):
         columns = slice(start, start + tile)
-        out_terms = terms(outputs, columns)
-        rows0 = jnp.dot(hit0, out_terms, preferred_element_type=F32)
-        rows1 = jnp.dot(hit1, out_terms, preferred_element_type=F32)
+        terms = returned_rows(returned, columns, (slots, tile))
+        rows0 = jnp.dot(hit0, terms, preferred_element_type=F32)
+        rows1 = jnp.dot(hit1, terms, preferred_element_type=F32)
         out_ref[:, columns] = (meta[:, 2:3] * rows0 + meta[:, 3:4] * rows1).astype(BF16)
         upstream = upstream_ref[:, columns].astype(F32)
         dots0 = dots0 + jnp.sum(upstream * rows0, axis=1, keepdims=True)
         dots1 = dots1 + jnp.sum(upstream * rows1, axis=1, keepdims=True)
-        summed = jnp.dot(both, terms(grads, columns), preferred_element_type=F32)
-        out_ref[:, width + start : width + start + tile] = summed.astype(BF16)
-    lane = lax.broadcasted_iota(jnp.int32, (count, 128), 1)
+    lane = lax.broadcasted_iota(jnp.int32, dots_ref.shape, 1)
     high0, high1 = dots0.astype(BF16).astype(F32), dots1.astype(BF16).astype(F32)
     extra = jnp.where(lane == 0, high0, 0.0)
     extra = jnp.where(lane == 1, dots0 - high0, extra)
     extra = jnp.where(lane == 2, high1, extra)
     extra = jnp.where(lane == 3, dots1 - high1, extra)
-    out_ref[:, 2 * width :] = extra.astype(BF16)
-
-
-def combine(position, meta, upstream, outputs, grads, slots):
+    dots_ref[...] = extra.astype(BF16)
+
+
+def combine_out(position, meta, upstream, returned, slots):
     count, width = upstream.shape
     vmem = pl.BlockSpec(memory_space=pltpu.VMEM)
     return pl.pallas_call(
-        functools.partial(combine_kernel, slots),
-        out_shape=jax.ShapeDtypeStruct((count, 2 * width + 128), BF16),
-        in_specs=[pl.BlockSpec(memory_space=pltpu.SMEM)] + [vmem] * (4 + 2 * SIDE),
+        functools.partial(combine_out_kernel, slots),
+        out_shape=[jax.ShapeDtypeStruct((count, size), BF16) for size in (width, 128)],
+        in_specs=[pl.BlockSpec(memory_space=pltpu.SMEM)] + [vmem] * (3 + SIDE),
+        out_specs=[vmem] * 2,
+        compiler_params=pltpu.CompilerParams(vmem_limit_bytes=VMEM_LIMIT),
+        cost_estimate=pl.CostEstimate(
+            flops=4 * count * 6 * slots * width, bytes_accessed=10 * slots * width + 4 * count * width, transcendentals=0
+        ),
+        name="combine_out",
+    )(position, meta, upstream, *returned)
+
+
+def combine_grad_kernel(slots, pos_ref, meta_ref, out_terms_ref, dots_ref, *refs):
+    returned, out_ref = refs[:-1], refs[-1]
+    width = returned[0].shape[1]
+    hit0, hit1 = combine_hits(slots, pos_ref, meta_ref[...])
+    both = (hit0 + hit1).astype(BF16)
+    tile = column_tile(width)
+    for start in range(0, width, tile):
+        columns = slice(start, start + tile)
+        terms = returned_rows(returned, columns, (slots, tile))
+        out_ref[:, columns] = out_terms_ref[:, columns]
+        grads = jnp.dot(both, terms, preferred_element_type=F32)
+        out_ref[:, width + start : width + start + tile] = grads.astype(BF16)
+    out_ref[:, 2 * width :] = dots_ref[...]
+
+
+def combine_grad(position, meta, out_terms, dots, returned, slots):
+    count, width = out_terms.shape
+    vmem = pl.BlockSpec(memory_space=pltpu.VMEM)
+    return pl.pallas_call(
+        functools.partial(combine_grad_kernel, slots),
+        out_shape=jax.ShapeDtypeStruct((count, 2 * width + dots.shape[1]), BF16),
+        in_specs=[pl.BlockSpec(memory_space=pltpu.SMEM)] + [vmem] * (4 + SIDE),
         out_specs=vmem,
         compiler_params=pltpu.CompilerParams(vmem_limit_bytes=VMEM_LIMIT),
         cost_estimate=pl.CostEstimate(
-            flops=6 * count * 6 * slots * width, bytes_accessed=20 * slots * width + 6 * count * width, transcendentals=0
-        ),
-        name="combine",
-    )(position, meta, upstream, *outputs, *grads)
+            flops=2 * count * 6 * slots * width, bytes_accessed=10 * slots * width + 6 * count * width, transcendentals=0
+        ),
+        name="combine_grad",
+    )(position, meta, out_terms, dots, *returned)
 
 
 def finish_kernel(slots, pos_ref, meta_ref, router_ref, parts_ref, layer_ref, rows_ref):
-    share = meta_ref.shape[0]
-    width = layer_ref.shape[1]
-    total = parts_ref[0:share, :].astype(F32)
+    share, width = layer_ref.shape
+    sums = parts_ref[0:share, :].astype(F32)
     for k in range(1, parts_ref.shape[0] // share):
-        total = total + parts_ref[k * share : (k + 1) * share, :].astype(F32)
-    layer_ref[...] = total[:, :width].astype(BF16)
-    grads = total[:, width : 2 * width]
-    extra = total[:, 2 * width :]
+        sums = sums + parts_ref[k * share : (k + 1) * share, :].astype(F32)
+    layer_ref[...] = sums[:, :width].astype(BF16)
+    grads, extra = sums[:, width : 2 * width], sums[:, 2 * width :]
     d_gap = (extra[:, 0:1] + extra[:, 1:2]) - (extra[:, 2:3] + extra[:, 3:4])
-    meta = meta_ref[...]
+    meta = meta_ref[pl.ds(pl.multiple_of(pos_ref[4] * share, share), share), :]
     d_left = meta[:, 2:3] * meta[:, 3:4] * d_gap
     d_left = d_left.astype(BF16).astype(F32)
     chosen = meta.astype(jnp.int32) // slots
@@ -522,23 +557,17 @@
 
 
 def finish(position, meta, router, parts, share, slots):
-    count, width = parts.shape[0], router.shape[1]
-    whole = lambda *shape: pl.BlockSpec(shape, lambda i, pos: (0,) * len(shape))
+    width = router.shape[1]
+    vmem = pl.BlockSpec(memory_space=pltpu.VMEM)
     return pl.pallas_call(
         functools.partial(finish_kernel, slots),
         out_shape=[jax.ShapeDtypeStruct((share, width), BF16)] * 2,
-        grid_spec=pltpu.PrefetchScalarGridSpec(
-            num_scalar_prefetch=1,
-            grid=(1,),
-            in_specs=[
-                pl.BlockSpec((share, meta.shape[1]), lambda i, pos: (pos[4], 0)),
-                whole(*router.shape),
-                whole(*parts.shape),
-            ],
-            out_specs=[whole(share, width)] * 2,
-        ),
-        compiler_params=pltpu.CompilerParams(vmem_limit_bytes=VMEM_LIMIT),
-        cost_estimate=pl.CostEstimate(flops=30 * count * width, bytes_accessed=5 * count * width, transcendentals=0),
+        in_specs=[pl.BlockSpec(memory_space=pltpu.SMEM)] + [vmem] * 3,
+        out_specs=[vmem] * 2,
+        compiler_params=pltpu.CompilerParams(vmem_limit_bytes=VMEM_LIMIT),
+        cost_estimate=pl.CostEstimate(
+            flops=30 * parts.shape[0] * width, bytes_accessed=5 * parts.shape[0] * width, transcendentals=0
+        ),
         name="finish",
     )(position, meta, router, parts)
 
@@ -564,18 +593,17 @@
     w_up = up_weight[0, 0]
     w_down = down_weight[0, 0]
     count = arrived.shape[0]
-    n_etp = lax.axis_size("etp")
     slots = 4 * count // lax.axis_size("expert")
-    share = count // n_etp
     group = lax.axis_index("expert")
     part = lax.axis_index("etp")
     position = jnp.stack([group, group // SIDE, group % SIDE, part % SIDE, part]).astype(jnp.int32)
-    meta, rows_head, *rows = dispatch_rows(position, routes, arrived, router, slots)
+    plan, hits = plan_slots(position, routes, count, slots)
+    rows_head, *rows = dispatch_rows(hits, arrived, slots)
     rows_head = exchange(rows_head, "expert")
     *rows, rows_far = [rows[by] for by in STEPS]
     rows = along("expert", 1, rows)
-    cot_head, *cot = dispatch_cot(position, meta, upstream, slots)
-    rows_head, rows, cot_head = lax.optimization_barrier((rows_head, rows, cot_head))
+    meta, cot_head, *cot = dispatch_cot(position, plan, arrived, upstream, router, slots)
+    rows_head, rows = lax.optimization_barrier((rows_head, rows))
     own, quarter = halves(position, rows_head, slots)
     quarters = along("etp", 1, [quarter] * SIDE)
     rows_far = moved(rows_far, "expert", STEPS[-1])
@@ -592,15 +620,15 @@
     out_quarters, out, grad = lax.optimization_barrier((out_quarters, out, grad))
     grad, own_grad, grad_quarters = grad[:SIDE], grad[SIDE], grad[1 + SIDE :]
     grad_quarters = along("etp", -1, grad_quarters)
-    *grad, grad_far = grad
     grad = along("expert", -1, grad)
+    in_order = lambda head, chunks: [head] + [chunks[STEPS.index(by)] for by in range(SIDE)]
     out_head = exchange(sum_quarters(position, [out_quarters], own_out), "expert")
-    grad_quarters, grad, out_head, grad_far = lax.optimization_barrier((grad_quarters, grad, out_head, grad_far))
+    grad_quarters, grad, out_head = lax.optimization_barrier((grad_quarters, grad, out_head))
+    out_terms, dots = combine_out(position, meta, upstream, in_order(out_head, out), slots)
     grad_head = exchange(sum_quarters(position, grad_quarters, own_grad), "expert")
-    grad = [*grad, moved(grad_far, "expert", -STEPS[-1])]
-    in_order = lambda head, chunks: [head] + [chunks[STEPS.index(by)] for by in range(SIDE)]
-    parts = exchange(combine(position, meta, upstream, in_order(out_head, out), in_order(grad_head, grad), slots), "etp")
-    layer_rows, grad_rows = finish(position, meta, router, parts, share, slots)
+    terms = combine_grad(position, meta, out_terms, dots, in_order(grad_head, grad), slots)
+    share = count // lax.axis_size("etp")
+    layer_rows, grad_rows = finish(position, meta, router, exchange(terms, "etp"), share, slots)
     return (layer_rows[None], grad_rows[None])
 
 

time: 199 us -> 192 us (0.965)
  waiting for transfers between devices: 45.8 us -> 40.3 us
  starting transfers between devices: 61.7 us -> 57.1 us
    ppermute x18, waiting for transfers between devices: 44.4 us -> 28 us  [moved(): return lax.ppermute(x, axis, pairs)]
    all_to_all x6, waiting for transfers between devices: 0.02 us -> 12.3 us  [exchange(): lax.all_to_all(blocks, axis, 0, 0, axis_index_groups=groups)]
    ppermute x18, starting transfers between devices: 33.8 us -> 31.2 us  [moved(): return lax.ppermute(x, axis, pairs)]
    pallas_call x3 -> x5, Pallas kernels: 13.6 us -> 16.1 us  [the longest x1 3.79 us: combine_out(): pl.pallas_call(functools.partial(combine_out_kernel, slots), out_shape=[j...]
  transfers between devices with their start and end apart: 26 -> 26, of which waited for: 9 -> 10; matrix products, arithmetic and copies ran while one was open for 1% -> 1% of each run, Pallas kernels for 22% -> 25%
where the time goes in v3:
time: 192 us; the launch traced here: 191 us
  Pallas kernels  58.6 us (31%)
  starting transfers between devices  57.1 us (30%)
  waiting for transfers between devices  40.3 us (21%)
  blocking collectives  24.6 us (13%)
  local copies, waits for them, and re-layouts  9.44 us (5%)
    ppermute x18, starting transfers between devices, moved(): return lax.ppermute(x, axis, pairs)  31.2 us
    ppermute x18, waiting for transfers between devices, moved(): return lax.ppermute(x, axis, pairs)  28 us
    all_to_all x6, starting transfers between devices, exchange(): lax.all_to_all(blocks, axis, 0, 0, axis_index_groups=groups)  25.4 us
    all_to_all x1, blocking collectives, exchange(): lax.all_to_all(blocks, axis, 0, 0, axis_index_groups=groups)  24.6 us
    pallas_call x1, Pallas kernels, backward(): pl.pallas_call(functools.partial(backward_kernel, slots), out_shape=outs,...  17.3 us
    pallas_call x1, Pallas kernels, forward(): pl.pallas_call(functools.partial(forward_kernel, slots), out_shape=outs +...  17.1 us
    all_to_all x6, waiting for transfers between devices, exchange(): lax.all_to_all(blocks, axis, 0, 0, axis_index_groups=groups)  12.3 us
    unnamed x48, local copies, waits for them, and re-layouts  5.73 us
  transfers between devices with their start and end apart: 26, of which 10 were waited for; matrix products, arithmetic and copies ran while one was open for 1% of the time, Pallas kernels for 25%

profile of v3, /device:TPU:0, one launch (start us, length us, event | category | flops | bytes accessed | tf_op | source)
XLA Modules:
  0.0 190.9 jit_solution(12892026773727209415)
XLA Ops:
  0.6 0.1 collective-permute-start
  0.7 0.5 collective-permute-start.1
  1.2 0.6 stack.23.pos_ref
  1.8 2.0 %plan_slots.1 = (f32[128,128]{1,0:T(8,128)}, bf16[320,128]{1,0:T(8,128)(2,1)}) custom-call(s32[5]{0:T(128)} %stack.23.pos_ref, s32[2,1024]{1,0:T(2,128)} %bitcast.56), custom_call_target="tpu_custom_call" | custom-call | flops 4194304 | bytes 327680 | tf_op jit(solution)/shard_map/plan_slots/pallas_call | solution.py:80
  3.8 0.9 copy-done.5
  4.7 3.1 %dispatch_rows.1 = (bf16[128,3072]{1,0:T(8,128)(2,1)}, bf16[48,3072]{1,0:T(8,128)(2,1)}, bf16[48,3072]{1,0:T(8,128)(2,1)}, bf16[48,3072]{1,0:T(8,128)(2,1)}, bf16[48,3072]{1,0:T(8,128)(2,1)}) custom-call(bf16[320,128]{1,0:T(8,128)(2,1)} %get-tuple-element.75.hits_ref, bf16[128,3072]{1,0:T(8,128)(2,1)} %copy-done.5), custom_call_target="tpu_custom_call" | custom-call | flops 251658240 | bytes 3145728 | tf_op jit(solution)/shard_map/dispatch_rows/pallas_call | solution.py:134
  7.8 5.4 %all-to-all-start = ((bf16[8,16,3072]{2,1,0:T(8,128)(2,1)}), bf16[8,16,3072]{2,1,0:T(8,128)(2,1)S(1)}, u32[]{:S(2)}, u32[]{:S(2)}) async-start(bf16[8,16,3072]{2,1,0:T(8,128)(2,1)} %bitcast.42), calls=%async_computation | async-start | bytes 1572864 | tf_op jit(solution)/shard_map/all_to_all | solution.py:30
  13.2 2.0 %collective-permute-start.2 = (bf16[48,3072]{1,0:T(8,128)(2,1)}, bf16[48,3072]{1,0:T(8,128)(2,1)S(1)}, u32[]{:S(2)}, u32[]{:S(2)}) collective-permute-start(bf16[48,3072]{1,0:T(8,128)(2,1)} %get-tuple-element.78), channel_id=1, source_target_pairs={{0,8},{8,16},{16,24},{24,0},{32,40},{40,48},{48,56},{56,32},{1,9},... | collective-permute-start | bytes 884744 | tf_op jit(solution)/shard_map/ppermute | solution.py:22
  15.2 1.2 collective-permute-start.3
  16.5 0.9 copy-done.2
  17.4 3.7 %dispatch_cot.1 = (f32[128,128]{1,0:T(8,128)}, bf16[128,3072]{1,0:T(8,128)(2,1)}, bf16[48,3072]{1,0:T(8,128)(2,1)}, bf16[48,3072]{1,0:T(8,128)(2,1)}, bf16[48,30...) custom-call(s32[5]{0:T(128)} %stack.23.pos_ref, f32[128,128]{1,0:T(8,128)} %get-tuple-element.73.plan_ref, ...), custom_call_target="tpu_custom_call" | custom-call | flops 251658240 | bytes 3932160 | tf_op jit(solution)/shard_map/dispatch_cot/pallas_call | solution.py:151
  21.1 5.6 %all-to-all-done = bf16[8,16,3072]{2,1,0:T(8,128)(2,1)S(1)} async-done(((bf16[8,16,3072]{2,1,0:T(8,128)(2,1)}), bf16[8,16,3072]{2,1,0:T(8,128)(2,1)S(1)}, u32[]{:S(2)}, u32[]{:S(2)}) %all-to-all-start) | async-done | bytes 786464 | tf_op jit(solution)/shard_map/all_to_all | solution.py:30
  26.8 3.5 %all-to-all-start.1 = ((bf16[8,16,3072]{2,1,0:T(8,128)(2,1)}), bf16[8,16,3072]{2,1,0:T(8,128)(2,1)S(1)}, u32[]{:S(2)}, u32[]{:S(2)}) async-start(bf16[8,16,3072]{2,1,0:T(8,128)(2,1)} %bitcast.43), calls=%async_computation.1 | async-start | bytes 1572864 | tf_op jit(solution)/shard_map/all_to_all | solution.py:30
  30.3 1.5 collective-permute-done.2.refs_1_
  31.8 0.0 collective-permute-done.3.refs_2_
  31.8 0.9 constant_dynamic-slice_fusion.2
  32.7 3.9 %collective-permute-start.7 = (bf16[64,3072]{1,0:T(8,128)(2,1)S(1)}, bf16[64,3072]{1,0:T(8,128)(2,1)S(1)}, u32[]{:S(2)}, u32[]{:S(2)}) collective-permute-start(bf16[64,3072]{1,0:T(8,128)(2,1)S(1)} %get-tuple-element.91.refs_5_), channel_id=1, source_target_pairs={{0,2},{1,3},{2,0},{3,1},{4,6},{5,7},{6,4},{7,5},{8,10},{9,11},{10,... | collective-permute-start | bytes 1179656 | tf_op jit(solution)/shard_map/ppermute | solution.py:22
  36.6 0.7 collective-permute-start.6
  37.3 1.3 collective-permute-start.5
  38.6 2.1 %collective-permute-start.4 = (bf16[48,3072]{1,0:T(8,128)(2,1)S(1)}, bf16[48,3072]{1,0:T(8,128)(2,1)S(1)}, u32[]{:S(2)}, u32[]{:S(2)}) collective-permute-start(bf16[48,3072]{1,0:T(8,128)(2,1)S(1)} %copy-done.20), channel_id=1, source_target_pairs={{0,16},{8,24},{16,0},{24,8},{32,48},{40,56},{48,32},{56,40},{1,17}... | collective-permute-start | bytes 884744 | tf_op jit(solution)/shard_map/ppermute | solution.py:22
  40.7 7.9 %collective-permute-done.4.refs_3_ = bf16[48,3072]{1,0:T(8,128)(2,1)S(1)} collective-permute-done((bf16[48,3072]{1,0:T(8,128)(2,1)S(1)}, bf16[48,3072]{1,0:T(8,128)(2,1)S(1)}, u32[]{:S(2)}, u32[]{:S(2)}) %collective-permute-start.4) | collective-permute-done | bytes 294944 | tf_op jit(solution)/shard_map/ppermute | solution.py:22
  48.6 0.0 all-to-all-done.1
  48.6 0.0 collective-permute-done.7.refs_8_
  48.6 6.1 %collective-permute-done.6.refs_7_ = bf16[64,3072]{1,0:T(8,128)(2,1)S(1)} collective-permute-done((bf16[64,3072]{1,0:T(8,128)(2,1)S(1)}, bf16[64,3072]{1,0:T(8,128)(2,1)S(1)}, u32[]{:S(2)}, u32[]{:S(2)}) %collective-permute-start.6) | collective-permute-done | bytes 393248 | tf_op jit(solution)/shard_map/ppermute | solution.py:22
  54.7 0.9 constant_dynamic-slice_fusion
  55.6 1.3 broadcast_in_dim.12
  56.9 3.9 %all-to-all-start.3 = ((bf16[4,64,3072]{2,1,0:T(8,128)(2,1)}), bf16[4,64,3072]{2,1,0:T(8,128)(2,1)S(1)}, u32[]{:S(2)}, u32[]{:S(2)}) async-start(bf16[4,64,3072]{2,1,0:T(8,128)(2,1)} %broadcast_in_dim.12), calls=%async_computation.3 | async-start | bytes 3145728 | tf_op jit(solution)/shard_map/all_to_all | solution.py:30
  60.8 0.0 collective-permute-start.11
  60.8 3.2 %collective-permute-start.12 = (bf16[48,3072]{1,0:T(8,128)(2,1)}, bf16[48,3072]{1,0:T(8,128)(2,1)}, u32[]{:S(2)}, u32[]{:S(2)}) collective-permute-start(bf16[48,3072]{1,0:T(8,128)(2,1)} %get-tuple-element.102), channel_id=1, source_target_pairs={{0,24},{8,0},{16,8},{24,16},{32,56},{40,32},{48,40},{56,48},{1,25}... | collective-permute-start | bytes 884744 | tf_op jit(solution)/shard_map/ppermute | solution.py:22
  64.1 0.1 collective-permute-start.13
  64.2 17.1 %expert_forward.1 = (bf16[48,3072]{1,0:T(8,128)(2,1)}, bf16[48,3072]{1,0:T(8,128)(2,1)}, bf16[48,3072]{1,0:T(8,128)(2,1)}, bf16[48,3072]{1,0:T(8,128)(2,1)}, bf1...) custom-call(s32[5]{0:T(128)} %stack.23.pos_ref, ...), custom_call_target="tpu_custom_call" | custom-call | flops 9663676416 | bytes 29360128 | tf_op jit(solution)/shard_map/expert_forward/pallas_call | solution.py:292
  81.3 0.4 all-to-all-done.3
  81.7 4.4 %all-to-all-start.2 = ((bf16[4,64,3072]{2,1,0:T(8,128)(2,1)}), bf16[4,64,3072]{2,1,0:T(8,128)(2,1)S(1)}, u32[]{:S(2)}, u32[]{:S(2)}) async-start(bf16[4,64,3072]{2,1,0:T(8,128)(2,1)} %bitcast.41), calls=%async_computation.2 | async-start | bytes 3145728 | tf_op jit(solution)/shard_map/all_to_all | solution.py:30
  86.2 1.4 collective-permute-start.8
  87.5 0.7 collective-permute-start.9
  88.2 0.0 collective-permute-done.11.refs_1_
  88.2 3.4 %collective-permute-start.10 = (bf16[48,3072]{1,0:T(8,128)(2,1)}, bf16[48,3072]{1,0:T(8,128)(2,1)}, u32[]{:S(2)}, u32[]{:S(2)}) collective-permute-start(bf16[48,3072]{1,0:T(8,128)(2,1)} %get-tuple-element.99), channel_id=1, source_target_pairs={{0,16},{8,24},{16,0},{24,8},{32,48},{40,56},{48,32},{56,40},{1,17}... | collective-permute-start | bytes 884744 | tf_op jit(solution)/shard_map/ppermute | solution.py:22
  91.6 0.0 collective-permute-done.12.refs_2_
  91.6 17.3 %expert_backward.1 = (bf16[48,3072]{1,0:T(8,128)(2,1)}, bf16[48,3072]{1,0:T(8,128)(2,1)}, bf16[48,3072]{1,0:T(8,128)(2,1)}, bf16[48,3072]{1,0:T(8,128)(2,1)}, bf...) custom-call(s32[5]{0:T(128)} %stack.23.pos_ref, ...), custom_call_target="tpu_custom_call" | custom-call | flops 9663676416 | bytes 29360128 | tf_op jit(solution)/shard_map/expert_backward/pallas_call | solution.py:396
  108.9 0.0 collective-permute-done.8.refs_2_
  108.9 0.0 collective-permute-done.9.refs_4_
  108.9 0.7 copy-done.11
  109.7 1.2 copy-done
  110.9 2.7 %sum_quarters.2 = bf16[128,3072]{1,0:T(8,128)(2,1)} custom-call(s32[5]{0:T(128)} %stack.23.pos_ref, bf16[64,3072]{1,0:T(8,128)(2,1)} %get-tuple-element.124.own_ref, bf16[256,3072]{1,0:T(8,128)(2,1)} %bitcast.33), custom_call_target="tpu_custom_call" | custom-call | flops 786432 | bytes 2752512 | tf_op jit(solution)/shard_map/sum_quarters/pallas_call | solution.py:445
  113.6 3.5 %all-to-all-start.4 = ((bf16[8,16,3072]{2,1,0:T(8,128)(2,1)}), bf16[8,16,3072]{2,1,0:T(8,128)(2,1)S(1)}, u32[]{:S(2)}, u32[]{:S(2)}) async-start(bf16[8,16,3072]{2,1,0:T(8,128)(2,1)} %bitcast.38), calls=%async_computation.4 | async-start | bytes 1572864 | tf_op jit(solution)/shard_map/all_to_all | solution.py:30
  117.1 3.1 %collective-permute-start.17 = (bf16[48,3072]{1,0:T(8,128)(2,1)S(1)}, bf16[48,3072]{1,0:T(8,128)(2,1)S(1)}, u32[]{:S(2)}, u32[]{:S(2)}) collective-permute-start(bf16[48,3072]{1,0:T(8,128)(2,1)S(1)} %copy-done.22), channel_id=1, source_target_pairs={{0,24},{8,0},{16,8},{24,16},{32,56},{40,32},{48,40},{56,48},{1,25}... | collective-permute-start | bytes 884744 | tf_op jit(solution)/shard_map/ppermute | solution.py:22
  120.3 3.2 %collective-permute-start.14 = (bf16[64,3072]{1,0:T(8,128)(2,1)}, bf16[64,3072]{1,0:T(8,128)(2,1)S(1)}, u32[]{:S(2)}, u32[]{:S(2)}) collective-permute-start(bf16[64,3072]{1,0:T(8,128)(2,1)} %get-tuple-element.117), channel_id=1, source_target_pairs={{0,3},{1,0},{2,1},{3,2},{4,7},{5,4},{6,5},{7,6},{8,11},{9,8},{10,9... | collective-permute-start | bytes 1179656 | tf_op jit(solution)/shard_map/ppermute | solution.py:22
  123.5 2.3 %collective-permute-start.16 = (bf16[64,3072]{1,0:T(8,128)(2,1)}, bf16[64,3072]{1,0:T(8,128)(2,1)S(1)}, u32[]{:S(2)}, u32[]{:S(2)}) collective-permute-start(bf16[64,3072]{1,0:T(8,128)(2,1)} %get-tuple-element.119), channel_id=1, source_target_pairs={{0,2},{1,3},{2,0},{3,1},{4,6},{5,7},{6,4},{7,5},{8,10},{9,11},{10,... | collective-permute-start | bytes 1179656 | tf_op jit(solution)/shard_map/ppermute | solution.py:22
  125.8 6.6 %collective-permute-done.17.refs_2_ = bf16[48,3072]{1,0:T(8,128)(2,1)S(1)} collective-permute-done((bf16[48,3072]{1,0:T(8,128)(2,1)S(1)}, bf16[48,3072]{1,0:T(8,128)(2,1)S(1)}, u32[]{:S(2)}, u32[]{:S(2)}) %collective-permute-start.17) | collective-permute-done | bytes 294944 | tf_op jit(solution)/shard_map/ppermute | solution.py:22
  132.4 2.4 %collective-permute-start.19 = (bf16[48,3072]{1,0:T(8,128)(2,1)S(1)}, bf16[48,3072]{1,0:T(8,128)(2,1)S(1)}, u32[]{:S(2)}, u32[]{:S(2)}) collective-permute-start(bf16[48,3072]{1,0:T(8,128)(2,1)S(1)} %copy-done.21), channel_id=1, source_target_pairs={{0,16},{8,24},{16,0},{24,8},{32,48},{40,56},{48,32},{56,40},{1,17}... | collective-permute-start | bytes 884744 | tf_op jit(solution)/shard_map/ppermute | solution.py:22
  134.8 2.3 %collective-permute-done.18.refs_4_ = bf16[48,3072]{1,0:T(8,128)(2,1)S(1)} collective-permute-done((bf16[48,3072]{1,0:T(8,128)(2,1)}, bf16[48,3072]{1,0:T(8,128)(2,1)S(1)}, u32[]{:S(2)}, u32[]{:S(2)}) %collective-permute-start.18) | collective-permute-done | bytes 294944 | tf_op jit(solution)/shard_map/ppermute | solution.py:22
  137.1 3.5 %collective-permute-done.19.refs_3_ = bf16[48,3072]{1,0:T(8,128)(2,1)S(1)} collective-permute-done((bf16[48,3072]{1,0:T(8,128)(2,1)S(1)}, bf16[48,3072]{1,0:T(8,128)(2,1)S(1)}, u32[]{:S(2)}, u32[]{:S(2)}) %collective-permute-start.19) | collective-permute-done | bytes 294944 | tf_op jit(solution)/shard_map/ppermute | solution.py:22
  140.7 0.1 collective-permute-done.15.refs_2_
  140.8 0.7 copy-done.7
  141.5 0.2 copy-done.8
  141.6 0.2 copy-done.9
  141.8 2.6 %sum_quarters.3 = bf16[128,3072]{1,0:T(8,128)(2,1)} custom-call(s32[5]{0:T(128)} %stack.23.pos_ref, bf16[64,3072]{1,0:T(8,128)(2,1)} %get-tuple-element.133.own_ref, bf16[64,3072]{1,0:T(8,128)(2,1)} %get-tuple-element.134.refs_0_, bf16[64,3072]{1,0:T(8,128)(2,1)} %copy-done.7, bf16[64,3072]{1,0:T(8,128)(2,1)} %copy-done.8, bf16[64,3072]{1,0:T(8,128)(2,1)} %copy-done.9), custom_call_target="tpu_custom_call" | custom-call | flops 786432 | bytes 2752512 | tf_op jit(solution)/shard_map/sum_quarters/pallas_call | solution.py:445
  144.4 4.5 %all-to-all-start.5 = ((bf16[8,16,3072]{2,1,0:T(8,128)(2,1)}), bf16[8,16,3072]{2,1,0:T(8,128)(2,1)S(1)}, u32[]{:S(2)}, u32[]{:S(2)}) async-start(bf16[8,16,3072]{2,1,0:T(8,128)(2,1)} %bitcast.39), calls=%async_computation.5 | async-start | bytes 1572864 | tf_op jit(solution)/shard_map/all_to_all | solution.py:30
  148.9 3.8 %combine_out.1 = (bf16[128,3072]{1,0:T(8,128)(2,1)}, bf16[128,128]{1,0:T(8,128)(2,1)}) custom-call(s32[5]{0:T(128)} %stack.23.pos_ref, f32[128,128]{1,0:T(8,128)} %get-tuple-element.74.meta_ref, bf16[128,3072]{1,0:T(8,128)(2,1)} %copy-done.2, bf16[128,3072]{1,0:T(8,128)(2,1)} %bitcast.35, bf16[48,3072]{1,0:T(8,128)(2,1)} %get-tuple-element.127.refs_1_, ...), custom_call_target="tpu_custom_call" | custom-call | flops 603979776 | bytes 3538944 | tf_op jit(solution)/shard_map/combine_out/pallas_call | solution.py:496
  152.7 6.3 %all-to-all-done.5 = bf16[8,16,3072]{2,1,0:T(8,128)(2,1)S(1)} async-done(((bf16[8,16,3072]{2,1,0:T(8,128)(2,1)}), bf16[8,16,3072]{2,1,0:T(8,128)(2,1)S(1)}, u32[]{:S(2)}, u32[]{:S(2)}) %all-to-all-start.5) | async-done | bytes 786464 | tf_op jit(solution)/shard_map/all_to_all | solution.py:30
  159.0 0.9 copy-done.1
  159.9 3.6 %combine_grad.1 = bf16[128,6272]{1,0:T(8,128)(2,1)} custom-call(s32[5]{0:T(128)} %stack.23.pos_ref, f32[128,128]{1,0:T(8,128)} %get-tuple-element.74.meta_ref, bf16[128,3072]{1,0:T(8,128)(2,1)} %get-tuple-element.131.out_terms_ref, bf16[128,128]{1,0:T(8,128)(2,1)} %get-tuple-element.132.dots_ref, bf16[128,3072]{1,0:T(8,128)(2,1)} %bitcast.34, ...), custom_call_target="tpu_custom_call" | custom-call | flops 301989888 | bytes 4325376 | tf_op jit(solution)/shard_map/combine_grad/pallas_call | solution.py:527
  163.5 24.6 %all_to_all.35 = bf16[8,16,6272]{2,1,0:T(8,128)(2,1)} all-to-all(bf16[8,16,6272]{2,1,0:T(8,128)(2,1)} %bitcast.31), channel_id=1, replica_groups=mesh['pipe'=2,'expert'=8,'etp'=8] {'etp'}, dimensions={0} | all-to-all | bytes 3211264 | tf_op jit(solution)/shard_map/all_to_all | solution.py:30
  188.1 2.8 %finish.1 = (bf16[16,3072]{1,0:T(8,128)(2,1)}, bf16[16,3072]{1,0:T(8,128)(2,1)}) custom-call(s32[5]{0:T(128)} %stack.23.pos_ref, f32[128,128]{1,0:T(8,128)} %get-tuple-element.74.meta_ref, bf16[8,3072]{1,0:T(8,128)(2,1)} %bitcast.45, bf16[128,6272]{1,0:T(8,128)(2,1)} %bitcast.32), custom_call_target="tpu_custom_call" | custom-call | flops 11796480 | bytes 1966080 | tf_op jit(solution)/shard_map/finish/pallas_call | solution.py:562
  (51 shorter events, 0.1 us)
Async XLA Ops:
  0.6 3.2 %collective-permute-start = (bf16[128,3072]{1,0:T(8,128)(2,1)}, bf16[128,3072]{1,0:T(8,128)(2,1)S(1)}, u32[]{:S(2)}, u32[]{:S(2)}) collective-permute-start(bf16[128,3072]{1,0:T(8,128)(2,1)} %bitcast.52), channel_id=1, source_target_pairs={{0,64},{64,0},{1,65},{65,1},{2,66},{66,2},{3,67},{67,3},{4,68},{68... | collective-permute-start | bytes 2359304 | tf_op jit(solution)/shard_map/ppermute | solution.py:588
  0.7 15.7 %collective-permute-start.1 = (bf16[128,3072]{1,0:T(8,128)(2,1)}, bf16[128,3072]{1,0:T(8,128)(2,1)S(1)}, u32[]{:S(2)}, u32[]{:S(2)}) collective-permute-start(bf16[128,3072]{1,0:T(8,128)(2,1)} %bitcast.53), channel_id=1, source_target_pairs={{0,64},{64,0},{1,65},{65,1},{2,66},{66,2},{3,67},{67,3},{4,68},{68... | collective-permute-start | bytes 2359304 | tf_op jit(solution)/shard_map/ppermute | solution.py:589
  3.8 0.9 copy-start.5
  7.8 19.0 %all-to-all-start = ((bf16[8,16,3072]{2,1,0:T(8,128)(2,1)}), bf16[8,16,3072]{2,1,0:T(8,128)(2,1)S(1)}, u32[]{:S(2)}, u32[]{:S(2)}) async-start(bf16[8,16,3072]{2,1,0:T(8,128)(2,1)} %bitcast.42), calls=%async_computation | async-start | bytes 1572864 | tf_op jit(solution)/shard_map/all_to_all | solution.py:30
  13.2 18.6 %collective-permute-start.2 = (bf16[48,3072]{1,0:T(8,128)(2,1)}, bf16[48,3072]{1,0:T(8,128)(2,1)S(1)}, u32[]{:S(2)}, u32[]{:S(2)}) collective-permute-start(bf16[48,3072]{1,0:T(8,128)(2,1)} %get-tuple-element.78), channel_id=1, source_target_pairs={{0,8},{8,16},{16,24},{24,0},{32,40},{40,48},{48,56},{56,32},{1,9},... | collective-permute-start | bytes 884744 | tf_op jit(solution)/shard_map/ppermute | solution.py:22
  15.2 16.6 %collective-permute-start.3 = (bf16[48,3072]{1,0:T(8,128)(2,1)}, bf16[48,3072]{1,0:T(8,128)(2,1)S(1)}, u32[]{:S(2)}, u32[]{:S(2)}) collective-permute-start(bf16[48,3072]{1,0:T(8,128)(2,1)} %get-tuple-element.79), channel_id=1, source_target_pairs={{0,24},{8,0},{16,8},{24,16},{32,56},{40,32},{48,40},{56,48},{1,25}... | collective-permute-start | bytes 884744 | tf_op jit(solution)/shard_map/ppermute | solution.py:22
  16.5 0.9 copy-start.2
  21.1 17.5 %copy-start.20 = (bf16[48,3072]{1,0:T(8,128)(2,1)S(1)}, bf16[48,3072]{1,0:T(8,128)(2,1)}, u32[]{:S(2)}) copy-start(bf16[48,3072]{1,0:T(8,128)(2,1)} %get-tuple-element.83) | copy-start | bytes 884740
  26.8 21.8 %all-to-all-start.1 = ((bf16[8,16,3072]{2,1,0:T(8,128)(2,1)}), bf16[8,16,3072]{2,1,0:T(8,128)(2,1)S(1)}, u32[]{:S(2)}, u32[]{:S(2)}) async-start(bf16[8,16,3072]{2,1,0:T(8,128)(2,1)} %bitcast.43), calls=%async_computation.1 | async-start | bytes 1572864 | tf_op jit(solution)/shard_map/all_to_all | solution.py:30
  31.8 4.8 %copy-start.18 = (bf16[48,3072]{1,0:T(8,128)(2,1)}, bf16[48,3072]{1,0:T(8,128)(2,1)S(1)}, u32[]{:S(2)}) copy-start(bf16[48,3072]{1,0:T(8,128)(2,1)S(1)} %collective-permute-done.2.refs_1_) | copy-start | bytes 884740
  31.8 4.8 %copy-start.19 = (bf16[48,3072]{1,0:T(8,128)(2,1)}, bf16[48,3072]{1,0:T(8,128)(2,1)S(1)}, u32[]{:S(2)}) copy-start(bf16[48,3072]{1,0:T(8,128)(2,1)S(1)} %collective-permute-done.3.refs_2_) | copy-start | bytes 884740
  32.7 24.3 %copy-start.6 = (bf16[64,3072]{1,0:T(8,128)(2,1)}, bf16[64,3072]{1,0:T(8,128)(2,1)S(1)}, u32[]{:S(2)}) copy-start(bf16[64,3072]{1,0:T(8,128)(2,1)S(1)} %get-tuple-element.91.refs_5_) | copy-start | bytes 1179652
  32.7 15.9 %collective-permute-start.7 = (bf16[64,3072]{1,0:T(8,128)(2,1)S(1)}, bf16[64,3072]{1,0:T(8,128)(2,1)S(1)}, u32[]{:S(2)}, u32[]{:S(2)}) collective-permute-start(bf16[64,3072]{1,0:T(8,128)(2,1)S(1)} %get-tuple-element.91.refs_5_), channel_id=1, source_target_pairs={{0,2},{1,3},{2,0},{3,1},{4,6},{5,7},{6,4},{7,5},{8,10},{9,11},{10,... | collective-permute-start | bytes 1179656 | tf_op jit(solution)/shard_map/ppermute | solution.py:22
  36.6 18.2 %collective-permute-start.6 = (bf16[64,3072]{1,0:T(8,128)(2,1)S(1)}, bf16[64,3072]{1,0:T(8,128)(2,1)S(1)}, u32[]{:S(2)}, u32[]{:S(2)}) collective-permute-start(bf16[64,3072]{1,0:T(8,128)(2,1)S(1)} %get-tuple-element.91.refs_5_), channel_id=1, source_target_pairs={{0,3},{1,0},{2,1},{3,2},{4,7},{5,4},{6,5},{7,6},{8,11},{9,8},{10,9... | collective-permute-start | bytes 1179656 | tf_op jit(solution)/shard_map/ppermute | solution.py:22
  37.3 17.5 %collective-permute-start.5 = (bf16[64,3072]{1,0:T(8,128)(2,1)S(1)}, bf16[64,3072]{1,0:T(8,128)(2,1)S(1)}, u32[]{:S(2)}, u32[]{:S(2)}) collective-permute-start(bf16[64,3072]{1,0:T(8,128)(2,1)S(1)} %get-tuple-element.91.refs_5_), channel_id=1, source_target_pairs={{0,1},{1,2},{2,3},{3,0},{4,5},{5,6},{6,7},{7,4},{8,9},{9,10},{10,1... | collective-permute-start | bytes 1179656 | tf_op jit(solution)/shard_map/ppermute | solution.py:22
  38.6 10.0 %collective-permute-start.4 = (bf16[48,3072]{1,0:T(8,128)(2,1)S(1)}, bf16[48,3072]{1,0:T(8,128)(2,1)S(1)}, u32[]{:S(2)}, u32[]{:S(2)}) collective-permute-start(bf16[48,3072]{1,0:T(8,128)(2,1)S(1)} %copy-done.20), channel_id=1, source_target_pairs={{0,16},{8,24},{16,0},{24,8},{32,48},{40,56},{48,32},{56,40},{1,17}... | collective-permute-start | bytes 884744 | tf_op jit(solution)/shard_map/ppermute | solution.py:22
  48.6 8.3 %copy-start.23 = (bf16[48,3072]{1,0:T(8,128)(2,1)}, bf16[48,3072]{1,0:T(8,128)(2,1)S(1)}, u32[]{:S(2)}) copy-start(bf16[48,3072]{1,0:T(8,128)(2,1)S(1)} %collective-permute-done.4.refs_3_) | copy-start | bytes 884740
  48.6 8.3 %copy-start.15 = (bf16[64,3072]{1,0:T(8,128)(2,1)}, bf16[64,3072]{1,0:T(8,128)(2,1)S(1)}, u32[]{:S(2)}) copy-start(bf16[64,3072]{1,0:T(8,128)(2,1)S(1)} %collective-permute-done.7.refs_8_) | copy-start | bytes 1179652
  54.7 2.2 %copy-start.16 = (bf16[64,3072]{1,0:T(8,128)(2,1)}, bf16[64,3072]{1,0:T(8,128)(2,1)S(1)}, u32[]{:S(2)}) copy-start(bf16[64,3072]{1,0:T(8,128)(2,1)S(1)} %collective-permute-done.6.refs_7_) | copy-start | bytes 1179652
  54.7 2.2 %copy-start.17 = (bf16[64,3072]{1,0:T(8,128)(2,1)}, bf16[64,3072]{1,0:T(8,128)(2,1)S(1)}, u32[]{:S(2)}) copy-start(bf16[64,3072]{1,0:T(8,128)(2,1)S(1)} %collective-permute-done.5.refs_6_) | copy-start | bytes 1179652
  56.9 24.8 %all-to-all-start.3 = ((bf16[4,64,3072]{2,1,0:T(8,128)(2,1)}), bf16[4,64,3072]{2,1,0:T(8,128)(2,1)S(1)}, u32[]{:S(2)}, u32[]{:S(2)}) async-start(bf16[4,64,3072]{2,1,0:T(8,128)(2,1)} %broadcast_in_dim.12), calls=%async_computation.3 | async-start | bytes 3145728 | tf_op jit(solution)/shard_map/all_to_all | solution.py:30
  60.8 27.3 %collective-permute-start.11 = (bf16[48,3072]{1,0:T(8,128)(2,1)}, bf16[48,3072]{1,0:T(8,128)(2,1)}, u32[]{:S(2)}, u32[]{:S(2)}) collective-permute-start(bf16[48,3072]{1,0:T(8,128)(2,1)} %get-tuple-element.101), channel_id=1, source_target_pairs={{0,8},{8,16},{16,24},{24,0},{32,40},{40,48},{48,56},{56,32},{1,9},... | collective-permute-start | bytes 884744 | tf_op jit(solution)/shard_map/ppermute | solution.py:22
  60.8 30.8 %collective-permute-start.12 = (bf16[48,3072]{1,0:T(8,128)(2,1)}, bf16[48,3072]{1,0:T(8,128)(2,1)}, u32[]{:S(2)}, u32[]{:S(2)}) collective-permute-start(bf16[48,3072]{1,0:T(8,128)(2,1)} %get-tuple-element.102), channel_id=1, source_target_pairs={{0,24},{8,0},{16,8},{24,16},{32,56},{40,32},{48,40},{56,48},{1,25}... | collective-permute-start | bytes 884744 | tf_op jit(solution)/shard_map/ppermute | solution.py:22
  64.1 27.5 %collective-permute-start.13 = (bf16[48,3072]{1,0:T(8,128)(2,1)}, bf16[48,3072]{1,0:T(8,128)(2,1)}, u32[]{:S(2)}, u32[]{:S(2)}) collective-permute-start(bf16[48,3072]{1,0:T(8,128)(2,1)} %get-tuple-element.103), channel_id=1, source_target_pairs={{0,16},{8,24},{16,0},{24,8},{32,48},{40,56},{48,32},{56,40},{1,17}... | collective-permute-start | bytes 884744 | tf_op jit(solution)/shard_map/ppermute | solution.py:22
  81.7 9.9 %copy-start.4 = (bf16[4,64,3072]{2,1,0:T(8,128)(2,1)}, bf16[4,64,3072]{2,1,0:T(8,128)(2,1)S(1)}, u32[]{:S(2)}) copy-start(bf16[4,64,3072]{2,1,0:T(8,128)(2,1)S(1)} %all-to-all-done.3) | copy-start | bytes 4718596
  81.7 27.9 %all-to-all-start.2 = ((bf16[4,64,3072]{2,1,0:T(8,128)(2,1)}), bf16[4,64,3072]{2,1,0:T(8,128)(2,1)S(1)}, u32[]{:S(2)}, u32[]{:S(2)}) async-start(bf16[4,64,3072]{2,1,0:T(8,128)(2,1)} %bitcast.41), calls=%async_computation.2 | async-start | bytes 3145728 | tf_op jit(solution)/shard_map/all_to_all | solution.py:30
  86.2 22.7 %collective-permute-start.8 = (bf16[48,3072]{1,0:T(8,128)(2,1)}, bf16[48,3072]{1,0:T(8,128)(2,1)S(1)}, u32[]{:S(2)}, u32[]{:S(2)}) collective-permute-start(bf16[48,3072]{1,0:T(8,128)(2,1)} %get-tuple-element.97), channel_id=1, source_target_pairs={{0,24},{8,0},{16,8},{24,16},{32,56},{40,32},{48,40},{56,48},{1,25}... | collective-permute-start | bytes 884744 | tf_op jit(solution)/shard_map/ppermute | solution.py:22
  87.5 21.4 %collective-permute-start.9 = (bf16[48,3072]{1,0:T(8,128)(2,1)}, bf16[48,3072]{1,0:T(8,128)(2,1)S(1)}, u32[]{:S(2)}, u32[]{:S(2)}) collective-permute-start(bf16[48,3072]{1,0:T(8,128)(2,1)} %get-tuple-element.98), channel_id=1, source_target_pairs={{0,8},{8,16},{16,24},{24,0},{32,40},{40,48},{48,56},{56,32},{1,9},... | collective-permute-start | bytes 884744 | tf_op jit(solution)/shard_map/ppermute | solution.py:22
  88.2 21.5 %collective-permute-start.10 = (bf16[48,3072]{1,0:T(8,128)(2,1)}, bf16[48,3072]{1,0:T(8,128)(2,1)}, u32[]{:S(2)}, u32[]{:S(2)}) collective-permute-start(bf16[48,3072]{1,0:T(8,128)(2,1)} %get-tuple-element.99), channel_id=1, source_target_pairs={{0,16},{8,24},{16,0},{24,8},{32,48},{40,56},{48,32},{56,40},{1,17}... | collective-permute-start | bytes 884744 | tf_op jit(solution)/shard_map/ppermute | solution.py:22
  108.9 40.0 %copy-start.10 = (bf16[48,3072]{1,0:T(8,128)(2,1)}, bf16[48,3072]{1,0:T(8,128)(2,1)S(1)}, u32[]{:S(2)}) copy-start(bf16[48,3072]{1,0:T(8,128)(2,1)S(1)} %collective-permute-done.8.refs_2_) | copy-start | bytes 884740
  108.9 0.8 copy-start.11
  109.7 1.2 copy-start
  110.9 6.3 %copy-start.22 = (bf16[48,3072]{1,0:T(8,128)(2,1)S(1)}, bf16[48,3072]{1,0:T(8,128)(2,1)}, u32[]{:S(2)}) copy-start(bf16[48,3072]{1,0:T(8,128)(2,1)} %get-tuple-element.121) | copy-start | bytes 884740
  110.9 21.5 %copy-start.21 = (bf16[48,3072]{1,0:T(8,128)(2,1)S(1)}, bf16[48,3072]{1,0:T(8,128)(2,1)}, u32[]{:S(2)}) copy-start(bf16[48,3072]{1,0:T(8,128)(2,1)} %get-tuple-element.123) | copy-start | bytes 884740
  113.6 27.2 %all-to-all-start.4 = ((bf16[8,16,3072]{2,1,0:T(8,128)(2,1)}), bf16[8,16,3072]{2,1,0:T(8,128)(2,1)S(1)}, u32[]{:S(2)}, u32[]{:S(2)}) async-start(bf16[8,16,3072]{2,1,0:T(8,128)(2,1)} %bitcast.38), calls=%async_computation.4 | async-start | bytes 1572864 | tf_op jit(solution)/shard_map/all_to_all | solution.py:30
  117.1 15.3 %collective-permute-start.17 = (bf16[48,3072]{1,0:T(8,128)(2,1)S(1)}, bf16[48,3072]{1,0:T(8,128)(2,1)S(1)}, u32[]{:S(2)}, u32[]{:S(2)}) collective-permute-start(bf16[48,3072]{1,0:T(8,128)(2,1)S(1)} %copy-done.22), channel_id=1, source_target_pairs={{0,24},{8,0},{16,8},{24,16},{32,56},{40,32},{48,40},{56,48},{1,25}... | collective-permute-start | bytes 884744 | tf_op jit(solution)/shard_map/ppermute | solution.py:22
  120.3 20.4 %collective-permute-start.14 = (bf16[64,3072]{1,0:T(8,128)(2,1)}, bf16[64,3072]{1,0:T(8,128)(2,1)S(1)}, u32[]{:S(2)}, u32[]{:S(2)}) collective-permute-start(bf16[64,3072]{1,0:T(8,128)(2,1)} %get-tuple-element.117), channel_id=1, source_target_pairs={{0,3},{1,0},{2,1},{3,2},{4,7},{5,4},{6,5},{7,6},{8,11},{9,8},{10,9... | collective-permute-start | bytes 1179656 | tf_op jit(solution)/shard_map/ppermute | solution.py:22
  123.5 17.2 %collective-permute-start.15 = (bf16[64,3072]{1,0:T(8,128)(2,1)}, bf16[64,3072]{1,0:T(8,128)(2,1)S(1)}, u32[]{:S(2)}, u32[]{:S(2)}) collective-permute-start(bf16[64,3072]{1,0:T(8,128)(2,1)} %get-tuple-element.118), channel_id=1, source_target_pairs={{0,1},{1,2},{2,3},{3,0},{4,5},{5,6},{6,7},{7,4},{8,9},{9,10},{10,1... | collective-permute-start | bytes 1179656 | tf_op jit(solution)/shard_map/ppermute | solution.py:22
  123.5 17.2 %collective-permute-start.16 = (bf16[64,3072]{1,0:T(8,128)(2,1)}, bf16[64,3072]{1,0:T(8,128)(2,1)S(1)}, u32[]{:S(2)}, u32[]{:S(2)}) collective-permute-start(bf16[64,3072]{1,0:T(8,128)(2,1)} %get-tuple-element.119), channel_id=1, source_target_pairs={{0,2},{1,3},{2,0},{3,1},{4,6},{5,7},{6,4},{7,5},{8,10},{9,11},{10,... | collective-permute-start | bytes 1179656 | tf_op jit(solution)/shard_map/ppermute | solution.py:22
  125.8 11.3 %collective-permute-start.18 = (bf16[48,3072]{1,0:T(8,128)(2,1)}, bf16[48,3072]{1,0:T(8,128)(2,1)S(1)}, u32[]{:S(2)}, u32[]{:S(2)}) collective-permute-start(bf16[48,3072]{1,0:T(8,128)(2,1)} %get-tuple-element.122), channel_id=1, source_target_pairs={{0,8},{8,16},{16,24},{24,0},{32,40},{40,48},{48,56},{56,32},{1,9},... | collective-permute-start | bytes 884744 | tf_op jit(solution)/shard_map/ppermute | solution.py:22
  132.4 26.6 %copy-start.12 = (bf16[48,3072]{1,0:T(8,128)(2,1)}, bf16[48,3072]{1,0:T(8,128)(2,1)S(1)}, u32[]{:S(2)}) copy-start(bf16[48,3072]{1,0:T(8,128)(2,1)S(1)} %collective-permute-done.17.refs_2_) | copy-start | bytes 884740
  132.4 8.2 %collective-permute-start.19 = (bf16[48,3072]{1,0:T(8,128)(2,1)S(1)}, bf16[48,3072]{1,0:T(8,128)(2,1)S(1)}, u32[]{:S(2)}, u32[]{:S(2)}) collective-permute-start(bf16[48,3072]{1,0:T(8,128)(2,1)S(1)} %copy-done.21), channel_id=1, source_target_pairs={{0,16},{8,24},{16,0},{24,8},{32,48},{40,56},{48,32},{56,40},{1,17}... | collective-permute-start | bytes 884744 | tf_op jit(solution)/shard_map/ppermute | solution.py:22
  137.1 21.9 %copy-start.13 = (bf16[48,3072]{1,0:T(8,128)(2,1)}, bf16[48,3072]{1,0:T(8,128)(2,1)S(1)}, u32[]{:S(2)}) copy-start(bf16[48,3072]{1,0:T(8,128)(2,1)S(1)} %collective-permute-done.18.refs_4_) | copy-start | bytes 884740
  140.6 18.4 %copy-start.14 = (bf16[48,3072]{1,0:T(8,128)(2,1)}, bf16[48,3072]{1,0:T(8,128)(2,1)S(1)}, u32[]{:S(2)}) copy-start(bf16[48,3072]{1,0:T(8,128)(2,1)S(1)} %collective-permute-done.19.refs_3_) | copy-start | bytes 884740
  140.6 0.8 copy-start.7
  140.8 0.9 copy-start.8
  140.8 1.0 copy-start.9
  140.8 3.6 %copy-start.3 = (bf16[8,16,3072]{2,1,0:T(8,128)(2,1)}, bf16[8,16,3072]{2,1,0:T(8,128)(2,1)S(1)}, u32[]{:S(2)}) copy-start(bf16[8,16,3072]{2,1,0:T(8,128)(2,1)S(1)} %all-to-all-done.4) | copy-start | bytes 2359300
  144.4 14.6 %all-to-all-start.5 = ((bf16[8,16,3072]{2,1,0:T(8,128)(2,1)}), bf16[8,16,3072]{2,1,0:T(8,128)(2,1)S(1)}, u32[]{:S(2)}, u32[]{:S(2)}) async-start(bf16[8,16,3072]{2,1,0:T(8,128)(2,1)} %bitcast.39), calls=%async_computation.5 | async-start | bytes 1572864 | tf_op jit(solution)/shard_map/all_to_all | solution.py:30
  159.0 0.9 copy-start.1

commit v4 on v3

--- a/solution.py
+++ b/solution.py
@@ -12,7 +12,7 @@
 SIDE = 4
 STEPS = (0, 1, SIDE - 1, 2)
 FORWARD_TILES = (256, 1024)
-BACKWARD_TILES = (512, 512)
+BACKWARD_TILES = (512, 1024)
 AHEAD = 2
 VMEM_LIMIT = 56 * 1024 * 1024
 
@@ -608,11 +608,12 @@
     quarters = along("etp", 1, [quarter] * SIDE)
     rows_far = moved(rows_far, "expert", STEPS[-1])
     cot_head = exchange(cot_head, "expert")
-    rows_far, quarters, cot_head, cot = lax.optimization_barrier((rows_far, quarters, cot_head, cot))
+    cot_far = moved(cot[STEPS[-1]], "expert", STEPS[-1])
+    rows_far, cot_far, quarters, cot_head, cot = lax.optimization_barrier((rows_far, cot_far, quarters, cot_head, cot))
     chunks = (*rows, rows_far, own, *quarters)
     own, quarter = halves(position, cot_head, slots)
     quarters = exchange(jnp.broadcast_to(quarter[None], (SIDE, *quarter.shape)).reshape(SIDE * slots, -1), "etp", low=True)
-    cot = along("expert", 1, [cot[by] for by in STEPS])
+    cot = [*along("expert", 1, [cot[by] for by in STEPS[:-1]]), cot_far]
     *out, own_out, out_quarters, swished, slope = forward(position, chunks, w_gate, w_up, w_down, slots)
     out_quarters = exchange(out_quarters, "etp", low=True)
     out = along("expert", -1, out)

time: 192 us -> 190 us (0.990)
  starting transfers between devices: 57.1 us -> 59.3 us
    all_to_all x6, starting transfers between devices: 25.4 us -> 29.5 us  [exchange(): lax.all_to_all(blocks, axis, 0, 0, axis_index_groups=groups)]
    ppermute x18, starting transfers between devices: 31.2 us -> 29.3 us  [moved(): return lax.ppermute(x, axis, pairs)]
    unnamed x48 -> x52, local copies, waits for them, and re-layouts: 5.73 us -> 5.78 us
  transfers between devices with their start and end apart: 26 -> 26, of which waited for: 10 -> 8; matrix products, arithmetic and copies ran while one was open for 1% -> 1% of each run, Pallas kernels for 25% -> 24%
where the time goes in v4:
time: 190 us; the launch traced here: 189 us
  starting transfers between devices  59.3 us (31%)
  Pallas kernels  57.7 us (30%)
  waiting for transfers between devices  38.5 us (20%)
  blocking collectives  23.4 us (12%)
  local copies, waits for them, and re-layouts  9.53 us (5%)
    all_to_all x6, starting transfers between devices, exchange(): lax.all_to_all(blocks, axis, 0, 0, axis_index_groups=groups)  29.5 us
    ppermute x18, starting transfers between devices, moved(): return lax.ppermute(x, axis, pairs)  29.3 us
    ppermute x18, waiting for transfers between devices, moved(): return lax.ppermute(x, axis, pairs)  26.5 us
    all_to_all x1, blocking collectives, exchange(): lax.all_to_all(blocks, axis, 0, 0, axis_index_groups=groups)  23.4 us
    pallas_call x1, Pallas kernels, forward(): pl.pallas_call(functools.partial(forward_kernel, slots), out_shape=outs +...  17.1 us
    pallas_call x1, Pallas kernels, backward(): pl.pallas_call(functools.partial(backward_kernel, slots), out_shape=outs,...  16.5 us
    all_to_all x6, waiting for transfers between devices, exchange(): lax.all_to_all(blocks, axis, 0, 0, axis_index_groups=groups)  12 us
    unnamed x52, local copies, waits for them, and re-layouts  5.78 us
  transfers between devices with their start and end apart: 26, of which 8 were waited for; matrix products, arithmetic and copies ran while one was open for 1% of the time, Pallas kernels for 24%

profile of v4, /device:TPU:0, one launch (start us, length us, event | category | flops | bytes accessed | tf_op | source)
XLA Modules:
  0.0 189.4 jit_solution(16040583583263036878)
XLA Ops:
  0.6 0.1 collective-permute-start
  0.7 0.5 collective-permute-start.1
  1.2 0.6 stack.23.pos_ref
  1.8 2.0 %plan_slots.1 = (f32[128,128]{1,0:T(8,128)}, bf16[320,128]{1,0:T(8,128)(2,1)}) custom-call(s32[5]{0:T(128)} %stack.23.pos_ref, s32[2,1024]{1,0:T(2,128)} %bitcast.56), custom_call_target="tpu_custom_call" | custom-call | flops 4194304 | bytes 327680 | tf_op jit(solution)/shard_map/plan_slots/pallas_call | solution.py:80
  3.8 0.9 copy-done.5
  4.7 3.0 %dispatch_rows.1 = (bf16[128,3072]{1,0:T(8,128)(2,1)}, bf16[48,3072]{1,0:T(8,128)(2,1)}, bf16[48,3072]{1,0:T(8,128)(2,1)}, bf16[48,3072]{1,0:T(8,128)(2,1)}, bf16[48,3072]{1,0:T(8,128)(2,1)}) custom-call(bf16[320,128]{1,0:T(8,128)(2,1)} %get-tuple-element.75.hits_ref, bf16[128,3072]{1,0:T(8,128)(2,1)} %copy-done.5), custom_call_target="tpu_custom_call" | custom-call | flops 251658240 | bytes 3145728 | tf_op jit(solution)/shard_map/dispatch_rows/pallas_call | solution.py:134
  7.8 5.4 %all-to-all-start = ((bf16[8,16,3072]{2,1,0:T(8,128)(2,1)}), bf16[8,16,3072]{2,1,0:T(8,128)(2,1)S(1)}, u32[]{:S(2)}, u32[]{:S(2)}) async-start(bf16[8,16,3072]{2,1,0:T(8,128)(2,1)} %bitcast.43), calls=%async_computation | async-start | bytes 1572864 | tf_op jit(solution)/shard_map/all_to_all | solution.py:30
  13.2 2.0 %collective-permute-start.2 = (bf16[48,3072]{1,0:T(8,128)(2,1)}, bf16[48,3072]{1,0:T(8,128)(2,1)S(1)}, u32[]{:S(2)}, u32[]{:S(2)}) collective-permute-start(bf16[48,3072]{1,0:T(8,128)(2,1)} %get-tuple-element.78), channel_id=1, source_target_pairs={{0,8},{8,16},{16,24},{24,0},{32,40},{40,48},{48,56},{56,32},{1,9},... | collective-permute-start | bytes 884744 | tf_op jit(solution)/shard_map/ppermute | solution.py:22
  15.2 1.2 collective-permute-start.3
  16.4 0.9 copy-done.2
  17.4 3.6 %dispatch_cot.1 = (f32[128,128]{1,0:T(8,128)}, bf16[128,3072]{1,0:T(8,128)(2,1)}, bf16[48,3072]{1,0:T(8,128)(2,1)}, bf16[48,3072]{1,0:T(8,128)(2,1)}, bf16[48,30...) custom-call(s32[5]{0:T(128)} %stack.23.pos_ref, f32[128,128]{1,0:T(8,128)} %get-tuple-element.73.plan_ref, ...), custom_call_target="tpu_custom_call" | custom-call | flops 251658240 | bytes 3932160 | tf_op jit(solution)/shard_map/dispatch_cot/pallas_call | solution.py:151
  21.0 5.7 %all-to-all-done = bf16[8,16,3072]{2,1,0:T(8,128)(2,1)S(1)} async-done(((bf16[8,16,3072]{2,1,0:T(8,128)(2,1)}), bf16[8,16,3072]{2,1,0:T(8,128)(2,1)S(1)}, u32[]{:S(2)}, u32[]{:S(2)}) %all-to-all-start) | async-done | bytes 786464 | tf_op jit(solution)/shard_map/all_to_all | solution.py:30
  26.7 3.5 %all-to-all-start.1 = ((bf16[8,16,3072]{2,1,0:T(8,128)(2,1)}), bf16[8,16,3072]{2,1,0:T(8,128)(2,1)S(1)}, u32[]{:S(2)}, u32[]{:S(2)}) async-start(bf16[8,16,3072]{2,1,0:T(8,128)(2,1)} %bitcast.42), calls=%async_computation.1 | async-start | bytes 1572864 | tf_op jit(solution)/shard_map/all_to_all | solution.py:30
  30.3 1.5 collective-permute-done.2.refs_1_
  31.7 0.0 collective-permute-done.3.refs_2_
  31.7 0.9 constant_dynamic-slice_fusion.2
  32.6 3.9 %collective-permute-start.8 = (bf16[64,3072]{1,0:T(8,128)(2,1)S(1)}, bf16[64,3072]{1,0:T(8,128)(2,1)S(1)}, u32[]{:S(2)}, u32[]{:S(2)}) collective-permute-start(bf16[64,3072]{1,0:T(8,128)(2,1)S(1)} %get-tuple-element.91.refs_5_), channel_id=1, source_target_pairs={{0,2},{1,3},{2,0},{3,1},{4,6},{5,7},{6,4},{7,5},{8,10},{9,11},{10,... | collective-permute-start | bytes 1179656 | tf_op jit(solution)/shard_map/ppermute | solution.py:22
  36.5 0.7 collective-permute-start.7
  37.2 1.3 collective-permute-start.6
  38.5 2.1 %collective-permute-start.4 = (bf16[48,3072]{1,0:T(8,128)(2,1)S(1)}, bf16[48,3072]{1,0:T(8,128)(2,1)S(1)}, u32[]{:S(2)}, u32[]{:S(2)}) collective-permute-start(bf16[48,3072]{1,0:T(8,128)(2,1)S(1)} %copy-done.21), channel_id=1, source_target_pairs={{0,16},{8,24},{16,0},{24,8},{32,48},{40,56},{48,32},{56,40},{1,17}... | collective-permute-start | bytes 884744 | tf_op jit(solution)/shard_map/ppermute | solution.py:22
  40.7 1.4 collective-permute-start.5
  42.1 7.9 %collective-permute-done.4.refs_3_ = bf16[48,3072]{1,0:T(8,128)(2,1)S(1)} collective-permute-done((bf16[48,3072]{1,0:T(8,128)(2,1)S(1)}, bf16[48,3072]{1,0:T(8,128)(2,1)S(1)}, u32[]{:S(2)}, u32[]{:S(2)}) %collective-permute-start.4) | collective-permute-done | bytes 294944 | tf_op jit(solution)/shard_map/ppermute | solution.py:22
  50.0 4.9 %collective-permute-done.5.refs_3_ = bf16[48,3072]{1,0:T(8,128)(2,1)S(1)} collective-permute-done((bf16[48,3072]{1,0:T(8,128)(2,1)S(1)}, bf16[48,3072]{1,0:T(8,128)(2,1)S(1)}, u32[]{:S(2)}, u32[]{:S(2)}) %collective-permute-start.5) | collective-permute-done | bytes 294944 | tf_op jit(solution)/shard_map/ppermute | solution.py:22
  54.9 0.0 all-to-all-done.1
  54.9 0.0 collective-permute-done.8.refs_8_
  54.9 0.0 collective-permute-done.6.refs_6_
  54.9 0.9 constant_dynamic-slice_fusion
  55.9 1.3 broadcast_in_dim.12
  57.2 5.3 %all-to-all-start.3 = ((bf16[4,64,3072]{2,1,0:T(8,128)(2,1)}), bf16[4,64,3072]{2,1,0:T(8,128)(2,1)S(1)}, u32[]{:S(2)}, u32[]{:S(2)}) async-start(bf16[4,64,3072]{2,1,0:T(8,128)(2,1)} %broadcast_in_dim.12), calls=%async_computation.3 | async-start | bytes 3145728 | tf_op jit(solution)/shard_map/all_to_all | solution.py:30
  62.5 0.5 collective-permute-start.12
  63.1 2.7 %collective-permute-start.13 = (bf16[48,3072]{1,0:T(8,128)(2,1)}, bf16[48,3072]{1,0:T(8,128)(2,1)}, u32[]{:S(2)}, u32[]{:S(2)}) collective-permute-start(bf16[48,3072]{1,0:T(8,128)(2,1)} %get-tuple-element.102), channel_id=1, source_target_pairs={{0,24},{8,0},{16,8},{24,16},{32,56},{40,32},{48,40},{56,48},{1,25}... | collective-permute-start | bytes 884744 | tf_op jit(solution)/shard_map/ppermute | solution.py:22
  65.8 17.1 %expert_forward.1 = (bf16[48,3072]{1,0:T(8,128)(2,1)}, bf16[48,3072]{1,0:T(8,128)(2,1)}, bf16[48,3072]{1,0:T(8,128)(2,1)}, bf16[48,3072]{1,0:T(8,128)(2,1)}, bf1...) custom-call(s32[5]{0:T(128)} %stack.23.pos_ref, ...), custom_call_target="tpu_custom_call" | custom-call | flops 9663676416 | bytes 29360128 | tf_op jit(solution)/shard_map/expert_forward/pallas_call | solution.py:292
  82.9 0.0 all-to-all-done.3
  82.9 4.8 %all-to-all-start.2 = ((bf16[4,64,3072]{2,1,0:T(8,128)(2,1)}), bf16[4,64,3072]{2,1,0:T(8,128)(2,1)S(1)}, u32[]{:S(2)}, u32[]{:S(2)}) async-start(bf16[4,64,3072]{2,1,0:T(8,128)(2,1)} %bitcast.41), calls=%async_computation.2 | async-start | bytes 3145728 | tf_op jit(solution)/shard_map/all_to_all | solution.py:30
  87.7 0.0 collective-permute-start.9
  87.8 2.0 %collective-permute-start.10 = (bf16[48,3072]{1,0:T(8,128)(2,1)}, bf16[48,3072]{1,0:T(8,128)(2,1)S(1)}, u32[]{:S(2)}, u32[]{:S(2)}) collective-permute-start(bf16[48,3072]{1,0:T(8,128)(2,1)} %get-tuple-element.98), channel_id=1, source_target_pairs={{0,8},{8,16},{16,24},{24,0},{32,40},{40,48},{48,56},{56,32},{1,9},... | collective-permute-start | bytes 884744 | tf_op jit(solution)/shard_map/ppermute | solution.py:22
  89.8 0.0 collective-permute-start.11
  89.8 0.0 collective-permute-done.12.refs_1_
  89.8 0.0 collective-permute-done.13.refs_2_
  89.8 16.5 %expert_backward.1 = (bf16[48,3072]{1,0:T(8,128)(2,1)}, bf16[48,3072]{1,0:T(8,128)(2,1)}, bf16[48,3072]{1,0:T(8,128)(2,1)}, bf16[48,3072]{1,0:T(8,128)(2,1)}, bf...) custom-call(s32[5]{0:T(128)} %stack.23.pos_ref, ...), custom_call_target="tpu_custom_call" | custom-call | flops 9663676416 | bytes 29360128 | tf_op jit(solution)/shard_map/expert_backward/pallas_call | solution.py:396
  106.3 0.0 collective-permute-done.9.refs_2_
  106.3 0.8 copy-done.11
  107.1 0.0 all-to-all-done.2
  107.1 1.2 copy-done
  108.3 2.7 %sum_quarters.2 = bf16[128,3072]{1,0:T(8,128)(2,1)} custom-call(s32[5]{0:T(128)} %stack.23.pos_ref, bf16[64,3072]{1,0:T(8,128)(2,1)} %get-tuple-element.124.own_ref, bf16[256,3072]{1,0:T(8,128)(2,1)} %bitcast.33), custom_call_target="tpu_custom_call" | custom-call | flops 786432 | bytes 2752512 | tf_op jit(solution)/shard_map/sum_quarters/pallas_call | solution.py:445
  111.0 5.7 %all-to-all-start.4 = ((bf16[8,16,3072]{2,1,0:T(8,128)(2,1)}), bf16[8,16,3072]{2,1,0:T(8,128)(2,1)S(1)}, u32[]{:S(2)}, u32[]{:S(2)}) async-start(bf16[8,16,3072]{2,1,0:T(8,128)(2,1)} %bitcast.38), calls=%async_computation.4 | async-start | bytes 1572864 | tf_op jit(solution)/shard_map/all_to_all | solution.py:30
  116.7 3.2 %collective-permute-start.17 = (bf16[48,3072]{1,0:T(8,128)(2,1)S(1)}, bf16[48,3072]{1,0:T(8,128)(2,1)S(1)}, u32[]{:S(2)}, u32[]{:S(2)}) collective-permute-start(bf16[48,3072]{1,0:T(8,128)(2,1)S(1)} %copy-done.24), channel_id=1, source_target_pairs={{0,24},{8,0},{16,8},{24,16},{32,56},{40,32},{48,40},{56,48},{1,25}... | collective-permute-start | bytes 884744 | tf_op jit(solution)/shard_map/ppermute | solution.py:22
  119.9 3.2 %collective-permute-start.14 = (bf16[64,3072]{1,0:T(8,128)(2,1)}, bf16[64,3072]{1,0:T(8,128)(2,1)S(1)}, u32[]{:S(2)}, u32[]{:S(2)}) collective-permute-start(bf16[64,3072]{1,0:T(8,128)(2,1)} %get-tuple-element.117), channel_id=1, source_target_pairs={{0,3},{1,0},{2,1},{3,2},{4,7},{5,4},{6,5},{7,6},{8,11},{9,8},{10,9... | collective-permute-start | bytes 1179656 | tf_op jit(solution)/shard_map/ppermute | solution.py:22
  123.2 2.3 %collective-permute-start.16 = (bf16[64,3072]{1,0:T(8,128)(2,1)}, bf16[64,3072]{1,0:T(8,128)(2,1)S(1)}, u32[]{:S(2)}, u32[]{:S(2)}) collective-permute-start(bf16[64,3072]{1,0:T(8,128)(2,1)} %get-tuple-element.119), channel_id=1, source_target_pairs={{0,2},{1,3},{2,0},{3,1},{4,6},{5,7},{6,4},{7,5},{8,10},{9,11},{10,... | collective-permute-start | bytes 1179656 | tf_op jit(solution)/shard_map/ppermute | solution.py:22
  125.5 6.5 %collective-permute-done.17.refs_2_ = bf16[48,3072]{1,0:T(8,128)(2,1)S(1)} collective-permute-done((bf16[48,3072]{1,0:T(8,128)(2,1)S(1)}, bf16[48,3072]{1,0:T(8,128)(2,1)S(1)}, u32[]{:S(2)}, u32[]{:S(2)}) %collective-permute-start.17) | collective-permute-done | bytes 294944 | tf_op jit(solution)/shard_map/ppermute | solution.py:22
  132.0 2.5 %collective-permute-start.19 = (bf16[48,3072]{1,0:T(8,128)(2,1)S(1)}, bf16[48,3072]{1,0:T(8,128)(2,1)S(1)}, u32[]{:S(2)}, u32[]{:S(2)}) collective-permute-start(bf16[48,3072]{1,0:T(8,128)(2,1)S(1)} %copy-done.22), channel_id=1, source_target_pairs={{0,16},{8,24},{16,0},{24,8},{32,48},{40,56},{48,32},{56,40},{1,17}... | collective-permute-start | bytes 884744 | tf_op jit(solution)/shard_map/ppermute | solution.py:22
  134.5 1.7 collective-permute-done.18.refs_4_
  136.1 4.1 %collective-permute-done.19.refs_3_ = bf16[48,3072]{1,0:T(8,128)(2,1)S(1)} collective-permute-done((bf16[48,3072]{1,0:T(8,128)(2,1)S(1)}, bf16[48,3072]{1,0:T(8,128)(2,1)S(1)}, u32[]{:S(2)}, u32[]{:S(2)}) %collective-permute-start.19) | collective-permute-done | bytes 294944 | tf_op jit(solution)/shard_map/ppermute | solution.py:22
  140.3 0.8 copy-done.7
  141.0 0.1 copy-done.8
  141.1 0.2 copy-done.9
  141.3 2.6 %sum_quarters.3 = bf16[128,3072]{1,0:T(8,128)(2,1)} custom-call(s32[5]{0:T(128)} %stack.23.pos_ref, bf16[64,3072]{1,0:T(8,128)(2,1)} %get-tuple-element.133.own_ref, bf16[64,3072]{1,0:T(8,128)(2,1)} %get-tuple-element.134.refs_0_, bf16[64,3072]{1,0:T(8,128)(2,1)} %copy-done.7, bf16[64,3072]{1,0:T(8,128)(2,1)} %copy-done.8, bf16[64,3072]{1,0:T(8,128)(2,1)} %copy-done.9), custom_call_target="tpu_custom_call" | custom-call | flops 786432 | bytes 2752512 | tf_op jit(solution)/shard_map/sum_quarters/pallas_call | solution.py:445
  143.9 4.7 %all-to-all-start.5 = ((bf16[8,16,3072]{2,1,0:T(8,128)(2,1)}), bf16[8,16,3072]{2,1,0:T(8,128)(2,1)S(1)}, u32[]{:S(2)}, u32[]{:S(2)}) async-start(bf16[8,16,3072]{2,1,0:T(8,128)(2,1)} %bitcast.39), calls=%async_computation.5 | async-start | bytes 1572864 | tf_op jit(solution)/shard_map/all_to_all | solution.py:30
  148.6 3.8 %combine_out.1 = (bf16[128,3072]{1,0:T(8,128)(2,1)}, bf16[128,128]{1,0:T(8,128)(2,1)}) custom-call(s32[5]{0:T(128)} %stack.23.pos_ref, f32[128,128]{1,0:T(8,128)} %get-tuple-element.74.meta_ref, bf16[128,3072]{1,0:T(8,128)(2,1)} %copy-done.2, bf16[128,3072]{1,0:T(8,128)(2,1)} %bitcast.35, bf16[48,3072]{1,0:T(8,128)(2,1)} %get-tuple-element.127.refs_1_, ...), custom_call_target="tpu_custom_call" | custom-call | flops 603979776 | bytes 3538944 | tf_op jit(solution)/shard_map/combine_out/pallas_call | solution.py:496
  152.4 6.3 %all-to-all-done.5 = bf16[8,16,3072]{2,1,0:T(8,128)(2,1)S(1)} async-done(((bf16[8,16,3072]{2,1,0:T(8,128)(2,1)}), bf16[8,16,3072]{2,1,0:T(8,128)(2,1)S(1)}, u32[]{:S(2)}, u32[]{:S(2)}) %all-to-all-start.5) | async-done | bytes 786464 | tf_op jit(solution)/shard_map/all_to_all | solution.py:30
  158.7 0.9 copy-done.1
  159.6 3.6 %combine_grad.1 = bf16[128,6272]{1,0:T(8,128)(2,1)} custom-call(s32[5]{0:T(128)} %stack.23.pos_ref, f32[128,128]{1,0:T(8,128)} %get-tuple-element.74.meta_ref, bf16[128,3072]{1,0:T(8,128)(2,1)} %get-tuple-element.131.out_terms_ref, bf16[128,128]{1,0:T(8,128)(2,1)} %get-tuple-element.132.dots_ref, bf16[128,3072]{1,0:T(8,128)(2,1)} %bitcast.34, ...), custom_call_target="tpu_custom_call" | custom-call | flops 301989888 | bytes 4325376 | tf_op jit(solution)/shard_map/combine_grad/pallas_call | solution.py:527
  163.1 23.4 %all_to_all.35 = bf16[8,16,6272]{2,1,0:T(8,128)(2,1)} all-to-all(bf16[8,16,6272]{2,1,0:T(8,128)(2,1)} %bitcast.31), channel_id=1, replica_groups=mesh['pipe'=2,'expert'=8,'etp'=8] {'etp'}, dimensions={0} | all-to-all | bytes 3211264 | tf_op jit(solution)/shard_map/all_to_all | solution.py:30
  186.6 2.8 %finish.1 = (bf16[16,3072]{1,0:T(8,128)(2,1)}, bf16[16,3072]{1,0:T(8,128)(2,1)}) custom-call(s32[5]{0:T(128)} %stack.23.pos_ref, f32[128,128]{1,0:T(8,128)} %get-tuple-element.74.meta_ref, bf16[8,3072]{1,0:T(8,128)(2,1)} %bitcast.45, bf16[128,6272]{1,0:T(8,128)(2,1)} %bitcast.32), custom_call_target="tpu_custom_call" | custom-call | flops 11796480 | bytes 1966080 | tf_op jit(solution)/shard_map/finish/pallas_call | solution.py:562
  (55 shorter events, 0.1 us)
Async XLA Ops:
  0.6 3.2 %collective-permute-start = (bf16[128,3072]{1,0:T(8,128)(2,1)}, bf16[128,3072]{1,0:T(8,128)(2,1)S(1)}, u32[]{:S(2)}, u32[]{:S(2)}) collective-permute-start(bf16[128,3072]{1,0:T(8,128)(2,1)} %bitcast.52), channel_id=1, source_target_pairs={{0,64},{64,0},{1,65},{65,1},{2,66},{66,2},{3,67},{67,3},{4,68},{68... | collective-permute-start | bytes 2359304 | tf_op jit(solution)/shard_map/ppermute | solution.py:588
  0.7 15.7 %collective-permute-start.1 = (bf16[128,3072]{1,0:T(8,128)(2,1)}, bf16[128,3072]{1,0:T(8,128)(2,1)S(1)}, u32[]{:S(2)}, u32[]{:S(2)}) collective-permute-start(bf16[128,3072]{1,0:T(8,128)(2,1)} %bitcast.53), channel_id=1, source_target_pairs={{0,64},{64,0},{1,65},{65,1},{2,66},{66,2},{3,67},{67,3},{4,68},{68... | collective-permute-start | bytes 2359304 | tf_op jit(solution)/shard_map/ppermute | solution.py:589
  3.8 0.9 copy-start.5
  7.8 19.0 %all-to-all-start = ((bf16[8,16,3072]{2,1,0:T(8,128)(2,1)}), bf16[8,16,3072]{2,1,0:T(8,128)(2,1)S(1)}, u32[]{:S(2)}, u32[]{:S(2)}) async-start(bf16[8,16,3072]{2,1,0:T(8,128)(2,1)} %bitcast.43), calls=%async_computation | async-start | bytes 1572864 | tf_op jit(solution)/shard_map/all_to_all | solution.py:30
  13.2 18.6 %collective-permute-start.2 = (bf16[48,3072]{1,0:T(8,128)(2,1)}, bf16[48,3072]{1,0:T(8,128)(2,1)S(1)}, u32[]{:S(2)}, u32[]{:S(2)}) collective-permute-start(bf16[48,3072]{1,0:T(8,128)(2,1)} %get-tuple-element.78), channel_id=1, source_target_pairs={{0,8},{8,16},{16,24},{24,0},{32,40},{40,48},{48,56},{56,32},{1,9},... | collective-permute-start | bytes 884744 | tf_op jit(solution)/shard_map/ppermute | solution.py:22
  15.2 16.5 %collective-permute-start.3 = (bf16[48,3072]{1,0:T(8,128)(2,1)}, bf16[48,3072]{1,0:T(8,128)(2,1)S(1)}, u32[]{:S(2)}, u32[]{:S(2)}) collective-permute-start(bf16[48,3072]{1,0:T(8,128)(2,1)} %get-tuple-element.79), channel_id=1, source_target_pairs={{0,24},{8,0},{16,8},{24,16},{32,56},{40,32},{48,40},{56,48},{1,25}... | collective-permute-start | bytes 884744 | tf_op jit(solution)/shard_map/ppermute | solution.py:22
  16.4 0.9 copy-start.2
  21.0 17.6 %copy-start.21 = (bf16[48,3072]{1,0:T(8,128)(2,1)S(1)}, bf16[48,3072]{1,0:T(8,128)(2,1)}, u32[]{:S(2)}) copy-start(bf16[48,3072]{1,0:T(8,128)(2,1)} %get-tuple-element.83) | copy-start | bytes 884740
  21.0 19.7 %copy-start.25 = (bf16[48,3072]{1,0:T(8,128)(2,1)S(1)}, bf16[48,3072]{1,0:T(8,128)(2,1)}, u32[]{:S(2)}) copy-start(bf16[48,3072]{1,0:T(8,128)(2,1)} %get-tuple-element.84) | copy-start | bytes 884740
  26.7 28.2 %all-to-all-start.1 = ((bf16[8,16,3072]{2,1,0:T(8,128)(2,1)}), bf16[8,16,3072]{2,1,0:T(8,128)(2,1)S(1)}, u32[]{:S(2)}, u32[]{:S(2)}) async-start(bf16[8,16,3072]{2,1,0:T(8,128)(2,1)} %bitcast.42), calls=%async_computation.1 | async-start | bytes 1572864 | tf_op jit(solution)/shard_map/all_to_all | solution.py:30
  31.7 4.8 %copy-start.18 = (bf16[48,3072]{1,0:T(8,128)(2,1)}, bf16[48,3072]{1,0:T(8,128)(2,1)S(1)}, u32[]{:S(2)}) copy-start(bf16[48,3072]{1,0:T(8,128)(2,1)S(1)} %collective-permute-done.2.refs_1_) | copy-start | bytes 884740
  31.7 4.8 %copy-start.19 = (bf16[48,3072]{1,0:T(8,128)(2,1)}, bf16[48,3072]{1,0:T(8,128)(2,1)S(1)}, u32[]{:S(2)}) copy-start(bf16[48,3072]{1,0:T(8,128)(2,1)S(1)} %collective-permute-done.3.refs_2_) | copy-start | bytes 884740
  32.6 24.6 %copy-start.6 = (bf16[64,3072]{1,0:T(8,128)(2,1)}, bf16[64,3072]{1,0:T(8,128)(2,1)S(1)}, u32[]{:S(2)}) copy-start(bf16[64,3072]{1,0:T(8,128)(2,1)S(1)} %get-tuple-element.91.refs_5_) | copy-start | bytes 1179652
  32.6 22.3 %collective-permute-start.8 = (bf16[64,3072]{1,0:T(8,128)(2,1)S(1)}, bf16[64,3072]{1,0:T(8,128)(2,1)S(1)}, u32[]{:S(2)}, u32[]{:S(2)}) collective-permute-start(bf16[64,3072]{1,0:T(8,128)(2,1)S(1)} %get-tuple-element.91.refs_5_), channel_id=1, source_target_pairs={{0,2},{1,3},{2,0},{3,1},{4,6},{5,7},{6,4},{7,5},{8,10},{9,11},{10,... | collective-permute-start | bytes 1179656 | tf_op jit(solution)/shard_map/ppermute | solution.py:22
  36.5 18.4 %collective-permute-start.7 = (bf16[64,3072]{1,0:T(8,128)(2,1)S(1)}, bf16[64,3072]{1,0:T(8,128)(2,1)S(1)}, u32[]{:S(2)}, u32[]{:S(2)}) collective-permute-start(bf16[64,3072]{1,0:T(8,128)(2,1)S(1)} %get-tuple-element.91.refs_5_), channel_id=1, source_target_pairs={{0,3},{1,0},{2,1},{3,2},{4,7},{5,4},{6,5},{7,6},{8,11},{9,8},{10,9... | collective-permute-start | bytes 1179656 | tf_op jit(solution)/shard_map/ppermute | solution.py:22
  37.2 17.7 %collective-permute-start.6 = (bf16[64,3072]{1,0:T(8,128)(2,1)S(1)}, bf16[64,3072]{1,0:T(8,128)(2,1)S(1)}, u32[]{:S(2)}, u32[]{:S(2)}) collective-permute-start(bf16[64,3072]{1,0:T(8,128)(2,1)S(1)} %get-tuple-element.91.refs_5_), channel_id=1, source_target_pairs={{0,1},{1,2},{2,3},{3,0},{4,5},{5,6},{6,7},{7,4},{8,9},{9,10},{10,1... | collective-permute-start | bytes 1179656 | tf_op jit(solution)/shard_map/ppermute | solution.py:22
  38.5 11.5 %collective-permute-start.4 = (bf16[48,3072]{1,0:T(8,128)(2,1)S(1)}, bf16[48,3072]{1,0:T(8,128)(2,1)S(1)}, u32[]{:S(2)}, u32[]{:S(2)}) collective-permute-start(bf16[48,3072]{1,0:T(8,128)(2,1)S(1)} %copy-done.21), channel_id=1, source_target_pairs={{0,16},{8,24},{16,0},{24,8},{32,48},{40,56},{48,32},{56,40},{1,17}... | collective-permute-start | bytes 884744 | tf_op jit(solution)/shard_map/ppermute | solution.py:22
  40.7 14.2 %collective-permute-start.5 = (bf16[48,3072]{1,0:T(8,128)(2,1)S(1)}, bf16[48,3072]{1,0:T(8,128)(2,1)S(1)}, u32[]{:S(2)}, u32[]{:S(2)}) collective-permute-start(bf16[48,3072]{1,0:T(8,128)(2,1)S(1)} %copy-done.25), channel_id=1, source_target_pairs={{0,16},{8,24},{16,0},{24,8},{32,48},{40,56},{48,32},{56,40},{1,17}... | collective-permute-start | bytes 884744 | tf_op jit(solution)/shard_map/ppermute | solution.py:22
  50.0 7.2 %copy-start.23 = (bf16[48,3072]{1,0:T(8,128)(2,1)}, bf16[48,3072]{1,0:T(8,128)(2,1)S(1)}, u32[]{:S(2)}) copy-start(bf16[48,3072]{1,0:T(8,128)(2,1)S(1)} %collective-permute-done.4.refs_3_) | copy-start | bytes 884740
  54.9 2.3 %copy-start.20 = (bf16[48,3072]{1,0:T(8,128)(2,1)}, bf16[48,3072]{1,0:T(8,128)(2,1)S(1)}, u32[]{:S(2)}) copy-start(bf16[48,3072]{1,0:T(8,128)(2,1)S(1)} %collective-permute-done.5.refs_3_) | copy-start | bytes 884740
  54.9 2.3 %copy-start.15 = (bf16[64,3072]{1,0:T(8,128)(2,1)}, bf16[64,3072]{1,0:T(8,128)(2,1)S(1)}, u32[]{:S(2)}) copy-start(bf16[64,3072]{1,0:T(8,128)(2,1)S(1)} %collective-permute-done.8.refs_8_) | copy-start | bytes 1179652
  54.9 2.3 %copy-start.16 = (bf16[64,3072]{1,0:T(8,128)(2,1)}, bf16[64,3072]{1,0:T(8,128)(2,1)S(1)}, u32[]{:S(2)}) copy-start(bf16[64,3072]{1,0:T(8,128)(2,1)S(1)} %collective-permute-done.7.refs_7_) | copy-start | bytes 1179652
  54.9 2.3 %copy-start.17 = (bf16[64,3072]{1,0:T(8,128)(2,1)}, bf16[64,3072]{1,0:T(8,128)(2,1)S(1)}, u32[]{:S(2)}) copy-start(bf16[64,3072]{1,0:T(8,128)(2,1)S(1)} %collective-permute-done.6.refs_6_) | copy-start | bytes 1179652
  57.2 25.7 %all-to-all-start.3 = ((bf16[4,64,3072]{2,1,0:T(8,128)(2,1)}), bf16[4,64,3072]{2,1,0:T(8,128)(2,1)S(1)}, u32[]{:S(2)}, u32[]{:S(2)}) async-start(bf16[4,64,3072]{2,1,0:T(8,128)(2,1)} %broadcast_in_dim.12), calls=%async_computation.3 | async-start | bytes 3145728 | tf_op jit(solution)/shard_map/all_to_all | solution.py:30
  62.5 27.2 %collective-permute-start.12 = (bf16[48,3072]{1,0:T(8,128)(2,1)}, bf16[48,3072]{1,0:T(8,128)(2,1)}, u32[]{:S(2)}, u32[]{:S(2)}) collective-permute-start(bf16[48,3072]{1,0:T(8,128)(2,1)} %get-tuple-element.101), channel_id=1, source_target_pairs={{0,8},{8,16},{16,24},{24,0},{32,40},{40,48},{48,56},{56,32},{1,9},... | collective-permute-start | bytes 884744 | tf_op jit(solution)/shard_map/ppermute | solution.py:22
  63.1 26.7 %collective-permute-start.13 = (bf16[48,3072]{1,0:T(8,128)(2,1)}, bf16[48,3072]{1,0:T(8,128)(2,1)}, u32[]{:S(2)}, u32[]{:S(2)}) collective-permute-start(bf16[48,3072]{1,0:T(8,128)(2,1)} %get-tuple-element.102), channel_id=1, source_target_pairs={{0,24},{8,0},{16,8},{24,16},{32,56},{40,32},{48,40},{56,48},{1,25}... | collective-permute-start | bytes 884744 | tf_op jit(solution)/shard_map/ppermute | solution.py:22
  82.9 6.9 %copy-start.4 = (bf16[4,64,3072]{2,1,0:T(8,128)(2,1)}, bf16[4,64,3072]{2,1,0:T(8,128)(2,1)S(1)}, u32[]{:S(2)}) copy-start(bf16[4,64,3072]{2,1,0:T(8,128)(2,1)S(1)} %all-to-all-done.3) | copy-start | bytes 4718596
  82.9 24.2 %all-to-all-start.2 = ((bf16[4,64,3072]{2,1,0:T(8,128)(2,1)}), bf16[4,64,3072]{2,1,0:T(8,128)(2,1)S(1)}, u32[]{:S(2)}, u32[]{:S(2)}) async-start(bf16[4,64,3072]{2,1,0:T(8,128)(2,1)} %bitcast.41), calls=%async_computation.2 | async-start | bytes 3145728 | tf_op jit(solution)/shard_map/all_to_all | solution.py:30
  87.7 18.6 %collective-permute-start.9 = (bf16[48,3072]{1,0:T(8,128)(2,1)}, bf16[48,3072]{1,0:T(8,128)(2,1)S(1)}, u32[]{:S(2)}, u32[]{:S(2)}) collective-permute-start(bf16[48,3072]{1,0:T(8,128)(2,1)} %get-tuple-element.97), channel_id=1, source_target_pairs={{0,24},{8,0},{16,8},{24,16},{32,56},{40,32},{48,40},{56,48},{1,25}... | collective-permute-start | bytes 884744 | tf_op jit(solution)/shard_map/ppermute | solution.py:22
  87.8 18.6 %collective-permute-start.10 = (bf16[48,3072]{1,0:T(8,128)(2,1)}, bf16[48,3072]{1,0:T(8,128)(2,1)S(1)}, u32[]{:S(2)}, u32[]{:S(2)}) collective-permute-start(bf16[48,3072]{1,0:T(8,128)(2,1)} %get-tuple-element.98), channel_id=1, source_target_pairs={{0,8},{8,16},{16,24},{24,0},{32,40},{40,48},{48,56},{56,32},{1,9},... | collective-permute-start | bytes 884744 | tf_op jit(solution)/shard_map/ppermute | solution.py:22
  89.8 17.3 %collective-permute-start.11 = (bf16[48,3072]{1,0:T(8,128)(2,1)}, bf16[48,3072]{1,0:T(8,128)(2,1)}, u32[]{:S(2)}, u32[]{:S(2)}) collective-permute-start(bf16[48,3072]{1,0:T(8,128)(2,1)} %get-tuple-element.99), channel_id=1, source_target_pairs={{0,16},{8,24},{16,0},{24,8},{32,48},{40,56},{48,32},{56,40},{1,17}... | collective-permute-start | bytes 884744 | tf_op jit(solution)/shard_map/ppermute | solution.py:22
  106.3 42.3 %copy-start.10 = (bf16[48,3072]{1,0:T(8,128)(2,1)}, bf16[48,3072]{1,0:T(8,128)(2,1)S(1)}, u32[]{:S(2)}) copy-start(bf16[48,3072]{1,0:T(8,128)(2,1)S(1)} %collective-permute-done.9.refs_2_) | copy-start | bytes 884740
  106.3 0.8 copy-start.11
  107.1 1.2 copy-start
  108.3 8.4 %copy-start.24 = (bf16[48,3072]{1,0:T(8,128)(2,1)S(1)}, bf16[48,3072]{1,0:T(8,128)(2,1)}, u32[]{:S(2)}) copy-start(bf16[48,3072]{1,0:T(8,128)(2,1)} %get-tuple-element.121) | copy-start | bytes 884740
  108.3 23.7 %copy-start.22 = (bf16[48,3072]{1,0:T(8,128)(2,1)S(1)}, bf16[48,3072]{1,0:T(8,128)(2,1)}, u32[]{:S(2)}) copy-start(bf16[48,3072]{1,0:T(8,128)(2,1)} %get-tuple-element.123) | copy-start | bytes 884740
  111.0 29.3 %all-to-all-start.4 = ((bf16[8,16,3072]{2,1,0:T(8,128)(2,1)}), bf16[8,16,3072]{2,1,0:T(8,128)(2,1)S(1)}, u32[]{:S(2)}, u32[]{:S(2)}) async-start(bf16[8,16,3072]{2,1,0:T(8,128)(2,1)} %bitcast.38), calls=%async_computation.4 | async-start | bytes 1572864 | tf_op jit(solution)/shard_map/all_to_all | solution.py:30
  116.7 15.3 %collective-permute-start.17 = (bf16[48,3072]{1,0:T(8,128)(2,1)S(1)}, bf16[48,3072]{1,0:T(8,128)(2,1)S(1)}, u32[]{:S(2)}, u32[]{:S(2)}) collective-permute-start(bf16[48,3072]{1,0:T(8,128)(2,1)S(1)} %copy-done.24), channel_id=1, source_target_pairs={{0,24},{8,0},{16,8},{24,16},{32,56},{40,32},{48,40},{56,48},{1,25}... | collective-permute-start | bytes 884744 | tf_op jit(solution)/shard_map/ppermute | solution.py:22
  119.9 20.3 %collective-permute-start.14 = (bf16[64,3072]{1,0:T(8,128)(2,1)}, bf16[64,3072]{1,0:T(8,128)(2,1)S(1)}, u32[]{:S(2)}, u32[]{:S(2)}) collective-permute-start(bf16[64,3072]{1,0:T(8,128)(2,1)} %get-tuple-element.117), channel_id=1, source_target_pairs={{0,3},{1,0},{2,1},{3,2},{4,7},{5,4},{6,5},{7,6},{8,11},{9,8},{10,9... | collective-permute-start | bytes 1179656 | tf_op jit(solution)/shard_map/ppermute | solution.py:22
  123.2 17.0 %collective-permute-start.15 = (bf16[64,3072]{1,0:T(8,128)(2,1)}, bf16[64,3072]{1,0:T(8,128)(2,1)S(1)}, u32[]{:S(2)}, u32[]{:S(2)}) collective-permute-start(bf16[64,3072]{1,0:T(8,128)(2,1)} %get-tuple-element.118), channel_id=1, source_target_pairs={{0,1},{1,2},{2,3},{3,0},{4,5},{5,6},{6,7},{7,4},{8,9},{9,10},{10,1... | collective-permute-start | bytes 1179656 | tf_op jit(solution)/shard_map/ppermute | solution.py:22
  123.2 17.0 %collective-permute-start.16 = (bf16[64,3072]{1,0:T(8,128)(2,1)}, bf16[64,3072]{1,0:T(8,128)(2,1)S(1)}, u32[]{:S(2)}, u32[]{:S(2)}) collective-permute-start(bf16[64,3072]{1,0:T(8,128)(2,1)} %get-tuple-element.119), channel_id=1, source_target_pairs={{0,2},{1,3},{2,0},{3,1},{4,6},{5,7},{6,4},{7,5},{8,10},{9,11},{10,... | collective-permute-start | bytes 1179656 | tf_op jit(solution)/shard_map/ppermute | solution.py:22
  125.5 10.6 %collective-permute-start.18 = (bf16[48,3072]{1,0:T(8,128)(2,1)}, bf16[48,3072]{1,0:T(8,128)(2,1)S(1)}, u32[]{:S(2)}, u32[]{:S(2)}) collective-permute-start(bf16[48,3072]{1,0:T(8,128)(2,1)} %get-tuple-element.122), channel_id=1, source_target_pairs={{0,8},{8,16},{16,24},{24,0},{32,40},{40,48},{48,56},{56,32},{1,9},... | collective-permute-start | bytes 884744 | tf_op jit(solution)/shard_map/ppermute | solution.py:22
  132.0 26.7 %copy-start.12 = (bf16[48,3072]{1,0:T(8,128)(2,1)}, bf16[48,3072]{1,0:T(8,128)(2,1)S(1)}, u32[]{:S(2)}) copy-start(bf16[48,3072]{1,0:T(8,128)(2,1)S(1)} %collective-permute-done.17.refs_2_) | copy-start | bytes 884740
  132.0 8.2 %collective-permute-start.19 = (bf16[48,3072]{1,0:T(8,128)(2,1)S(1)}, bf16[48,3072]{1,0:T(8,128)(2,1)S(1)}, u32[]{:S(2)}, u32[]{:S(2)}) collective-permute-start(bf16[48,3072]{1,0:T(8,128)(2,1)S(1)} %copy-done.22), channel_id=1, source_target_pairs={{0,16},{8,24},{16,0},{24,8},{32,48},{40,56},{48,32},{56,40},{1,17}... | collective-permute-start | bytes 884744 | tf_op jit(solution)/shard_map/ppermute | solution.py:22
  136.1 22.6 %copy-start.13 = (bf16[48,3072]{1,0:T(8,128)(2,1)}, bf16[48,3072]{1,0:T(8,128)(2,1)S(1)}, u32[]{:S(2)}) copy-start(bf16[48,3072]{1,0:T(8,128)(2,1)S(1)} %collective-permute-done.18.refs_4_) | copy-start | bytes 884740
  140.2 18.5 %copy-start.14 = (bf16[48,3072]{1,0:T(8,128)(2,1)}, bf16[48,3072]{1,0:T(8,128)(2,1)S(1)}, u32[]{:S(2)}) copy-start(bf16[48,3072]{1,0:T(8,128)(2,1)S(1)} %collective-permute-done.19.refs_3_) | copy-start | bytes 884740
  140.2 0.8 copy-start.7
  140.2 0.9 copy-start.8
  140.2 1.1 copy-start.9
  140.3 3.7 %copy-start.3 = (bf16[8,16,3072]{2,1,0:T(8,128)(2,1)}, bf16[8,16,3072]{2,1,0:T(8,128)(2,1)S(1)}, u32[]{:S(2)}) copy-start(bf16[8,16,3072]{2,1,0:T(8,128)(2,1)S(1)} %all-to-all-done.4) | copy-start | bytes 2359300
  143.9 14.8 %all-to-all-start.5 = ((bf16[8,16,3072]{2,1,0:T(8,128)(2,1)}), bf16[8,16,3072]{2,1,0:T(8,128)(2,1)S(1)}, u32[]{:S(2)}, u32[]{:S(2)}) async-start(bf16[8,16,3072]{2,1,0:T(8,128)(2,1)} %bitcast.39), calls=%async_computation.5 | async-start | bytes 1572864 | tf_op jit(solution)/shard_map/all_to_all | solution.py:30
  158.7 0.9 copy-start.1
